TPU v7x, 512 devices: a whole 4x4x16 slice. The times are simulated.
512 devices in a mesh: vid: 16 (over z_hi, y, core), seq: 32 (over x, z_lo).
Axes of the slice: x: 4, y: 4, z: 16 (z_hi: 2, z_lo: 8; z = z_hi * 8 + z_lo), core: 2. Of those that a mesh axis runs over, the one named last changes fastest.
Arguments:
- time_qkv: bfloat16 [3, 16, 32, 256, 704], P(None, 'vid', None, 'seq'), may hold values from -6 to 6
- space_qkv: bfloat16 [3, 16, 32, 256, 704], P(None, 'vid', 'seq'), may hold values from -6 to 6
- residual: bfloat16 [16, 32, 256, 1408], P('vid', 'seq'), may hold values from -6.4 to 6.4
- space_proj: bfloat16 [704, 1408], P('seq', 'vid'), may hold values from -0.875 to 0.875
- time_proj: bfloat16 [704, 1408], P('seq', 'vid'), may hold values from -0.875 to 0.875
- norm_gain: float32 [1408], replicated, may hold values from 0.1 to 1.9
- text_emb: float32 [16, 1408], P('vid'), may hold values from -6.8 to 6.8
- teacher: int32 [16, 16], P('vid'), may hold values from 0 to 40
Outputs:
- space_qkv_grad: bfloat16 [3, 16, 32, 256, 704], P(None, 'vid', 'seq')
- time_qkv_grad: bfloat16 [3, 16, 32, 256, 704], P(None, 'vid', None, 'seq')
- score_grad: float32 [16, 16], P('vid')
All inputs are finite; a program needn't handle non-finite values.
Results may differ from a plain program's by a relative error of at most 0.0049.
Values may be sent and summed in bfloat16 or wider, within the bound.
No kernel may reach another device: no remote copies, remote signals or barrier semaphores. Data moves between devices by JAX's collectives and lax.ppermute only.
A program may use at most 64 MiB of HBM per device.

v0:
```python
import math

import jax
import jax.numpy as jnp
from jax import lax
from jax.sharding import PartitionSpec as P

HEAD_DIM = 88


logit_scale = 20.0
teacher_softness = 4.0
space_layout = ("blhe", "bmhe", "bhlm")
time_layout = ("lbhe", "mbhe", "bhlm")


def probabilities(queries, key_rows, layout):
    scores = jnp.einsum(
        layout[0] + "," + layout[1] + "->" + layout[2],
        queries,
        key_rows,
        preferred_element_type=jnp.float32,
    ) / math.sqrt(queries.shape[-1])
    row_peak = jnp.max(scores, axis=-1, keepdims=True)
    weights = jnp.exp(scores - row_peak)
    weights = weights / jnp.sum(weights, axis=-1, keepdims=True)
    return (weights, weights.astype(jnp.bfloat16))


def attention_back(queries, key_rows, values, weights, weights_low, grad_out, layout):
    out_dots = jnp.einsum(
        layout[0] + "," + layout[1] + "->" + layout[2],
        grad_out,
        values,
        preferred_element_type=jnp.float32,
    )
    row_delta = jnp.sum(weights * out_dots, axis=-1, keepdims=True)
    slopes = (weights * (out_dots - row_delta) / math.sqrt(queries.shape[-1])).astype(jnp.bfloat16)
    grad_queries = jnp.einsum(
        layout[2] + "," + layout[1] + "->" + layout[0],
        slopes,
        key_rows,
        preferred_element_type=jnp.float32,
    ).astype(jnp.bfloat16)
    grad_keys = jnp.einsum(
        layout[2] + "," + layout[0] + "->" + layout[1],
        slopes,
        queries,
        preferred_element_type=jnp.float32,
    ).astype(jnp.bfloat16)
    grad_values = jnp.einsum(
        layout[2] + "," + layout[0] + "->" + layout[1],
        weights_low,
        grad_out,
        preferred_element_type=jnp.float32,
    ).astype(jnp.bfloat16)
    return jnp.stack([grad_queries, grad_keys, grad_values])


def shards(time_qkv, space_qkv, residual, space_proj, time_proj, norm_gain, text_emb, teacher):
    rows_space, rows_time = (
        lax.all_gather(space_proj, "seq", axis=0, tiled=True),
        lax.all_gather(time_proj, "seq", axis=0, tiled=True),
    )
    w_space, w_time = (
        lax.all_gather(rows_space, "vid", axis=1, tiled=True),
        lax.all_gather(rows_time, "vid", axis=1, tiled=True),
    )
    model_width = residual.shape[3]
    frames_dev = residual.shape[1]
    patches = residual.shape[2]
    head_width = w_space.shape[0]
    head_count = head_width // HEAD_DIM
    frames = frames_dev * lax.axis_size("seq")
    patch_dev = time_qkv.shape[3]
    videos = lax.axis_size("vid")
    token_count = frames_dev * patches
    space_parts = [
        space_qkv[slot, 0].reshape(frames_dev, patches, head_count, HEAD_DIM) for slot in range(3)
    ]
    weights, weights_low = probabilities(space_parts[0], space_parts[1], space_layout)
    attended = jnp.einsum(
        "bhlm,bmhe->blhe", weights_low, space_parts[2], preferred_element_type=jnp.float32
    ).astype(jnp.bfloat16)
    attended = attended.reshape(token_count, head_width)
    mixed_sum = residual[0].reshape(token_count, model_width).astype(jnp.float32) + jnp.dot(
        attended, w_space, preferred_element_type=jnp.float32
    )
    center = mixed_sum - jnp.mean(mixed_sum, axis=-1, keepdims=True)
    inv_scale = 1.0 / jnp.sqrt(jnp.mean(center * center, axis=-1, keepdims=True) + 1e-05)
    normalized_rows = center * inv_scale
    frame_emb = jnp.mean(
        (normalized_rows * norm_gain).reshape(frames_dev, patches, model_width), axis=1
    )
    frame_norm = jnp.sqrt(jnp.sum(frame_emb * frame_emb, axis=-1, keepdims=True) + 1e-06)
    frame_unit = frame_emb / frame_norm
    texts = lax.all_gather(text_emb, "vid", axis=0, tiled=True)
    text_unit = texts / jnp.sqrt(jnp.sum(texts * texts, axis=-1, keepdims=True) + 1e-06)
    frame_cosines = jnp.dot(frame_unit, text_unit.T, precision=lax.Precision.HIGHEST)
    partial_row = logit_scale / frames * jnp.sum(frame_cosines, axis=0)
    own_row = lax.psum(partial_row, "seq")
    all_scores = lax.all_gather(own_row[None, :], "vid", axis=0, tiled=True)
    own_video = lax.axis_index("vid")
    one_hot = (jnp.arange(videos) == own_video).astype(jnp.float32)
    own_exp = jnp.exp(own_row)
    row_soft = own_exp / jnp.sum(own_exp)
    col_soft = own_exp / jnp.sum(jnp.exp(all_scores), axis=0)
    teacher_exponent = jnp.exp(teacher[0].astype(jnp.float32) / teacher_softness)
    teacher_soft = teacher_exponent / jnp.sum(teacher_exponent)
    gradient_row_slice = (row_soft - one_hot + (col_soft - one_hot)) / (2.0 * videos) + (
        row_soft - teacher_soft
    ) / videos
    direction = (
        videos
        * logit_scale
        * jnp.dot(gradient_row_slice, text_unit, precision=lax.Precision.HIGHEST)
    )
    along = jnp.sum(frame_unit * direction[None, :], axis=-1, keepdims=True)
    frame_grad = (direction[None, :] - frame_unit * along) / frame_norm
    token_grad = jnp.broadcast_to(
        (frame_grad * norm_gain)[:, None, :], (frames_dev, patches, model_width)
    ).reshape(token_count, model_width)
    mean_grad = jnp.mean(token_grad, axis=-1, keepdims=True)
    mean_cross = jnp.mean(token_grad * normalized_rows, axis=-1, keepdims=True)
    mixed_grad = (inv_scale * (token_grad - mean_grad - normalized_rows * mean_cross)).astype(
        jnp.bfloat16
    )
    space_out_grad = jnp.einsum(
        "td,ad->ta", mixed_grad, w_space, preferred_element_type=jnp.float32
    ).astype(jnp.bfloat16)
    space_out_grad = space_out_grad.reshape(frames_dev, patches, head_count, HEAD_DIM)
    space_grad = attention_back(
        space_parts[0],
        space_parts[1],
        space_parts[2],
        weights,
        weights_low,
        space_out_grad,
        space_layout,
    )
    space_grad = space_grad.reshape(3, 1, frames_dev, patches, head_width)
    moved = lax.all_to_all(
        mixed_grad.reshape(1, frames_dev, patches, model_width),
        "seq",
        split_axis=2,
        concat_axis=1,
        tiled=True,
    )
    time_out_grad = jnp.einsum(
        "td,ad->ta",
        moved.reshape(frames * patch_dev, model_width),
        w_time,
        preferred_element_type=jnp.float32,
    ).astype(jnp.bfloat16)
    time_out_grad = time_out_grad.reshape(frames, patch_dev, head_count, HEAD_DIM)
    time_parts = [
        time_qkv[slot, 0].reshape(frames, patch_dev, head_count, HEAD_DIM) for slot in range(3)
    ]
    time_weights, time_low = probabilities(time_parts[0], time_parts[1], time_layout)
    time_grad = attention_back(
        time_parts[0],
        time_parts[1],
        time_parts[2],
        time_weights,
        time_low,
        time_out_grad,
        time_layout,
    )
    time_grad = time_grad.reshape(3, 1, frames, patch_dev, head_width)
    return (space_grad, time_grad, gradient_row_slice[None, :])


def solution(mesh):
    in_specs = (
        P(None, "vid", None, "seq", None),
        P(None, "vid", "seq", None, None),
        P("vid", "seq", None, None),
        P("seq", "vid"),
        P("seq", "vid"),
        P(),
        P("vid", None),
        P("vid", None),
    )
    out_specs = (
        P(None, "vid", "seq", None, None),
        P(None, "vid", None, "seq", None),
        P("vid", None),
    )
    return jax.shard_map(shards, mesh=mesh, in_specs=in_specs, out_specs=out_specs, check_vma=False)
```

profile of v0, /device:TPU:1, one launch (start us, length us, event | category | flops | bytes accessed | tf_op | source)
XLA Modules:
  0.0 579.4 jit_solution(1124590042645385510)
XLA Ops:
  7.2 113.2 %all-gather.1 = bf16[32,22,88]{2,1,0:T(8,128)(2,1)S(1)} all-gather(bf16[1,22,88]{2,1,0:T(8,128)(2,1)} %bitcast.113), channel_id=1, replica_groups=mesh['vid'=16,'seq'=32] {'seq'}, dimensions={0}, use_global_device_ids=true | all-gather | bytes 127776 | tf_op jit(solution)/shard_map/all_gather | solution.py:62
  120.5 0.8 copy.73
  121.4 110.9 %all-gather.3 = bf16[32,22,88]{2,1,0:T(8,128)(2,1)S(1)} all-gather(bf16[1,22,88]{2,1,0:T(8,128)(2,1)} %bitcast.114), channel_id=1, replica_groups=mesh['vid'=16,'seq'=32] {'seq'}, dimensions={0}, use_global_device_ids=true | all-gather | bytes 127776 | tf_op jit(solution)/shard_map/all_gather | solution.py:63
  233.3 74.6 %all-gather.2 = f32[16,1,1408]{2,1,0:T(1,128)S(1)} all-gather(f32[1,1,1408]{2,1,0:T(1,128)S(1)} %bitcast.115), channel_id=1, replica_groups=mesh['vid'=16,'seq'=32] {'vid'}, dimensions={0}, use_global_device_ids=true | all-gather | bytes 95744 | tf_op jit(solution)/shard_map/all_gather | solution.py:97
  308.6 2.2 fusion.82
  310.8 1.3 dynamic-slice
  312.7 2.0 convolution_convert_fusion.6
  314.7 2.5 fusion.83
  319.5 106.9 %psum.7 = f32[16]{0:T(128)S(1)} all-reduce(f32[16]{0:T(128)S(1)} %fusion.29), channel_id=1, replica_groups=mesh['vid'=16,'seq'=32] {'seq'}, use_global_device_ids=true, to_apply=%region_7.0 | all-reduce | flops 16 | bytes 128 | tf_op jit(solution)/shard_map/psum | solution.py:101
  427.2 75.1 %all-reduce = f32[256]{0:T(256)S(1)} all-reduce(f32[256]{0:T(256)S(1)} %dynamic-update-slice), channel_id=2, replica_groups=mesh['vid'=16,'seq'=32] {'vid'}, use_global_device_ids=true, to_apply=%add | all-reduce | flops 256 | bytes 2048
  502.4 1.2 fusion.58
  504.5 1.3 fusion.79
  507.3 1.1 copy.133
  508.9 5.9 %reduce.18 = bf16[256,1408]{1,0:T(8,128)(2,1)} reduce(bf16[256,1,1,1408]{3,2,1,0:T(2,128)(2,1)S(1)} %bitcast.99, bf16[]{:T(256)} %broadcast.166), dimensions={1,2}, to_apply=%bitcast.98.reduce_sub_computation | reduce | bytes 1441794
  514.8 2.6 reshape.214
  517.4 4.1 all-to-all-start
  521.5 1.3 fusion.80
  522.8 1.4 reshape_squeeze.14
  524.3 1.4 reshape_squeeze.6
  526.3 3.1 fusion.84
  529.4 2.8 convolution_convert_fusion.5
  532.2 1.8 fusion.89
  534.0 4.3 fusion.23
  538.3 4.2 fusion.20
  542.5 2.0 convolution_convert_fusion.4
  544.6 1.1 pad_maximum_fusion.1
  545.7 12.9 %all-to-all-done = bf16[32,2,5632]{2,1,0:T(2,128)(2,1)S(1)} async-done(((bf16[32,2,5632]{2,1,0:T(2,128)(2,1)}), bf16[32,2,5632]{2,1,0:T(2,128)(2,1)S(1)}, u32[]{:S(2)}, u32[]{:S(2)}) %all-to-all-start) | async-done | bytes 720928 | tf_op jit(solution)/shard_map/all_to_all | solution.py:142
  559.2 2.6 convolution_convert_fusion.3
  563.3 1.7 fusion.28
  565.1 2.3 fusion.27
  567.4 2.3 fusion.26
  571.4 1.2 pad_maximum_fusion
  (73 shorter events, 10.9 us)
Async XLA Ops:
  7.2 226.0 %copy-start.2 = (bf16[3,1,1,256,704]{3,4,2,1,0:T(8,128)(2,1)S(1)}, bf16[3,1,1,256,704]{3,4,2,1,0:T(8,128)(2,1)}, u32[]{:S(2)}) copy-start(bf16[3,1,1,256,704]{3,4,2,1,0:T(8,128)(2,1)} %param.9) | copy-start | bytes 3244036
  7.2 307.5 %all-gather.7.cloned.1.call-start = ((), (), s32[]{:S(2)}) async-start(), calls=%async_computation.1 | async-start | bytes 2297856 | tf_op jit(solution)/shard_map/all_gather | solution.py:66
  7.2 226.1 %copy-start.11 = (f32[1,1408]{1,0:T(1,128)S(1)}, f32[1,1408]{1,0:T(1,128)}, u32[]{:S(2)}) copy-start(f32[1,1408]{1,0:T(1,128)} %param.14) | copy-start | bytes 16900
  120.5 187.6 %copy-start.12 = (s32[1,16]{1,0:T(1,128)S(1)}, s32[1,16]{1,0:T(1,128)}, u32[]{:S(2)}) copy-start(s32[1,16]{1,0:T(1,128)} %param.15) | copy-start | bytes 196
  121.4 437.8 %all-gather.9.cloned.1.call-start = ((), (), s32[]{:S(2)}) async-start(), calls=%async_computation.2 | async-start | bytes 2297856 | tf_op jit(solution)/shard_map/all_gather | solution.py:67
  233.3 79.4 %copy-start.6 = (bf16[1,1,1,256,704]{3,4,2,1,0:T(8,128)(2,1)}, bf16[1,1,1,256,704]{3,4,2,1,0:T(8,128)(2,1)S(1)}, u32[]{:S(2)}) copy-start(bf16[1,1,1,256,704]{3,4,2,1,0:T(8,128)(2,1)S(1)} %get-tuple-element.8) | copy-start | bytes 1081348
  233.3 79.4 %copy-start.8 = (bf16[1,1,1,256,704]{3,4,2,1,0:T(8,128)(2,1)}, bf16[1,1,1,256,704]{3,4,2,1,0:T(8,128)(2,1)S(1)}, u32[]{:S(2)}) copy-start(bf16[1,1,1,256,704]{3,4,2,1,0:T(8,128)(2,1)S(1)} %get-tuple-element.9) | copy-start | bytes 1081348
  233.3 81.4 %copy-start = (bf16[1,1,1,256,704]{3,4,2,1,0:T(8,128)(2,1)}, bf16[1,1,1,256,704]{3,4,2,1,0:T(8,128)(2,1)S(1)}, u32[]{:S(2)}) copy-start(bf16[1,1,1,256,704]{3,4,2,1,0:T(8,128)(2,1)S(1)} %get-tuple-element.10) | copy-start | bytes 1081348
  312.7 2.0 copy-start.3
  314.7 2.9 copy-start.10
  503.7 4.7 copy-start.13
  517.4 41.2 %all-to-all-start = ((bf16[32,2,5632]{2,1,0:T(2,128)(2,1)}), bf16[32,2,5632]{2,1,0:T(2,128)(2,1)S(1)}, u32[]{:S(2)}, u32[]{:S(2)}) async-start(bf16[32,2,5632]{2,1,0:T(2,128)(2,1)} %reshape.214), calls=%async_computation | async-start | bytes 1441792 | tf_op jit(solution)/shard_map/all_to_all | solution.py:142
  529.4 2.8 copy-start.1
  532.2 1.8 copy-start.9
  534.0 4.3 copy-start.7
  563.3 1.7 copy-start.5
  565.1 2.3 copy-start.4
Sparse Core Ops, SparseCore 0:
  121.5 103.1 all-gather.6
  233.3 121.4 all-gather.8
where the time goes:
time: 580 us; the launch traced here: 579 us
  blocking collectives  481 us (83%)
  matrix products  35 us (6%)
  between operations  16.5 us (3%)
  local copies, waits for them, and re-layouts  15.5 us (3%)
  other arithmetic  14.5 us (2%)
  waiting for transfers between devices  13 us (2%)
    all_gather x1, blocking collectives, shards(): lax.all_gather(space_proj, 'seq', axis=0, tiled=True)  113 us
    all_gather x1, blocking collectives, shards(): lax.all_gather(time_proj, 'seq', axis=0, tiled=True)  111 us
    psum x1, blocking collectives, shards(): own_row = lax.psum(partial_row, 'seq')  107 us
    unnamed x1, blocking collectives  75.1 us
    all_gather x1, blocking collectives, shards(): texts = lax.all_gather(text_emb, 'vid', axis=0, tiled=True)  74.6 us
    all_to_all x1, waiting for transfers between devices, shards(): lax.all_to_all(mixed_grad.reshape(1, frames_dev, patches, model_width), '...  12.9 us
  transfers between devices with their start and end apart: 3, of which 1 were waited for; matrix products, arithmetic and copies ran while one was open for 9% of the time, Pallas kernels for 0%

commit v1 on v0

--- a/solution.py
+++ b/solution.py
@@ -3,10 +3,14 @@
 import jax
 import jax.numpy as jnp
 from jax import lax
+from jax.sharding import Mesh
 from jax.sharding import PartitionSpec as P
 
 HEAD_DIM = 88
-
+VID = ("zh", "y", "c")
+SEQ = ("x", "zl")
+RING = ("zh", "zl")
+SIZES = {"zh": 2, "y": 4, "c": 2, "x": 4, "zl": 8}
 
 logit_scale = 20.0
 teacher_softness = 4.0
@@ -57,23 +61,64 @@
     return jnp.stack([grad_queries, grad_keys, grad_values])
 
 
+def spread(block, axes):
+    count = math.prod(SIZES[axis] for axis in axes)
+    return lax.all_to_all(jnp.broadcast_to(block[None], (count,) + block.shape), axes, 0, 0)
+
+
+def swap(block, axis):
+    return lax.ppermute(block, axis, [(0, 1), (1, 0)])
+
+
+def in_order(own, other, axis):
+    first = lax.axis_index(axis) == 0
+    return jnp.where(first, jnp.stack([own, other]), jnp.stack([other, own]))
+
+
+def gather_texts(text_emb):
+    pair = in_order(text_emb, swap(text_emb, "zh"), "zh")
+    turns = [pair] + [
+        lax.ppermute(pair, "y", [(i, (i + k) % 4) for i in range(4)]) for k in range(1, 4)
+    ]
+    turns = jnp.stack(turns)[(lax.axis_index("y") - jnp.arange(4)) % 4]
+    both = in_order(turns, swap(turns, "c"), "c")
+    return both.transpose(2, 1, 0, 3, 4).reshape(16, -1)
+
+
+def gather_projections(space_proj, time_proj):
+    rows, cols = space_proj.shape
+    pack = jnp.pad(jnp.concatenate([space_proj, time_proj]), ((0, 48 - 2 * rows), (0, 128 - cols)))
+    ring = spread(pack, RING).reshape(2, 8, 48, 128)
+
+    def columns(blocks):
+        return blocks.transpose(0, 3, 1, 2).reshape(2, cols, 8 * rows)
+
+    space = columns(ring[:, :, :rows, :cols])
+    time = columns(ring[:, :, rows : 2 * rows, :cols])
+    w_time = lax.all_gather(time, ("c", "x", "y"))
+    own = spread(space, ("x", "y"))
+    w_space = in_order(own, swap(own, "c"), "c")
+
+    def natural(w):
+        return (
+            w.reshape(2, 4, 4, 2, cols, 8 * rows)
+            .transpose(3, 2, 0, 4, 1, 5)
+            .reshape(16 * cols, 32 * rows)
+        )
+
+    return natural(w_space), natural(w_time)
+
+
 def shards(time_qkv, space_qkv, residual, space_proj, time_proj, norm_gain, text_emb, teacher):
-    rows_space, rows_time = (
-        lax.all_gather(space_proj, "seq", axis=0, tiled=True),
-        lax.all_gather(time_proj, "seq", axis=0, tiled=True),
-    )
-    w_space, w_time = (
-        lax.all_gather(rows_space, "vid", axis=1, tiled=True),
-        lax.all_gather(rows_time, "vid", axis=1, tiled=True),
-    )
+    w_space, w_time = gather_projections(space_proj, time_proj)
     model_width = residual.shape[3]
     frames_dev = residual.shape[1]
     patches = residual.shape[2]
-    head_width = w_space.shape[0]
+    head_width = w_space.shape[1]
     head_count = head_width // HEAD_DIM
-    frames = frames_dev * lax.axis_size("seq")
+    frames = frames_dev * 32
     patch_dev = time_qkv.shape[3]
-    videos = lax.axis_size("vid")
+    videos = 16
     token_count = frames_dev * patches
     space_parts = [
         space_qkv[slot, 0].reshape(frames_dev, patches, head_count, HEAD_DIM) for slot in range(3)
@@ -83,8 +128,8 @@
         "bhlm,bmhe->blhe", weights_low, space_parts[2], preferred_element_type=jnp.float32
     ).astype(jnp.bfloat16)
     attended = attended.reshape(token_count, head_width)
-    mixed_sum = residual[0].reshape(token_count, model_width).astype(jnp.float32) + jnp.dot(
-        attended, w_space, preferred_element_type=jnp.float32
+    mixed_sum = residual[0].reshape(token_count, model_width).astype(jnp.float32) + jnp.einsum(
+        "ta,da->td", attended, w_space, preferred_element_type=jnp.float32
     )
     center = mixed_sum - jnp.mean(mixed_sum, axis=-1, keepdims=True)
     inv_scale = 1.0 / jnp.sqrt(jnp.mean(center * center, axis=-1, keepdims=True) + 1e-05)
@@ -94,13 +139,15 @@
     )
     frame_norm = jnp.sqrt(jnp.sum(frame_emb * frame_emb, axis=-1, keepdims=True) + 1e-06)
     frame_unit = frame_emb / frame_norm
-    texts = lax.all_gather(text_emb, "vid", axis=0, tiled=True)
+    texts = gather_texts(text_emb)
     text_unit = texts / jnp.sqrt(jnp.sum(texts * texts, axis=-1, keepdims=True) + 1e-06)
     frame_cosines = jnp.dot(frame_unit, text_unit.T, precision=lax.Precision.HIGHEST)
     partial_row = logit_scale / frames * jnp.sum(frame_cosines, axis=0)
-    own_row = lax.psum(partial_row, "seq")
-    all_scores = lax.all_gather(own_row[None, :], "vid", axis=0, tiled=True)
-    own_video = lax.axis_index("vid")
+    along_ring = spread(partial_row, RING).reshape(2, 8, videos).sum(1)
+    everywhere = spread(along_ring, ("y", "c", "x")).reshape(4, 2, 4, 2, videos).sum(2)
+    all_scores = everywhere.transpose(2, 0, 1, 3).reshape(videos, videos)
+    own_video = lax.axis_index(VID)
+    own_row = lax.dynamic_index_in_dim(all_scores, own_video, 0, False)
     one_hot = (jnp.arange(videos) == own_video).astype(jnp.float32)
     own_exp = jnp.exp(own_row)
     row_soft = own_exp / jnp.sum(own_exp)
@@ -125,8 +172,12 @@
     mixed_grad = (inv_scale * (token_grad - mean_grad - normalized_rows * mean_cross)).astype(
         jnp.bfloat16
     )
+    time_out_grad = jnp.einsum(
+        "td,da->ta", mixed_grad, w_time, preferred_element_type=jnp.float32
+    ).astype(jnp.bfloat16)
+    moved = lax.all_to_all(time_out_grad.reshape(32, patch_dev, head_width), SEQ, 0, 0)
     space_out_grad = jnp.einsum(
-        "td,ad->ta", mixed_grad, w_space, preferred_element_type=jnp.float32
+        "td,da->ta", mixed_grad, w_space, preferred_element_type=jnp.float32
     ).astype(jnp.bfloat16)
     space_out_grad = space_out_grad.reshape(frames_dev, patches, head_count, HEAD_DIM)
     space_grad = attention_back(
@@ -139,20 +190,7 @@
         space_layout,
     )
     space_grad = space_grad.reshape(3, 1, frames_dev, patches, head_width)
-    moved = lax.all_to_all(
-        mixed_grad.reshape(1, frames_dev, patches, model_width),
-        "seq",
-        split_axis=2,
-        concat_axis=1,
-        tiled=True,
-    )
-    time_out_grad = jnp.einsum(
-        "td,ad->ta",
-        moved.reshape(frames * patch_dev, model_width),
-        w_time,
-        preferred_element_type=jnp.float32,
-    ).astype(jnp.bfloat16)
-    time_out_grad = time_out_grad.reshape(frames, patch_dev, head_count, HEAD_DIM)
+    time_out_grad = moved.reshape(frames, patch_dev, head_count, HEAD_DIM)
     time_parts = [
         time_qkv[slot, 0].reshape(frames, patch_dev, head_count, HEAD_DIM) for slot in range(3)
     ]
@@ -171,19 +209,20 @@
 
 
 def solution(mesh):
+    fine = Mesh(mesh.devices.reshape(2, 4, 2, 4, 8), ("zh", "y", "c", "x", "zl"))
     in_specs = (
-        P(None, "vid", None, "seq", None),
-        P(None, "vid", "seq", None, None),
-        P("vid", "seq", None, None),
-        P("seq", "vid"),
-        P("seq", "vid"),
+        P(None, VID, None, SEQ, None),
+        P(None, VID, SEQ, None, None),
+        P(VID, SEQ, None, None),
+        P(SEQ, VID),
+        P(SEQ, VID),
         P(),
-        P("vid", None),
-        P("vid", None),
+        P(VID, None),
+        P(VID, None),
     )
     out_specs = (
-        P(None, "vid", "seq", None, None),
-        P(None, "vid", None, "seq", None),
-        P("vid", None),
-    )
-    return jax.shard_map(shards, mesh=mesh, in_specs=in_specs, out_specs=out_specs, check_vma=False)
+        P(None, VID, SEQ, None, None),
+        P(None, VID, None, SEQ, None),
+        P(VID, None),
+    )
+    return jax.shard_map(shards, mesh=fine, in_specs=in_specs, out_specs=out_specs, check_vma=False)

time: 580 us -> 220 us (0.38)
  blocking collectives: 481 us -> 0 us
  starting transfers between devices: 4.21 us -> 70.2 us
  local copies, waits for them, and re-layouts: 15.5 us -> 56.2 us
  waiting for transfers between devices: 13 us -> 28.5 us
    all_gather x3 -> x0, blocking collectives: 299 us -> none  [the longest x1 113 us: shards(): lax.all_gather(space_proj, 'seq', axis=0, tiled=True)]
    psum x1 -> x0, blocking collectives: 107 us -> none  [shards(): own_row = lax.psum(partial_row, 'seq')]
    unnamed x1 -> x0, blocking collectives: 75.1 us -> none
    all_to_all x1 -> x5, starting transfers between devices: 4.13 us -> 38.8 us  [the longest x4 34.2 us: spread(): lax.all_to_all(jnp.broadcast_to(block[None], (count,) + block.shape), axe...]
    ppermute x0 -> x6, starting transfers between devices: none -> 31.3 us  [the longest x3 21.9 us: swap(): return lax.ppermute(block, axis, [(0, 1), (1, 0)])]
    reshape x2 -> x4, local copies, waits for them, and re-layouts: 1.74 us -> 30.4 us  [the longest x2 18 us: natural(): return w.reshape(2, 4, 4, 2, cols, 8 * rows).transpose(3, 2, 0, 4, 1, 5)....]
    all_to_all x1 -> x5, waiting for transfers between devices: 12.9 us -> 23.9 us  [the longest x1 12.9 us: shards(): lax.all_to_all(time_out_grad.reshape(32, patch_dev, head_width), SEQ, 0, 0)]
    transpose x0 -> x5, local copies, waits for them, and re-layouts: none -> 8.91 us  [the longest x1 7.15 us: natural(): return w.reshape(2, 4, 4, 2, cols, 8 * rows).transpose(3, 2, 0, 4, 1, 5)....]
  transfers between devices with their start and end apart: 3 -> 12, of which waited for: 1 -> 5; matrix products, arithmetic and copies ran while one was open for 9% -> 29% of each run, Pallas kernels for 0% -> 0%
where the time goes in v1:
time: 220 us; the launch traced here: 218 us
  starting transfers between devices  70.2 us (32%)
  local copies, waits for them, and re-layouts  56.2 us (26%)
  matrix products  31.6 us (14%)
  waiting for transfers between devices  28.5 us (13%)
  between operations  16 us (7%)
  other arithmetic  15.7 us (7%)
    all_to_all x4, starting transfers between devices, spread(): lax.all_to_all(jnp.broadcast_to(block[None], (count,) + block.shape), axe...  34.2 us
    ppermute x3, starting transfers between devices, swap(): return lax.ppermute(block, axis, [(0, 1), (1, 0)])  21.9 us
    reshape x2, local copies, waits for them, and re-layouts, natural(): return w.reshape(2, 4, 4, 2, cols, 8 * rows).transpose(3, 2, 0, 4, 1, 5)....  18 us
    all_to_all x1, waiting for transfers between devices, shards(): lax.all_to_all(time_out_grad.reshape(32, patch_dev, head_width), SEQ, 0, 0)  12.9 us
    all_to_all x4, waiting for transfers between devices, spread(): lax.all_to_all(jnp.broadcast_to(block[None], (count,) + block.shape), axe...  11 us
    reshape x1, local copies, waits for them, and re-layouts, natural(): w.reshape(2, 4, 4, 2, cols, 8 * rows).transpose(3, 2, 0, 4, 1, 5)  10.8 us
    ppermute x3, starting transfers between devices, gather_texts(): lax.ppermute(pair, 'y', [(i, (i + k) % 4) for i in range(4)])  9.45 us
    transpose x1, local copies, waits for them, and re-layouts, natural(): return w.reshape(2, 4, 4, 2, cols, 8 * rows).transpose(3, 2, 0, 4, 1, 5)....  7.15 us
  transfers between devices with their start and end apart: 12, of which 5 were waited for; matrix products, arithmetic and copies ran while one was open for 29% of the time, Pallas kernels for 0%

profile of v1, /device:TPU:1, one launch (start us, length us, event | category | flops | bytes accessed | tf_op | source)
XLA Modules:
  0.0 218.2 jit_solution(1915947489718873268)
XLA Ops:
  8.6 15.7 %all-to-all-start = ((bf16[16,48,128]{2,1,0:T(8,128)(2,1)}), bf16[16,48,128]{2,1,0:T(8,128)(2,1)S(1)}, u32[]{:S(2)}, u32[]{:S(2)}) async-start(bf16[16,48,128]{2,1,0:T(8,128)(2,1)} %broadcast_in_dim.10), calls=%async_computation | async-start | bytes 393216 | tf_op jit(solution)/shard_map/all_to_all | solution.py:66
  24.3 12.0 %collective-permute-start.1 = (f32[1,1408]{1,0:T(1,128)}, f32[1,1408]{1,0:T(1,128)S(1)}, u32[]{:S(2)}, u32[]{:S(2)}) collective-permute-start(f32[1,1408]{1,0:T(1,128)} %param.14), channel_id=1, source_target_pairs={{0,256},{256,0},{1,257},{257,1},{2,258},{258,2},{3,259},{259,3},{4... | collective-permute-start | bytes 16904 | tf_op jit(solution)/shard_map/ppermute | solution.py:70
  37.6 2.2 fusion.90
  41.9 6.8 %all-to-all-start.1 = ((bf16[16,2,88,176]{3,2,1,0:T(8,128)(2,1)}), bf16[16,2,88,176]{3,2,1,0:T(8,128)(2,1)S(1)}, u32[]{:S(2)}, u32[]{:S(2)}) async-start(bf16[16,2,88,176]{3,2,1,0:T(8,128)(2,1)} %broadcast_in_dim.12), calls=%async_computation.1 | async-start | bytes 2883584 | tf_op jit(solution)/shard_map/all_to_all | solution.py:66
  48.8 2.7 %convolution_convert_fusion.4 = bf16[8,256,88]{1,2,0:T(8,128)(2,1)} fusion(bf16[256,8,88]{0,2,1:T(8,128)(2,1)S(1)} %bitcast.133, f32[8,256,256]{1,2,0:T(8,128)} %get-tuple-element.16, f32[8,256]{1,0:T(8,128)S(1)} %get-tuple-element.15), kind=kOutput, calls=%fused_computation.34 | convolution fusion | flops 93503488 | bytes 2826240 | tf_op jit(solution)/shard_map/bhlm,bmhe->blhe/dot_general | solution.py:127
  51.6 4.5 %collective-permute-start.4 = (f32[2,1,1408]{2,0,1:T(2,128)S(1)}, f32[2,1,1408]{2,0,1:T(2,128)S(1)}, u32[]{:S(2)}, u32[]{:S(2)}) collective-permute-start(f32[2,1,1408]{2,0,1:T(2,128)S(1)} %maximum_select_fusion.3), channel_id=1, source_target_pairs={{0,192},{64,0},{128,64},{192,128},{1,193},{65,1},{129,65},{193,129... | collective-permute-start | bytes 33800 | tf_op jit(solution)/shard_map/ppermute | solution.py:81
  56.1 2.5 %collective-permute-start.3 = (f32[2,1,1408]{2,0,1:T(2,128)S(1)}, f32[2,1,1408]{2,0,1:T(2,128)S(1)}, u32[]{:S(2)}, u32[]{:S(2)}) collective-permute-start(f32[2,1,1408]{2,0,1:T(2,128)S(1)} %maximum_select_fusion.3), channel_id=1, source_target_pairs={{0,128},{64,192},{128,0},{192,64},{1,129},{65,193},{129,1},{193,65... | collective-permute-start | bytes 33800 | tf_op jit(solution)/shard_map/ppermute | solution.py:81
  58.6 2.5 %collective-permute-start.2 = (f32[2,1,1408]{2,0,1:T(2,128)S(1)}, f32[2,1,1408]{2,0,1:T(2,128)S(1)}, u32[]{:S(2)}, u32[]{:S(2)}) collective-permute-start(f32[2,1,1408]{2,0,1:T(2,128)S(1)} %maximum_select_fusion.3), channel_id=1, source_target_pairs={{0,64},{64,128},{128,192},{192,0},{1,65},{65,129},{129,193},{193,1... | collective-permute-start | bytes 33800 | tf_op jit(solution)/shard_map/ppermute | solution.py:81
  61.1 2.0 collective-permute-done.3
  63.1 2.5 %collective-permute-done.2 = f32[2,1,1408]{2,0,1:T(2,128)S(1)} collective-permute-done((f32[2,1,1408]{2,0,1:T(2,128)S(1)}, f32[2,1,1408]{2,0,1:T(2,128)S(1)}, u32[]{:S(2)}, u32[]{:S(2)}) %collective-permute-start.2) | collective-permute-done | bytes 11296 | tf_op jit(solution)/shard_map/ppermute | solution.py:81
  66.3 8.0 %collective-permute-start.5 = (f32[4,2,1,1408]{3,1,0,2:T(2,128)S(1)}, f32[4,2,1,1408]{3,1,0,2:T(2,128)S(1)}, u32[]{:S(2)}, u32[]{:S(2)}) collective-permute-start(f32[4,2,1,1408]{3,1,0,2:T(2,128)S(1)} %bitcast.148), channel_id=1, source_target_pairs={{0,32},{32,0},{1,33},{33,1},{2,34},{34,2},{3,35},{35,3},{4,36},{36... | collective-permute-start | bytes 135176 | tf_op jit(solution)/shard_map/ppermute | solution.py:70
  82.1 3.7 %fusion.4 = bf16[2,4,2,88,4,176]{5,3,0,1,4,2:T(8,128)(2,1)S(1)} fusion(bf16[1,4,4,2,88,176]{5,4,3,2,1,0:T(8,128)(2,1)} %bitcast.12, bf16[1,4,4,2,88,176]{5,4,3,2,1,0:T(8,128)(2,1)} %bitcast.130, pred[]{:T(512)S(6)} %eq.23), kind=kLoop, calls=%fused_computation.6 | loop fusion | flops 2973696 | bytes 3964929 | tf_op jit(solution)/shard_map/transpose | solution.py:105
  85.8 7.1 %copy.140 = bf16[2,4,2,88,4,176]{3,2,1,0,5,4:T(2,128)(2,1)} copy(bf16[2,4,2,88,4,176]{5,3,0,1,4,2:T(8,128)(2,1)S(1)} %fusion.4) | data formatting | bytes 3964928 | tf_op jit(solution)/shard_map/transpose | solution.py:105
  93.0 8.6 %reshape.501 = bf16[1408,704]{0,1:T(8,128)(2,1)S(1)} reshape(bf16[2,4,2,88,4,176]{3,2,1,0,5,4:T(2,128)(2,1)} %copy.140) | data formatting | bytes 3964928 | tf_op jit(solution)/shard_map/reshape | solution.py:106
  101.6 2.1 fusion.91
  106.8 5.0 %all-to-all-start.2 = ((f32[16,1,16]{2,1,0:T(1,128)}), f32[16,1,16]{2,1,0:T(1,128)S(1)}, u32[]{:S(2)}, u32[]{:S(2)}) async-start(f32[16,1,16]{2,1,0:T(1,128)} %broadcast_in_dim.13), calls=%async_computation.2 | async-start | bytes 16384 | tf_op jit(solution)/shard_map/all_to_all | solution.py:66
  111.8 3.7 %fusion.92 = (f32[8,8,32]{2,1,0:T(8,128)}, f32[8,8,32,32]{2,3,1,0:T(8,128)}) fusion(bf16[32,8,8,88]{3,2,1,0:T(8,128)(2,1)} %reshape_squeeze.14, bf16[32,8,8,88]{3,2,1,0:T(8,128)(2,1)} %reshape_squeeze.6), kind=kOutput, calls=%fused_computation.128 | convolution fusion | flops 11730975 | bytes 991232 | tf_op jit(solution)/shard_map/sub | solution.py:29
  115.5 7.5 %all-to-all-done.2 = f32[16,1,16]{2,1,0:T(1,128)S(1)} async-done(((f32[16,1,16]{2,1,0:T(1,128)}), f32[16,1,16]{2,1,0:T(1,128)S(1)}, u32[]{:S(2)}, u32[]{:S(2)}) %all-to-all-start.2) | async-done | bytes 1056 | tf_op jit(solution)/shard_map/all_to_all | solution.py:66
  123.7 6.7 %all-to-all-start.3 = ((f32[32,2,16]{2,1,0:T(2,128)}), f32[32,2,16]{2,1,0:T(2,128)S(1)}, u32[]{:S(2)}, u32[]{:S(2)}) async-start(f32[32,2,16]{2,1,0:T(2,128)} %broadcast_in_dim.14), calls=%async_computation.3 | async-start | bytes 65536 | tf_op jit(solution)/shard_map/all_to_all | solution.py:66
  131.6 2.5 %reshape_squeeze.15 = bf16[32,8,8,88]{3,2,1,0:T(8,128)(2,1)} reshape(bf16[1,1,32,8,704]{4,3,2,1,0:T(8,128)(2,1)} %get-tuple-element.7) | data formatting | bytes 720896 | tf_op jit(solution)/shard_map/reshape;squeeze | solution.py:195
  134.1 3.4 %all-to-all-done.3 = f32[32,2,16]{2,1,0:T(2,128)S(1)} async-done(((f32[32,2,16]{2,1,0:T(2,128)}), f32[32,2,16]{2,1,0:T(2,128)S(1)}, u32[]{:S(2)}, u32[]{:S(2)}) %all-to-all-start.3) | async-done | bytes 4128 | tf_op jit(solution)/shard_map/all_to_all | solution.py:66
  144.8 10.8 %copy.154 = bf16[2,4,4,2,88,176]{4,0,2,3,5,1:T(2,128)(2,1)} copy(bf16[2,4,4,2,88,176]{5,4,3,2,1,0:T(8,128)(2,1)} %bitcast.131) | data formatting | bytes 3964928 | tf_op jit(solution)/shard_map/reshape | solution.py:104
  155.5 9.4 %reshape.509 = bf16[1408,704]{0,1:T(8,128)(2,1)} reshape(bf16[2,4,2,88,4,176]{3,2,1,0,5,4:T(2,128)(2,1)} %bitcast.129) | data formatting | bytes 3964928 | tf_op jit(solution)/shard_map/reshape | solution.py:106
  164.9 3.2 %convolution_convert_fusion.5 = bf16[256,704]{0,1:T(8,128)(2,1)} fusion(bf16[1408,704]{0,1:T(8,128)(2,1)} %reshape.509, f32[256,1408]{1,0:T(8,128)S(1)} %get-tuple-element.18, f32[256]{0:T(256)S(1)} %broadcast_multiply_fusion, f32[1408]{0:T(1024)S(1)} %broadcast_subtract_fusion, f32[256]{0:T(256)S(1)} %copy-done.19, f32[256]{0:T(256)S(1)} %copy-done.17), kind=kOutput, calls=%fused_computation.35 | convolution fusion | flops 509853696 | bytes 3793408 | tf_op jit(solution)/shard_map/td,da->ta/dot_general | solution.py:175
  170.0 4.6 %all-to-all-start.4 = ((bf16[32,8,704]{2,1,0:T(8,128)(2,1)}), bf16[32,8,704]{2,1,0:T(8,128)(2,1)}, u32[]{:S(2)}, u32[]{:S(2)}) async-start(bf16[32,8,704]{2,1,0:T(8,128)(2,1)} %bitcast.132), calls=%async_computation.4 | async-start | bytes 786432 | tf_op jit(solution)/shard_map/all_to_all | solution.py:178
  176.7 3.0 %fusion.24 = bf16[8,256,88]{1,2,0:T(8,128)(2,1)S(1)} fusion(bf16[256,8,88]{0,2,1:T(8,128)(2,1)S(1)} %bitcast.141, f32[8,256,256]{1,2,0:T(8,128)S(1)} %fusion.97, f32[8,256,256]{1,2,0:T(8,128)} %get-tuple-element.16, f32[8,256]{1,0:T(8,128)S(1)} %copy-done.22), kind=kOutput, calls=%fused_computation.32 | convolution fusion | flops 96127232 | bytes 4923392 | tf_op jit(solution)/shard_map/bhlm,blhe->bmhe/dot_general | solution.py:49
  179.8 3.0 %fusion.21 = bf16[8,256,88]{1,2,0:T(8,128)(2,1)S(1)} fusion(bf16[256,8,88]{0,2,1:T(8,128)(2,1)S(1)} %bitcast.139, f32[8,256,256]{1,2,0:T(8,128)S(1)} %fusion.97, f32[8,256,256]{1,2,0:T(8,128)} %get-tuple-element.16, f32[8,256]{1,0:T(8,128)S(1)} %copy-done.22), kind=kOutput, calls=%fused_computation.31 | convolution fusion | flops 96127232 | bytes 4923392 | tf_op jit(solution)/shard_map/bhlm,bmhe->blhe/dot_general | solution.py:43
  182.8 2.0 convolution_convert_fusion.3
  185.9 12.9 %all-to-all-done.4 = bf16[32,8,704]{2,1,0:T(8,128)(2,1)} async-done(((bf16[32,8,704]{2,1,0:T(8,128)(2,1)}), bf16[32,8,704]{2,1,0:T(8,128)(2,1)}, u32[]{:S(2)}, u32[]{:S(2)}) %all-to-all-start.4) | async-done | bytes 360480 | tf_op jit(solution)/shard_map/all_to_all | solution.py:178
  201.2 2.5 %fusion.29 = bf16[32,8,8,88]{3,0,2,1:T(8,128)(2,1)} fusion(bf16[32,8,8,88]{3,2,1,0:T(8,128)(2,1)S(1)} %reshape.511, f32[8,8,32,32]{2,3,1,0:T(8,128)} %get-tuple-element.20, f32[8,8,32]{2,1,0:T(8,128)S(1)} %copy-done.23), kind=kOutput, calls=%fused_computation.39 | convolution fusion | flops 11845632 | bytes 991232 | tf_op jit(solution)/shard_map/bhlm,lbhe->mbhe/dot_general | solution.py:55
  203.8 2.3 %fusion.28 = bf16[32,8,8,88]{3,0,2,1:T(8,128)(2,1)S(1)} fusion(f32[8,8,32,32]{2,3,1,0:T(8,128)S(1)} %fusion.39, bf16[32,8,8,88]{3,2,1,0:T(8,128)(2,1)S(1)} %copy-done.6, f32[8,8,32,32]{2,3,1,0:T(8,128)} %get-tuple-element.20, f32[8,8,32]{2,1,0:T(8,128)S(1)} %copy-done.23), kind=kOutput, calls=%fused_computation.38 | convolution fusion | flops 12175391 | bytes 1253376 | tf_op jit(solution)/shard_map/bhlm,lbhe->mbhe/dot_general | solution.py:49
  206.1 2.3 %fusion.27 = bf16[32,8,8,88]{3,0,2,1:T(8,128)(2,1)S(1)} fusion(f32[8,8,32,32]{2,3,1,0:T(8,128)S(1)} %fusion.39, bf16[32,8,8,88]{3,2,1,0:T(8,128)(2,1)S(1)} %copy-done.5, f32[8,8,32,32]{2,3,1,0:T(8,128)} %get-tuple-element.20, f32[8,8,32]{2,1,0:T(8,128)S(1)} %copy-done.23), kind=kOutput, calls=%fused_computation.37 | convolution fusion | flops 12175391 | bytes 1253376 | tf_op jit(solution)/shard_map/bhlm,mbhe->lbhe/dot_general | solution.py:43
  (117 shorter events, 34.3 us)
Async XLA Ops:
  8.6 31.2 %all-to-all-start = ((bf16[16,48,128]{2,1,0:T(8,128)(2,1)}), bf16[16,48,128]{2,1,0:T(8,128)(2,1)S(1)}, u32[]{:S(2)}, u32[]{:S(2)}) async-start(bf16[16,48,128]{2,1,0:T(8,128)(2,1)} %broadcast_in_dim.10), calls=%async_computation | async-start | bytes 393216 | tf_op jit(solution)/shard_map/all_to_all | solution.py:66
  24.3 27.2 %collective-permute-start.1 = (f32[1,1408]{1,0:T(1,128)}, f32[1,1408]{1,0:T(1,128)S(1)}, u32[]{:S(2)}, u32[]{:S(2)}) collective-permute-start(f32[1,1408]{1,0:T(1,128)} %param.14), channel_id=1, source_target_pairs={{0,256},{256,0},{1,257},{257,1},{2,258},{258,2},{3,259},{259,3},{4... | collective-permute-start | bytes 16904 | tf_op jit(solution)/shard_map/ppermute | solution.py:70
  37.6 2.2 %copy-start.8 = (bf16[1,1,1,256,704]{3,4,2,1,0:T(8,128)(2,1)}, bf16[1,1,1,256,704]{3,4,2,1,0:T(8,128)(2,1)S(1)}, u32[]{:S(2)}) copy-start(bf16[1,1,1,256,704]{3,4,2,1,0:T(8,128)(2,1)S(1)} %get-tuple-element.10) | copy-start | bytes 1081348
  37.6 4.3 %copy-start.10 = (bf16[1,1,1,256,704]{3,4,2,1,0:T(8,128)(2,1)}, bf16[1,1,1,256,704]{3,4,2,1,0:T(8,128)(2,1)S(1)}, u32[]{:S(2)}) copy-start(bf16[1,1,1,256,704]{3,4,2,1,0:T(8,128)(2,1)S(1)} %get-tuple-element.11) | copy-start | bytes 1081348
  37.6 11.1 %copy-start.2 = (bf16[1,1,1,256,704]{3,4,2,1,0:T(8,128)(2,1)}, bf16[1,1,1,256,704]{3,4,2,1,0:T(8,128)(2,1)S(1)}, u32[]{:S(2)}) copy-start(bf16[1,1,1,256,704]{3,4,2,1,0:T(8,128)(2,1)S(1)} %get-tuple-element.12) | copy-start | bytes 1081348
  39.8 8.9 %copy-start.21 = (f32[8,256]{1,0:T(8,128)}, f32[8,256]{1,0:T(8,128)S(1)}, u32[]{:S(2)}) copy-start(f32[8,256]{1,0:T(8,128)S(1)} %get-tuple-element.15) | copy-start | bytes 24580
  41.9 32.4 %all-to-all-start.1 = ((bf16[16,2,88,176]{3,2,1,0:T(8,128)(2,1)}), bf16[16,2,88,176]{3,2,1,0:T(8,128)(2,1)S(1)}, u32[]{:S(2)}, u32[]{:S(2)}) async-start(bf16[16,2,88,176]{3,2,1,0:T(8,128)(2,1)} %broadcast_in_dim.12), calls=%async_computation.1 | async-start | bytes 2883584 | tf_op jit(solution)/shard_map/all_to_all | solution.py:66
  48.7 96.1 %all-gather.2.cloned.1.call-start = ((), (), s32[]{:S(2)}) async-start(), calls=%async_computation.5 | async-start | bytes 2973696 | tf_op jit(solution)/shard_map/all_gather | solution.py:98
  48.7 2.8 %copy-start.15 = (f32[1,1408]{1,0:T(1,128)S(1)}, f32[1,1408]{1,0:T(1,128)}, u32[]{:S(2)}) copy-start(f32[1,1408]{1,0:T(1,128)} %param.14) | copy-start | bytes 16900
  48.8 27.5 %copy-start.4 = (bf16[3,1,32,8,704]{4,3,2,1,0:T(8,128)(2,1)S(1)}, bf16[3,1,32,8,704]{4,3,2,1,0:T(8,128)(2,1)}, u32[]{:S(2)}) copy-start(bf16[3,1,32,8,704]{4,3,2,1,0:T(8,128)(2,1)} %param.8) | copy-start | bytes 3244036
  51.6 9.5 %collective-permute-start.4 = (f32[2,1,1408]{2,0,1:T(2,128)S(1)}, f32[2,1,1408]{2,0,1:T(2,128)S(1)}, u32[]{:S(2)}, u32[]{:S(2)}) collective-permute-start(f32[2,1,1408]{2,0,1:T(2,128)S(1)} %maximum_select_fusion.3), channel_id=1, source_target_pairs={{0,192},{64,0},{128,64},{192,128},{1,193},{65,1},{129,65},{193,129... | collective-permute-start | bytes 33800 | tf_op jit(solution)/shard_map/ppermute | solution.py:81
  56.1 7.1 %collective-permute-start.3 = (f32[2,1,1408]{2,0,1:T(2,128)S(1)}, f32[2,1,1408]{2,0,1:T(2,128)S(1)}, u32[]{:S(2)}, u32[]{:S(2)}) collective-permute-start(f32[2,1,1408]{2,0,1:T(2,128)S(1)} %maximum_select_fusion.3), channel_id=1, source_target_pairs={{0,128},{64,192},{128,0},{192,64},{1,129},{65,193},{129,1},{193,65... | collective-permute-start | bytes 33800 | tf_op jit(solution)/shard_map/ppermute | solution.py:81
  58.6 7.1 %collective-permute-start.2 = (f32[2,1,1408]{2,0,1:T(2,128)S(1)}, f32[2,1,1408]{2,0,1:T(2,128)S(1)}, u32[]{:S(2)}, u32[]{:S(2)}) collective-permute-start(f32[2,1,1408]{2,0,1:T(2,128)S(1)} %maximum_select_fusion.3), channel_id=1, source_target_pairs={{0,64},{64,128},{128,192},{192,0},{1,65},{65,129},{129,193},{193,1... | collective-permute-start | bytes 33800 | tf_op jit(solution)/shard_map/ppermute | solution.py:81
  66.3 13.7 %collective-permute-start.5 = (f32[4,2,1,1408]{3,1,0,2:T(2,128)S(1)}, f32[4,2,1,1408]{3,1,0,2:T(2,128)S(1)}, u32[]{:S(2)}, u32[]{:S(2)}) collective-permute-start(f32[4,2,1,1408]{3,1,0,2:T(2,128)S(1)} %bitcast.148), channel_id=1, source_target_pairs={{0,32},{32,0},{1,33},{33,1},{2,34},{34,2},{3,35},{35,3},{4,36},{36... | collective-permute-start | bytes 135176 | tf_op jit(solution)/shard_map/ppermute | solution.py:70
  74.3 5.7 %copy-start = (bf16[16,2,88,176]{3,2,1,0:T(8,128)(2,1)}, bf16[16,2,88,176]{3,2,1,0:T(8,128)(2,1)S(1)}, u32[]{:S(2)}) copy-start(bf16[16,2,88,176]{3,2,1,0:T(8,128)(2,1)S(1)} %all-to-all-done.1) | copy-start | bytes 2973700
  74.3 7.8 %collective-permute-start = (bf16[16,2,88,176]{3,2,1,0:T(8,128)(2,1)S(1)}, bf16[16,2,88,176]{3,2,1,0:T(8,128)(2,1)}, u32[]{:S(2)}, u32[]{:S(2)}) collective-permute-start(bf16[16,2,88,176]{3,2,1,0:T(8,128)(2,1)S(1)} %all-to-all-done.1), channel_id=1, source_target_pairs={{0,32},{32,0},{1,33},{33,1},{2,34},{34,2},{3,35},{35,3},{4,36},{36... | collective-permute-start | bytes 2973704 | tf_op jit(solution)/shard_map/ppermute | solution.py:70
  101.6 2.4 %copy-start.14 = (f32[1408]{0:T(1024)S(1)}, f32[1408]{0:T(1024)}, u32[]{:S(2)}) copy-start(f32[1408]{0:T(1024)} %param.13) | copy-start | bytes 16900
  106.8 16.3 %all-to-all-start.2 = ((f32[16,1,16]{2,1,0:T(1,128)}), f32[16,1,16]{2,1,0:T(1,128)S(1)}, u32[]{:S(2)}, u32[]{:S(2)}) async-start(f32[16,1,16]{2,1,0:T(1,128)} %broadcast_in_dim.13), calls=%async_computation.2 | async-start | bytes 16384 | tf_op jit(solution)/shard_map/all_to_all | solution.py:66
  123.7 13.9 %all-to-all-start.3 = ((f32[32,2,16]{2,1,0:T(2,128)}), f32[32,2,16]{2,1,0:T(2,128)S(1)}, u32[]{:S(2)}, u32[]{:S(2)}) async-start(f32[32,2,16]{2,1,0:T(2,128)} %broadcast_in_dim.14), calls=%async_computation.3 | async-start | bytes 65536 | tf_op jit(solution)/shard_map/all_to_all | solution.py:66
  140.2 15.3 %copy-start.20 = (f32[1,16]{1,0:T(1,128)}, f32[1,16]{1,0:T(1,128)S(1)}, u32[]{:S(2)}) copy-start(f32[1,16]{1,0:T(1,128)S(1)} %multiply_add_fusion) | copy-start | bytes 196
  155.5 9.4 %copy-start.17 = (f32[256]{0:T(256)S(1)}, f32[256]{0:T(256)}, u32[]{:S(2)}) copy-start(f32[256]{0:T(256)} %copy-done.16) | copy-start | bytes 3076
  155.5 9.4 %copy-start.19 = (f32[256]{0:T(256)S(1)}, f32[256]{0:T(256)}, u32[]{:S(2)}) copy-start(f32[256]{0:T(256)} %copy-done.18) | copy-start | bytes 3076
  170.0 28.9 %all-to-all-start.4 = ((bf16[32,8,704]{2,1,0:T(8,128)(2,1)}), bf16[32,8,704]{2,1,0:T(8,128)(2,1)}, u32[]{:S(2)}, u32[]{:S(2)}) async-start(bf16[32,8,704]{2,1,0:T(8,128)(2,1)} %bitcast.132), calls=%async_computation.4 | async-start | bytes 786432 | tf_op jit(solution)/shard_map/all_to_all | solution.py:178
  174.6 1.6 copy-start.3
  175.5 1.2 copy-start.11
  176.7 3.0 %copy-start.9 = (bf16[1,1,1,256,704]{3,4,2,1,0:T(8,128)(2,1)S(1)}, bf16[1,1,1,256,704]{3,4,2,1,0:T(8,128)(2,1)}, u32[]{:S(2)}) copy-start(bf16[1,1,1,256,704]{3,4,2,1,0:T(8,128)(2,1)} %copy-done.8) | copy-start | bytes 1081348
  179.7 3.0 %copy-start.13 = (bf16[256,704]{0,1:T(8,128)(2,1)S(1)}, bf16[256,704]{0,1:T(8,128)(2,1)}, u32[]{:S(2)}) copy-start(bf16[256,704]{0,1:T(8,128)(2,1)} %copy-done.12) | copy-start | bytes 1081348
  184.8 15.7 %copy-start.1 = (bf16[32,8,8,88]{3,2,1,0:T(8,128)(2,1)S(1)}, bf16[32,8,8,88]{3,2,1,0:T(8,128)(2,1)}, u32[]{:S(2)}) copy-start(bf16[32,8,8,88]{3,2,1,0:T(8,128)(2,1)} %reshape_squeeze.15) | copy-start | bytes 1081348
  185.9 15.3 %copy-start.23 = (f32[8,8,32]{2,1,0:T(8,128)S(1)}, f32[8,8,32]{2,1,0:T(8,128)}, u32[]{:S(2)}) copy-start(f32[8,8,32]{2,1,0:T(8,128)} %get-tuple-element.19) | copy-start | bytes 24580
  201.2 2.5 %copy-start.6 = (bf16[32,8,8,88]{3,2,1,0:T(8,128)(2,1)S(1)}, bf16[32,8,8,88]{3,2,1,0:T(8,128)(2,1)}, u32[]{:S(2)}) copy-start(bf16[32,8,8,88]{3,2,1,0:T(8,128)(2,1)} %reshape_squeeze.6) | copy-start | bytes 1081348
  203.8 2.3 %copy-start.5 = (bf16[32,8,8,88]{3,2,1,0:T(8,128)(2,1)S(1)}, bf16[32,8,8,88]{3,2,1,0:T(8,128)(2,1)}, u32[]{:S(2)}) copy-start(bf16[32,8,8,88]{3,2,1,0:T(8,128)(2,1)} %reshape_squeeze.14) | copy-start | bytes 1081348
  206.1 2.4 %copy-start.7 = (bf16[32,8,8,88]{3,0,2,1:T(8,128)(2,1)S(1)}, bf16[32,8,8,88]{3,0,2,1:T(8,128)(2,1)}, u32[]{:S(2)}) copy-start(bf16[32,8,8,88]{3,0,2,1:T(8,128)(2,1)} %fusion.29) | copy-start | bytes 1081348
  (4 other events, 3.1 us)
Sparse Core Ops, SparseCore 0:
  82.2 52.5 all-gather.1

commit v2 on v1

v2 whole, which is shorter than its diff:
```python
import functools
import math

import jax
import jax.numpy as jnp
from jax import lax
from jax.experimental import pallas as pl
from jax.experimental.pallas import tpu as pltpu
from jax.sharding import Mesh
from jax.sharding import PartitionSpec as P

HEAD_DIM = 88
HEADS = 8
ATT = 704
WIDTH = 1408
HALF = 704
TOKENS = 256
VIDEOS = 16
FRAMES = 32
PAIR = 2 * HEAD_DIM
WINDOW = 96
BACK = PAIR - WINDOW
VID = ("zh", "y", "c")
SEQ = ("x", "zl")
RING = ("zh", "zl")
SIZES = {"zh": 2, "y": 4, "c": 2, "x": 4, "zl": 8}

logit_scale = 20.0
teacher_softness = 4.0
F32 = jnp.float32
BF16 = jnp.bfloat16
ROOT = 1.0 / math.sqrt(HEAD_DIM)
VMEM = pl.BlockSpec(memory_space=pltpu.VMEM)
SMEM = pl.BlockSpec(memory_space=pltpu.SMEM)


def dot(a, b, contract):
    return lax.dot_general(a, b, (contract, ((), ())), preferred_element_type=F32)


NN = ((1,), (0,))
NT = ((1,), (1,))
TN = ((0,), (0,))


def call(kernel, out_shape, args, flops, moved, scalars=0):
    return pl.pallas_call(
        kernel,
        out_shape=out_shape,
        in_specs=[SMEM] * scalars + [VMEM] * (len(args) - scalars),
        out_specs=jax.tree.map(lambda _: VMEM, out_shape),
        compiler_params=pltpu.CompilerParams(vmem_limit_bytes=16 * 2**20),
        cost_estimate=pl.CostEstimate(flops=flops, bytes_accessed=moved, transcendentals=0),
    )(*args)


def spread(block, axes):
    count = math.prod(SIZES[axis] for axis in axes)
    return lax.all_to_all(jnp.broadcast_to(block[None], (count,) + block.shape), axes, 0, 0)


def swap(block, axis):
    return lax.ppermute(block, axis, [(0, 1), (1, 0)])


def in_order(own, other, axis):
    first = lax.axis_index(axis) == 0
    return jnp.where(first, jnp.stack([own, other]), jnp.stack([other, own]))


def gather_column_texts(text_emb):
    both = in_order(text_emb, swap(text_emb, "c"), "c")
    turns = [both] + [
        lax.ppermute(both, "y", [(i, (i + k) % 4) for i in range(4)]) for k in range(1, 4)
    ]
    return jnp.stack(turns)[(lax.axis_index("y") - jnp.arange(4)) % 4]


def halves(rows):
    parts = []
    for c in range(2):
        blocks = [(zh * 4 + y) * 2 + c for y in range(4) for zh in range(2)]
        parts.append(
            jnp.concatenate([rows[:, b * HEAD_DIM : (b + 1) * HEAD_DIM] for b in blocks], axis=1)
        )
    return parts


def split_kernel(core_ref, res_ref, gain_ref, res_out, gain_out):
    core = core_ref[0]
    for ref, out in ((res_ref, res_out), (gain_ref, gain_out)):
        parts = halves(ref[...])
        for c in range(2):
            out[core ^ c] = parts[c]


def text_kernel(core_ref, text_ref, out):
    core = core_ref[0]
    text = text_ref[...]
    unit = text / jnp.sqrt(jnp.sum(text * text, axis=1, keepdims=True) + 1e-06)
    parts = halves(unit)
    for c in range(2):
        out[core ^ c] = parts[c]


def assemble_kernel(ring_ref, space_out, time_out):
    rows = 22
    piece = lax.broadcasted_iota(jnp.int32, (48, PAIR), 0)
    column = lax.broadcasted_iota(jnp.int32, (48, PAIR), 1)
    for first, out in ((0, space_out), (rows, time_out)):
        pick = jnp.concatenate(
            [
                ((piece - first + rows * zl == column) & (piece >= first) & (piece < first + rows))
                .astype(F32)
                .astype(BF16)
                for zl in range(8)
            ]
        )
        both = []
        for zh in range(2):
            blocks = ring_ref[8 * zh : 8 * zh + 8].reshape(8 * 48, 128)
            both.append(dot(blocks, pick, TN)[:HEAD_DIM])
        whole = jnp.concatenate(both).astype(BF16)
        if len(out.shape) == 3:
            for i in range(out.shape[0]):
                out[i] = whole
        else:
            out[...] = whole


def head_rows(head):
    start = (head // 2) * PAIR + (head % 2) * BACK
    return slice(start, start + WINDOW)


def head_valid(head):
    row = lax.broadcasted_iota(jnp.int32, (WINDOW, 1), 0)
    return row < HEAD_DIM if head % 2 == 0 else row >= WINDOW - HEAD_DIM


def own_rows(block, head):
    return block[:HEAD_DIM] if head % 2 == 0 else block[WINDOW - HEAD_DIM :]


def keep(valid, block):
    return jnp.where(valid, block, jnp.zeros_like(block))


def softmax_down(scores):
    peak = jnp.max(scores, axis=0, keepdims=True)
    weights = jnp.exp(scores - peak)
    return (weights * (1.0 / jnp.sum(weights, axis=0, keepdims=True))).astype(BF16)


def slopes_down(weights, dots):
    weights = weights.astype(F32)
    delta = jnp.sum(weights * dots, axis=0, keepdims=True)
    return (weights * (dots - delta) * ROOT).astype(BF16)


def space_forward_kernel(qkv_ref, weights_out, att_out):
    pair = []
    for head in range(HEADS):
        rows, valid = head_rows(head), head_valid(head)
        scores = dot(qkv_ref[1, rows], keep(valid, qkv_ref[0, rows]), TN) * ROOT
        weights = softmax_down(scores)
        weights_out[head] = weights
        pair.append(own_rows(dot(qkv_ref[2, rows], weights, NN), head))
        if head % 2:
            att_out[head // 2] = jnp.concatenate(pair).T.astype(BF16)
            pair = []


def space_back_kernel(mixed_ref, own_ref, other_ref, qkv_ref, weights_ref, out):
    for x in range(4):
        grad = dot(mixed_ref[0], own_ref[x], NN) + dot(mixed_ref[1], other_ref[x], NN)
        grad = grad.T.astype(BF16)
        pairs = [[], [], []]
        for head in (2 * x, 2 * x + 1):
            rows, valid = head_rows(head), head_valid(head)
            grad_rows = grad[:WINDOW] if head % 2 == 0 else grad[BACK:]
            dots = dot(qkv_ref[2, rows], keep(valid, grad_rows), TN)
            weights = weights_ref[head]
            slopes = slopes_down(weights, dots)
            pairs[0].append(own_rows(dot(qkv_ref[1, rows], slopes, NN), head))
            pairs[1].append(own_rows(dot(qkv_ref[0, rows], slopes, NT), head))
            pairs[2].append(own_rows(dot(grad_rows, weights, NT), head))
        for slot in range(3):
            out[slot, x * PAIR : (x + 1) * PAIR] = jnp.concatenate(pairs[slot]).astype(BF16)


def head_lanes(head):
    start = (head * HEAD_DIM) // 128 * 128
    width = min(256, ATT - start)
    lane = lax.broadcasted_iota(jnp.int32, (1, width), 1) + (start - head * HEAD_DIM)
    return slice(start, start + width), (lane >= 0) & (lane < HEAD_DIM)


def time_forward_kernel(qkv_ref, weights_out):
    key = lax.broadcasted_iota(jnp.int32, (TOKENS, TOKENS), 0)
    query = lax.broadcasted_iota(jnp.int32, (TOKENS, TOKENS), 1)
    same = ((key ^ query) & 7) == 0
    for head in range(HEADS):
        lanes, valid = head_lanes(head)
        scores = dot(qkv_ref[1, :, lanes], keep(valid, qkv_ref[0, :, lanes]), NT) * ROOT
        weights_out[head] = softmax_down(jnp.where(same, scores, -1e30))


def time_back_kernel(grad_ref, qkv_ref, weights_ref, out, total):
    for head in range(HEADS):
        lanes, valid = head_lanes(head)
        grad = grad_ref[:, lanes]
        dots = dot(qkv_ref[2, :, lanes], keep(valid, grad), NT)
        weights = weights_ref[head]
        slopes = slopes_down(weights, dots)
        for slot, part in enumerate(
            (
                dot(slopes, qkv_ref[1, :, lanes], TN),
                dot(slopes, qkv_ref[0, :, lanes], NN),
                dot(weights, grad, NN),
            )
        ):
            total[slot, :, lanes] = jnp.where(valid, part, total[slot, :, lanes])
    out[...] = total[...].astype(BF16)


def eye():
    row = lax.broadcasted_iota(jnp.int32, (VIDEOS, 128), 0)
    column = lax.broadcasted_iota(jnp.int32, (VIDEOS, 128), 1)
    return (row == column).astype(F32)


def embed_kernel(
    att_ref, res_ref, own_ref, other_ref, gain_ref, text_ref, normed_out, inv_out, unit_out, norm_out, row_out
):
    sums = []
    for half, w_ref in enumerate((own_ref, other_ref)):
        mixed = res_ref[half].astype(F32)
        for x in range(4):
            mixed += dot(att_ref[x], w_ref[x], NT)
        sums.append(mixed)
    mean = sum(jnp.sum(s, axis=1, keepdims=True) for s in sums) / WIDTH
    sums = [s - mean for s in sums]
    square = sum(jnp.sum(s * s, axis=1, keepdims=True) for s in sums) / WIDTH
    inv = 1.0 / jnp.sqrt(square + 1e-05)
    inv_out[...] = inv
    embs = []
    for half in range(2):
        normed = sums[half] * inv
        normed_out[half] = normed
        embs.append(jnp.sum(normed, axis=0, keepdims=True) * gain_ref[half] / TOKENS)
    norm = jnp.sqrt(sum(jnp.sum(e * e, axis=1, keepdims=True) for e in embs) + 1e-06)
    norm_out[...] = norm
    cosines = jnp.zeros((VIDEOS, 1), F32)
    for half in range(2):
        unit = embs[half] / norm
        unit_out[half] = unit
        cosines += jnp.sum(text_ref[half] * unit, axis=1, keepdims=True)
    row = jnp.sum(cosines * (logit_scale / FRAMES) * eye(), axis=0, keepdims=True)
    for i in range(VIDEOS):
        row_out[i] = row


def mixed_grad_kernel(
    place_ref,
    shares_ref,
    teacher_ref,
    normed_ref,
    inv_ref,
    unit_ref,
    norm_ref,
    gain_ref,
    text_ref,
    w_ref,
    score_out,
    mixed_out,
    time_out,
):
    core, own = place_ref[0], place_ref[1]
    scores = shares_ref[...].reshape(8, 4, 2, 128).sum(axis=1)
    video = lax.broadcasted_iota(jnp.int32, scores.shape, 0) + 8 * lax.broadcasted_iota(
        jnp.int32, scores.shape, 1
    )
    lane = lax.broadcasted_iota(jnp.int32, (1, 128), 1)
    exps = jnp.exp(scores)
    own_exp = jnp.sum(jnp.sum(jnp.where(video == own, exps, 0.0), axis=0), axis=0, keepdims=True)
    own_exp = jnp.where(lane < VIDEOS, own_exp, 0.0)
    column = jnp.sum(jnp.sum(exps, axis=0), axis=0, keepdims=True)
    row_soft = own_exp / jnp.sum(own_exp, axis=1, keepdims=True)
    col_soft = own_exp / column
    teacher = jnp.exp(teacher_ref[...].astype(F32) / teacher_softness)
    teacher = jnp.where(lane < VIDEOS, teacher, 0.0)
    teacher_soft = teacher / jnp.sum(teacher, axis=1, keepdims=True)
    one_hot = (lane == own).astype(F32)
    score_grad = (row_soft - one_hot + (col_soft - one_hot)) / (2.0 * VIDEOS) + (
        row_soft - teacher_soft
    ) / VIDEOS
    score_out[...] = score_grad[:, :VIDEOS]
    pull = jnp.sum(score_grad * eye(), axis=1, keepdims=True) * (VIDEOS * logit_scale)
    direction = [jnp.sum(pull * text_ref[half], axis=0, keepdims=True) for half in range(2)]
    along = sum(
        jnp.sum(unit_ref[half] * direction[half], axis=1, keepdims=True) for half in range(2)
    )
    token = [
        (direction[half] - unit_ref[half] * along) / norm_ref[...] * gain_ref[half]
        for half in range(2)
    ]
    mean = sum(jnp.sum(t, axis=1, keepdims=True) for t in token) / WIDTH
    cross = (
        sum(jnp.sum(normed_ref[half] * token[half], axis=1, keepdims=True) for half in range(2))
        / WIDTH
    )
    inv = inv_ref[...]
    mixed = []
    for half in range(2):
        part = (inv * (token[half] - mean - normed_ref[half] * cross)).astype(BF16)
        mixed_out[half] = part
        mixed.append(part)
    parts = [
        dot(mixed[0], w_ref[core, x], NN) + dot(mixed[1], w_ref[1 - core, x], NN) for x in range(4)
    ]
    time_out[...] = jnp.concatenate(parts, axis=1).astype(BF16)


def shaped(shape, dtype):
    return jax.ShapeDtypeStruct(shape, dtype)


def shards(time_qkv, space_qkv, residual, space_proj, time_proj, norm_gain, text_emb, teacher):
    core = lax.axis_index("c")
    own_video = lax.axis_index(VID)
    rows, cols = space_proj.shape
    pack = jnp.pad(jnp.concatenate([space_proj, time_proj]), ((0, 48 - 2 * rows), (0, 128 - cols)))
    ring = spread(pack, RING)

    space = space_qkv.reshape(3, TOKENS, ATT).swapaxes(1, 2)
    space_weights, attended = call(
        space_forward_kernel,
        (shaped((HEADS, TOKENS, TOKENS), BF16), shaped((4, TOKENS, PAIR), BF16)),
        (space,),
        6 * 10**8,
        3 * 10**6,
    )
    res, gain = call(
        split_kernel,
        (shaped((2, TOKENS, HALF), BF16), shaped((2, 1, HALF), F32)),
        (core[None], residual.reshape(TOKENS, WIDTH), norm_gain[None]),
        10**8,
        2 * 10**6,
        scalars=1,
    )
    texts = gather_column_texts(text_emb)
    ring, space_weights, attended, res, gain, texts = lax.optimization_barrier(
        (ring, space_weights, attended, res, gain, texts)
    )

    space_copies, time_piece = call(
        assemble_kernel,
        (shaped((16, PAIR, PAIR), BF16), shaped((PAIR, PAIR), BF16)),
        (ring,),
        2 * 10**7,
        2 * 10**6,
    )
    w_time = lax.all_gather(time_piece, ("c", "x", "y")).reshape(2, 4, HALF, PAIR)
    w_own = lax.all_to_all(space_copies, ("x", "y"), 0, 0)

    text = call(
        text_kernel,
        shaped((2, VIDEOS, HALF), F32),
        (core[None], in_order(texts, swap(texts, "zh"), "zh").reshape(VIDEOS, WIDTH)),
        10**6,
        10**6,
        scalars=1,
    )
    time = time_qkv.reshape(3, TOKENS, ATT)
    time_weights = call(
        time_forward_kernel,
        shaped((HEADS, TOKENS, TOKENS), BF16),
        (time,),
        6 * 10**8,
        3 * 10**6,
    )
    w_own, text, time_weights = lax.optimization_barrier((w_own, text, time_weights))
    w_other = swap(w_own, "c").reshape(4, HALF, PAIR)
    w_own = w_own.reshape(4, HALF, PAIR)

    normed, inv, unit, norm, row = call(
        embed_kernel,
        (
            shaped((2, TOKENS, HALF), F32),
            shaped((TOKENS, 1), F32),
            shaped((2, 1, HALF), F32),
            shaped((1, 1), F32),
            shaped((VIDEOS, 1, 128), F32),
        ),
        (attended, res, w_own, w_other, gain, text),
        10**9,
        6 * 10**6,
    )
    ring_rows = lax.all_to_all(row, RING, 0, 0).reshape(2, 8, 128).sum(axis=1)
    shares = spread(ring_rows, ("y", "c", "x"))
    score_grad, mixed, time_grad = call(
        mixed_grad_kernel,
        (
            shaped((1, VIDEOS), F32),
            shaped((2, TOKENS, HALF), BF16),
            shaped((TOKENS, ATT), BF16),
        ),
        (
            jnp.stack([core, own_video]),
            shares,
            jnp.pad(teacher, ((0, 0), (0, 128 - VIDEOS))),
            normed,
            inv,
            unit,
            norm,
            gain,
            text,
            w_time,
        ),
        10**9,
        6 * 10**6,
        scalars=1,
    )
    moved = lax.all_to_all(time_grad.reshape(FRAMES, 8, ATT), SEQ, 0, 0).reshape(TOKENS, ATT)
    space_grad = call(
        space_back_kernel,
        shaped((3, ATT, TOKENS), BF16),
        (mixed, w_own, w_other, space, space_weights),
        2 * 10**9,
        8 * 10**6,
    )
    moved, space_grad = lax.optimization_barrier((moved, space_grad))
    time_out = pl.pallas_call(
        time_back_kernel,
        out_shape=shaped((3, TOKENS, ATT), BF16),
        in_specs=[VMEM] * 3,
        out_specs=VMEM,
        scratch_shapes=[pltpu.VMEM((3, TOKENS, ATT), F32)],
        compiler_params=pltpu.CompilerParams(vmem_limit_bytes=16 * 2**20),
        cost_estimate=pl.CostEstimate(flops=10**9, bytes_accessed=5 * 10**6, transcendentals=0),
    )(moved, time, time_weights)
    return (
        space_grad.swapaxes(1, 2).reshape(3, 1, 1, TOKENS, ATT),
        time_out.reshape(3, 1, FRAMES, 8, ATT),
        score_grad,
    )


def solution(mesh):
    fine = Mesh(mesh.devices.reshape(2, 4, 2, 4, 8), ("zh", "y", "c", "x", "zl"))
    in_specs = (
        P(None, VID, None, SEQ, None),
        P(None, VID, SEQ, None, None),
        P(VID, SEQ, None, None),
        P(SEQ, VID),
        P(SEQ, VID),
        P(),
        P(VID, None),
        P(VID, None),
    )
    out_specs = (
        P(None, VID, SEQ, None, None),
        P(None, VID, None, SEQ, None),
        P(VID, None),
    )
    return jax.shard_map(shards, mesh=fine, in_specs=in_specs, out_specs=out_specs, check_vma=False)
```

time: 220 us -> 174 us (0.79)
  local copies, waits for them, and re-layouts: 56.2 us -> 23.4 us
  matrix products: 31.6 us -> 0 us
  Pallas kernels: 0 us -> 21.7 us
  other arithmetic: 15.7 us -> 0.94 us
  waiting for transfers between devices: 28.5 us -> 39.9 us
  starting transfers between devices: 70.2 us -> 72.9 us
    reshape x4 -> x0, local copies, waits for them, and re-layouts: 30.4 us -> none  [the longest x2 18 us: natural(): return w.reshape(2, 4, 4, 2, cols, 8 * rows).transpose(3, 2, 0, 4, 1, 5)....]
    dot_general x14 -> x0, matrix products: 25.8 us -> none  [the longest x2 5.35 us: attention_back(): jnp.einsum(layout[2] + ',' + layout[0] + '->' + layout[1], slopes, querie...]
    pallas_call x0 -> x9, Pallas kernels: none -> 21.7 us  [the longest x8 17.9 us: call(): pl.pallas_call(kernel, out_shape=out_shape, in_specs=[SMEM] * scalars + [...]
    unnamed x48 -> x51, local copies, waits for them, and re-layouts: 1.06 us -> 20.1 us
    all_to_all x4 -> x2, starting transfers between devices: 34.2 us -> 16.1 us  [spread(): lax.all_to_all(jnp.broadcast_to(block[None], (count,) + block.shape), axe...]
    all_to_all x1 -> x3, starting transfers between devices: 4.59 us -> 19.8 us  [the longest x1 11.5 us: shards(): ring_rows = lax.all_to_all(row, RING, 0, 0).reshape(2, 8, 128).sum(axis=1)]
    all_to_all x1 -> x3, waiting for transfers between devices: 12.9 us -> 26.5 us  [the longest x1 12.7 us: shards(): lax.all_to_all(time_grad.reshape(FRAMES, 8, ATT), SEQ, 0, 0)]
    transpose x5 -> x0, local copies, waits for them, and re-layouts: 8.91 us -> none  [the longest x1 7.15 us: natural(): return w.reshape(2, 4, 4, 2, cols, 8 * rows).transpose(3, 2, 0, 4, 1, 5)....]
  transfers between devices with their start and end apart: 12 -> 12, of which waited for: 5 -> 7; matrix products, arithmetic and copies ran while one was open for 29% -> 2% of each run, Pallas kernels for 0% -> 8%
where the time goes in v2:
time: 174 us; the launch traced here: 173 us
  starting transfers between devices  72.9 us (42%)
  waiting for transfers between devices  39.9 us (23%)
  local copies, waits for them, and re-layouts  23.4 us (13%)
  Pallas kernels  21.7 us (12%)
  between operations  14.3 us (8%)
    ppermute x3, starting transfers between devices, swap(): return lax.ppermute(block, axis, [(0, 1), (1, 0)])  26.9 us
    unnamed x51, local copies, waits for them, and re-layouts  20.1 us
    pallas_call x8, Pallas kernels, call(): pl.pallas_call(kernel, out_shape=out_shape, in_specs=[SMEM] * scalars + [...  17.9 us
    all_to_all x2, starting transfers between devices, spread(): lax.all_to_all(jnp.broadcast_to(block[None], (count,) + block.shape), axe...  16.1 us
    all_to_all x1, waiting for transfers between devices, shards(): lax.all_to_all(time_grad.reshape(FRAMES, 8, ATT), SEQ, 0, 0)  12.7 us
    all_to_all x1, starting transfers between devices, shards(): ring_rows = lax.all_to_all(row, RING, 0, 0).reshape(2, 8, 128).sum(axis=1)  11.5 us
    all_to_all x1, waiting for transfers between devices, shards(): ring_rows = lax.all_to_all(row, RING, 0, 0).reshape(2, 8, 128).sum(axis=1)  11.3 us
    ppermute x3, starting transfers between devices, gather_column_texts(): lax.ppermute(both, 'y', [(i, (i + k) % 4) for i in range(4)])  10.1 us
  transfers between devices with their start and end apart: 12, of which 7 were waited for; matrix products, arithmetic and copies ran while one was open for 2% of the time, Pallas kernels for 8%

profile of v2, /device:TPU:1, one launch (start us, length us, event | category | flops | bytes accessed | tf_op | source)
XLA Modules:
  0.0 173.2 jit_solution(13851113542670536631)
XLA Ops:
  7.2 8.9 %collective-permute-start = (f32[1,1408]{1,0:T(1,128)}, f32[1,1408]{1,0:T(1,128)S(1)}, u32[]{:S(2)}, u32[]{:S(2)}) collective-permute-start(f32[1,1408]{1,0:T(1,128)} %param.14), channel_id=1, source_target_pairs={{0,32},{32,0},{1,33},{33,1},{2,34},{34,2},{3,35},{35,3},{4,36},{36... | collective-permute-start | bytes 16904 | tf_op jit(solution)/shard_map/ppermute | solution.py:63
  17.5 9.5 %all-to-all-start = ((bf16[16,48,128]{2,1,0:T(8,128)(2,1)}), bf16[16,48,128]{2,1,0:T(8,128)(2,1)S(1)}, u32[]{:S(2)}, u32[]{:S(2)}) async-start(bf16[16,48,128]{2,1,0:T(8,128)(2,1)} %broadcast_in_dim.6), calls=%async_computation | async-start | bytes 393216 | tf_op jit(solution)/shard_map/all_to_all | solution.py:59
  27.9 1.2 copy-done.15
  29.1 2.9 %shard_map.103 = (bf16[8,256,256]{2,1,0:T(8,128)(2,1)S(1)}, bf16[4,256,176]{2,1,0:T(8,128)(2,1)S(1)}) custom-call(bf16[3,704,256]{2,1,0:T(8,128)(2,1)S(1)} %bitcast.49), custom_call_target="tpu_custom_call" | custom-call | flops 600000000 | bytes 3000000 | tf_op jit(solution)/shard_map/pallas_call | solution.py:47
  33.8 4.8 %collective-permute-start.2 = (f32[2,1,1408]{2,1,0:T(1,128)S(1)}, f32[2,1,1408]{2,1,0:T(1,128)S(1)}, u32[]{:S(2)}, u32[]{:S(2)}) collective-permute-start(f32[2,1,1408]{2,1,0:T(1,128)S(1)} %broadcast_select_fusion), channel_id=1, source_target_pairs={{0,128},{64,192},{128,0},{192,64},{1,129},{65,193},{129,1},{193,65... | collective-permute-start | bytes 33800 | tf_op jit(solution)/shard_map/ppermute | solution.py:74
  38.6 2.7 %collective-permute-start.3 = (f32[2,1,1408]{2,1,0:T(1,128)S(1)}, f32[2,1,1408]{2,1,0:T(1,128)S(1)}, u32[]{:S(2)}, u32[]{:S(2)}) collective-permute-start(f32[2,1,1408]{2,1,0:T(1,128)S(1)} %broadcast_select_fusion), channel_id=1, source_target_pairs={{0,192},{64,0},{128,64},{192,128},{1,193},{65,1},{129,65},{193,129... | collective-permute-start | bytes 33800 | tf_op jit(solution)/shard_map/ppermute | solution.py:74
  41.3 2.6 %collective-permute-start.1 = (f32[2,1,1408]{2,1,0:T(1,128)S(1)}, f32[2,1,1408]{2,1,0:T(1,128)S(1)}, u32[]{:S(2)}, u32[]{:S(2)}) collective-permute-start(f32[2,1,1408]{2,1,0:T(1,128)S(1)} %broadcast_select_fusion), channel_id=1, source_target_pairs={{0,64},{64,128},{128,192},{192,0},{1,65},{65,129},{129,193},{193,1... | collective-permute-start | bytes 33800 | tf_op jit(solution)/shard_map/ppermute | solution.py:74
  43.9 3.0 %collective-permute-done.1 = f32[2,1,1408]{2,1,0:T(1,128)S(1)} collective-permute-done((f32[2,1,1408]{2,1,0:T(1,128)S(1)}, f32[2,1,1408]{2,1,0:T(1,128)S(1)}, u32[]{:S(2)}, u32[]{:S(2)}) %collective-permute-start.1) | collective-permute-done | bytes 11296 | tf_op jit(solution)/shard_map/ppermute | solution.py:74
  48.6 1.2 copy-done.8
  49.8 4.3 %all-to-all-start.1 = ((bf16[16,176,176]{2,1,0:T(8,128)(2,1)}), bf16[16,176,176]{2,1,0:T(8,128)(2,1)S(1)}, u32[]{:S(2)}, u32[]{:S(2)}) async-start(bf16[16,176,176]{2,1,0:T(8,128)(2,1)} %copy-done.8), calls=%async_computation.1 | async-start | bytes 2883584 | tf_op jit(solution)/shard_map/all_to_all | solution.py:365
  54.1 12.0 %collective-permute-start.4 = (f32[4,2,1,1408]{3,1,0,2:T(2,128)S(1)}, f32[4,2,1,1408]{3,1,0,2:T(2,128)S(1)}, u32[]{:S(2)}, u32[]{:S(2)}) collective-permute-start(f32[4,2,1,1408]{3,1,0,2:T(2,128)S(1)} %bitcast.53), channel_id=1, source_target_pairs={{0,256},{256,0},{1,257},{257,1},{2,258},{258,2},{3,259},{259,3},{4... | collective-permute-start | bytes 135176 | tf_op jit(solution)/shard_map/ppermute | solution.py:63
  70.4 2.6 %all-to-all-done.1 = bf16[16,176,176]{2,1,0:T(8,128)(2,1)S(1)} async-done(((bf16[16,176,176]{2,1,0:T(8,128)(2,1)}), bf16[16,176,176]{2,1,0:T(8,128)(2,1)S(1)}, u32[]{:S(2)}, u32[]{:S(2)}) %all-to-all-start.1) | async-done | bytes 991264 | tf_op jit(solution)/shard_map/all_to_all | solution.py:365
  73.0 6.0 %collective-permute-start.5 = (bf16[16,176,176]{2,1,0:T(8,128)(2,1)S(1)}, bf16[16,176,176]{2,1,0:T(8,128)(2,1)S(1)}, u32[]{:S(2)}, u32[]{:S(2)}) collective-permute-start(bf16[16,176,176]{2,1,0:T(8,128)(2,1)S(1)} %all-to-all-done.1), channel_id=1, source_target_pairs={{0,32},{32,0},{1,33},{33,1},{2,34},{34,2},{3,35},{35,3},{4,36},{36... | collective-permute-start | bytes 2973704 | tf_op jit(solution)/shard_map/ppermute | solution.py:63
  79.0 2.8 %collective-permute-done.5 = bf16[16,176,176]{2,1,0:T(8,128)(2,1)S(1)} collective-permute-done((bf16[16,176,176]{2,1,0:T(8,128)(2,1)S(1)}, bf16[16,176,176]{2,1,0:T(8,128)(2,1)S(1)}, u32[]{:S(2)}, u32[]{:S(2)}) %collective-permute-start.5) | collective-permute-done | bytes 991264 | tf_op jit(solution)/shard_map/ppermute | solution.py:63
  81.8 1.4 copy-done.11
  83.2 2.4 %shard_map.108 = (f32[2,256,704]{2,1,0:T(8,128)S(1)}, f32[256,1]{1,0:T(8,128)S(1)}, f32[2,1,704]{2,1,0:T(1,128)S(1)}, f32[1,1]{1,0:T(1,128)}, f32[16,1,128]{2,1,0:T(1,128)}) custom-call(bf16[4,256,176]{2,1,0:T(8,128)(2,1)S(1)} %copy-done.11, bf16[2,256,704]{2,1,0:T(8,128)(2,1)S(1)} %get-tuple-element.33.res_ref, bf16[4,704,176]{2,1,0:T(8,128)(2,1)S(1)} %bitcast.40, ...), custom_call_target="tpu_custom_call" | custom-call | flops 1000000000 | bytes 6000000 | tf_op jit(solution)/shard_map/pallas_call | solution.py:47
  85.6 1.2 copy-done.4
  87.4 11.5 %all-to-all-start.2 = ((f32[16,1,128]{2,1,0:T(1,128)}), f32[16,1,128]{2,1,0:T(1,128)S(1)}, u32[]{:S(2)}, u32[]{:S(2)}) async-start(f32[16,1,128]{2,1,0:T(1,128)} %get-tuple-element.40), calls=%async_computation.2 | async-start | bytes 16384 | tf_op jit(solution)/shard_map/all_to_all | solution.py:400
  98.9 11.3 %all-to-all-done.2 = f32[16,1,128]{2,1,0:T(1,128)S(1)} async-done(((f32[16,1,128]{2,1,0:T(1,128)}), f32[16,1,128]{2,1,0:T(1,128)S(1)}, u32[]{:S(2)}, u32[]{:S(2)}) %all-to-all-start.2) | async-done | bytes 8224 | tf_op jit(solution)/shard_map/all_to_all | solution.py:400
  110.8 6.5 %all-to-all-start.3 = ((f32[32,2,128]{2,1,0:T(2,128)}), f32[32,2,128]{2,1,0:T(2,128)S(1)}, u32[]{:S(2)}, u32[]{:S(2)}) async-start(f32[32,2,128]{2,1,0:T(2,128)} %broadcast_in_dim.8), calls=%async_computation.3 | async-start | bytes 65536 | tf_op jit(solution)/shard_map/all_to_all | solution.py:59
  117.4 7.1 %all-to-all-done.3.shares_ref = f32[32,2,128]{2,1,0:T(2,128)S(1)} async-done(((f32[32,2,128]{2,1,0:T(2,128)}), f32[32,2,128]{2,1,0:T(2,128)S(1)}, u32[]{:S(2)}, u32[]{:S(2)}) %all-to-all-start.3) | async-done | bytes 32800 | tf_op jit(solution)/shard_map/all_to_all | solution.py:59
  124.6 1.8 %copy-done.3 = bf16[5632,176]{1,0:T(8,128)(2,1)S(1)} copy-done((bf16[5632,176]{1,0:T(8,128)(2,1)S(1)}, bf16[5632,176]{1,0:T(8,128)(2,1)}, u32[]{:S(2)}) %copy-start.3) | copy-done | bytes 1982488
  126.4 1.4 copy-done.5
  128.7 3.6 %shard_map.109 = (f32[1,16]{1,0:T(1,128)}, bf16[2,256,704]{2,1,0:T(8,128)(2,1)S(1)}, bf16[256,704]{1,0:T(8,128)(2,1)}) custom-call(s32[2]{0:T(128)S(1)} %pad_add_fusion.place_ref, f32[32,2,128]{2,1,0:T(2,128)S(1)} %all-to-all-done.3.shares_ref, s32[1,128]{1,0:T(1,128)S(1)} %pad.9.teacher_ref, f32[2,256,704]{2,1,0:T(8,128)S(1)} %copy-done.5, ...), custom_call_target="tpu_custom_call" | custom-call | flops 1000000000 | bytes 6000000 | tf_op jit(solution)/shard_map/pallas_call | solution.py:47
  133.1 4.1 %all-to-all-start.4 = ((bf16[32,8,704]{2,1,0:T(8,128)(2,1)}), bf16[32,8,704]{2,1,0:T(8,128)(2,1)S(1)}, u32[]{:S(2)}, u32[]{:S(2)}) async-start(bf16[32,8,704]{2,1,0:T(8,128)(2,1)} %bitcast.21), calls=%async_computation.4 | async-start | bytes 786432 | tf_op jit(solution)/shard_map/all_to_all | solution.py:425
  137.2 1.4 copy-done.7
  138.6 1.2 copy-done.16
  140.9 1.2 copy-done.20
  142.2 6.5 %shard_map.110 = bf16[3,704,256]{2,1,0:T(8,128)(2,1)} custom-call(bf16[2,256,704]{2,1,0:T(8,128)(2,1)S(1)} %copy-done.18, bf16[4,704,176]{2,1,0:T(8,128)(2,1)S(1)} %bitcast.41, bf16[4,704,176]{2,1,0:T(8,128)(2,1)S(1)} %bitcast.47, bf16[3,704,256]{2,1,0:T(8,128)(2,1)S(1)} %bitcast.50, bf16[8,256,256]{2,1,0:T(8,128)(2,1)S(1)} %copy-done.20), custom_call_target="tpu_custom_call" | custom-call | flops 2000000000 | bytes 8000000 | tf_op jit(solution)/shard_map/pallas_call | solution.py:47
  148.7 12.7 %all-to-all-done.4 = bf16[32,8,704]{2,1,0:T(8,128)(2,1)S(1)} async-done(((bf16[32,8,704]{2,1,0:T(8,128)(2,1)}), bf16[32,8,704]{2,1,0:T(8,128)(2,1)S(1)}, u32[]{:S(2)}, u32[]{:S(2)}) %all-to-all-start.4) | async-done | bytes 360480 | tf_op jit(solution)/shard_map/all_to_all | solution.py:425
  161.3 1.2 copy-done.2
  162.6 3.8 %shard_map.111 = bf16[3,256,704]{2,1,0:T(8,128)(2,1)} custom-call(bf16[256,704]{1,0:T(8,128)(2,1)S(1)} %bitcast.45, bf16[3,256,704]{2,1,0:T(8,128)(2,1)S(1)} %bitcast.43, bf16[8,256,256]{2,1,0:T(8,128)(2,1)S(1)} %copy-done.2), custom_call_target="tpu_custom_call" | custom-call | flops 1000000000 | bytes 5000000 | tf_op jit(solution)/shard_map/pallas_call | solution.py:434
  (68 shorter events, 14.2 us)
Async XLA Ops:
  7.2 25.8 %copy-start.9 = (bf16[1,1,256,1408]{3,2,1,0:T(8,128)(2,1)S(1)}, bf16[1,1,256,1408]{3,2,1,0:T(8,128)(2,1)}, u32[]{:S(2)}) copy-start(bf16[1,1,256,1408]{3,2,1,0:T(8,128)(2,1)} %param.10) | copy-start | bytes 2162692
  7.2 26.6 %collective-permute-start = (f32[1,1408]{1,0:T(1,128)}, f32[1,1408]{1,0:T(1,128)S(1)}, u32[]{:S(2)}, u32[]{:S(2)}) collective-permute-start(f32[1,1408]{1,0:T(1,128)} %param.14), channel_id=1, source_target_pairs={{0,32},{32,0},{1,33},{33,1},{2,34},{34,2},{3,35},{35,3},{4,36},{36... | collective-permute-start | bytes 16904 | tf_op jit(solution)/shard_map/ppermute | solution.py:63
  17.5 30.1 %all-to-all-start = ((bf16[16,48,128]{2,1,0:T(8,128)(2,1)}), bf16[16,48,128]{2,1,0:T(8,128)(2,1)S(1)}, u32[]{:S(2)}, u32[]{:S(2)}) async-start(bf16[16,48,128]{2,1,0:T(8,128)(2,1)} %broadcast_in_dim.6), calls=%async_computation | async-start | bytes 393216 | tf_op jit(solution)/shard_map/all_to_all | solution.py:59
  27.1 97.5 %all-gather.3.cloned.1.call-start = ((), (), s32[]{:S(2)}) async-start(), calls=%async_computation.5 | async-start | bytes 2973696 | tf_op jit(solution)/shard_map/all_gather | solution.py:364
  27.9 1.2 copy-start.15
  29.1 4.7 %copy-start.23 = (f32[1,1408]{1,0:T(1,128)S(1)}, f32[1,1408]{1,0:T(1,128)}, u32[]{:S(2)}) copy-start(f32[1,1408]{1,0:T(1,128)} %param.14) | copy-start | bytes 16900
  32.0 1.0 copy-start.19
  33.8 10.2 %collective-permute-start.2 = (f32[2,1,1408]{2,1,0:T(1,128)S(1)}, f32[2,1,1408]{2,1,0:T(1,128)S(1)}, u32[]{:S(2)}, u32[]{:S(2)}) collective-permute-start(f32[2,1,1408]{2,1,0:T(1,128)S(1)} %broadcast_select_fusion), channel_id=1, source_target_pairs={{0,128},{64,192},{128,0},{192,64},{1,129},{65,193},{129,1},{193,65... | collective-permute-start | bytes 33800 | tf_op jit(solution)/shard_map/ppermute | solution.py:74
  38.6 5.3 %collective-permute-start.3 = (f32[2,1,1408]{2,1,0:T(1,128)S(1)}, f32[2,1,1408]{2,1,0:T(1,128)S(1)}, u32[]{:S(2)}, u32[]{:S(2)}) collective-permute-start(f32[2,1,1408]{2,1,0:T(1,128)S(1)} %broadcast_select_fusion), channel_id=1, source_target_pairs={{0,192},{64,0},{128,64},{192,128},{1,193},{65,1},{129,65},{193,129... | collective-permute-start | bytes 33800 | tf_op jit(solution)/shard_map/ppermute | solution.py:74
  41.3 5.6 %collective-permute-start.1 = (f32[2,1,1408]{2,1,0:T(1,128)S(1)}, f32[2,1,1408]{2,1,0:T(1,128)S(1)}, u32[]{:S(2)}, u32[]{:S(2)}) collective-permute-start(f32[2,1,1408]{2,1,0:T(1,128)S(1)} %broadcast_select_fusion), channel_id=1, source_target_pairs={{0,64},{64,128},{128,192},{192,0},{1,65},{65,129},{129,193},{193,1... | collective-permute-start | bytes 33800 | tf_op jit(solution)/shard_map/ppermute | solution.py:74
  47.6 6.5 %copy-start.21 = (f32[4,2,1408]{2,1,0:T(2,128)}, f32[4,2,1408]{2,1,0:T(2,128)S(1)}, u32[]{:S(2)}) copy-start(f32[4,2,1408]{2,1,0:T(2,128)S(1)} %gather_fusion) | copy-start | bytes 135172
  48.6 1.2 copy-start.8
  49.8 16.3 %copy-start = (bf16[3,1,32,8,704]{4,3,2,1,0:T(8,128)(2,1)S(1)}, bf16[3,1,32,8,704]{4,3,2,1,0:T(8,128)(2,1)}, u32[]{:S(2)}) copy-start(bf16[3,1,32,8,704]{4,3,2,1,0:T(8,128)(2,1)} %param.8) | copy-start | bytes 3244036
  49.8 23.2 %all-to-all-start.1 = ((bf16[16,176,176]{2,1,0:T(8,128)(2,1)}), bf16[16,176,176]{2,1,0:T(8,128)(2,1)S(1)}, u32[]{:S(2)}, u32[]{:S(2)}) async-start(bf16[16,176,176]{2,1,0:T(8,128)(2,1)} %copy-done.8), calls=%async_computation.1 | async-start | bytes 2883584 | tf_op jit(solution)/shard_map/all_to_all | solution.py:365
  54.1 14.4 %collective-permute-start.4 = (f32[4,2,1,1408]{3,1,0,2:T(2,128)S(1)}, f32[4,2,1,1408]{3,1,0,2:T(2,128)S(1)}, u32[]{:S(2)}, u32[]{:S(2)}) collective-permute-start(f32[4,2,1,1408]{3,1,0,2:T(2,128)S(1)} %bitcast.53), channel_id=1, source_target_pairs={{0,256},{256,0},{1,257},{257,1},{2,258},{258,2},{3,259},{259,3},{4... | collective-permute-start | bytes 135176 | tf_op jit(solution)/shard_map/ppermute | solution.py:63
  66.1 2.5 %copy-start.22 = (f32[4,2,1408]{2,1,0:T(2,128)S(1)}, f32[4,2,1408]{2,1,0:T(2,128)}, u32[]{:S(2)}) copy-start(f32[4,2,1408]{2,1,0:T(2,128)} %copy-done.21) | copy-start | bytes 135172
  67.2 1.0 copy-start.1
  73.0 8.8 %collective-permute-start.5 = (bf16[16,176,176]{2,1,0:T(8,128)(2,1)S(1)}, bf16[16,176,176]{2,1,0:T(8,128)(2,1)S(1)}, u32[]{:S(2)}, u32[]{:S(2)}) collective-permute-start(bf16[16,176,176]{2,1,0:T(8,128)(2,1)S(1)} %all-to-all-done.1), channel_id=1, source_target_pairs={{0,32},{32,0},{1,33},{33,1},{2,34},{34,2},{3,35},{35,3},{4,36},{36... | collective-permute-start | bytes 2973704 | tf_op jit(solution)/shard_map/ppermute | solution.py:63
  81.8 3.8 %copy-start.6 = (bf16[16,176,176]{2,1,0:T(8,128)(2,1)}, bf16[16,176,176]{2,1,0:T(8,128)(2,1)S(1)}, u32[]{:S(2)}) copy-start(bf16[16,176,176]{2,1,0:T(8,128)(2,1)S(1)} %collective-permute-done.5) | copy-start | bytes 2973700
  81.8 1.4 copy-start.11
  83.2 34.2 %copy-start.24 = (s32[1,16]{1,0:T(1,128)S(1)}, s32[1,16]{1,0:T(1,128)}, u32[]{:S(2)}) copy-start(s32[1,16]{1,0:T(1,128)} %param.15) | copy-start | bytes 196
  85.6 1.2 copy-start.4
  87.4 22.8 %all-to-all-start.2 = ((f32[16,1,128]{2,1,0:T(1,128)}), f32[16,1,128]{2,1,0:T(1,128)S(1)}, u32[]{:S(2)}, u32[]{:S(2)}) async-start(f32[16,1,128]{2,1,0:T(1,128)} %get-tuple-element.40), calls=%async_computation.2 | async-start | bytes 16384 | tf_op jit(solution)/shard_map/all_to_all | solution.py:400
  110.8 13.8 %all-to-all-start.3 = ((f32[32,2,128]{2,1,0:T(2,128)}), f32[32,2,128]{2,1,0:T(2,128)S(1)}, u32[]{:S(2)}, u32[]{:S(2)}) async-start(f32[32,2,128]{2,1,0:T(2,128)} %broadcast_in_dim.8), calls=%async_computation.3 | async-start | bytes 65536 | tf_op jit(solution)/shard_map/all_to_all | solution.py:59
  124.6 1.8 %copy-start.3 = (bf16[5632,176]{1,0:T(8,128)(2,1)S(1)}, bf16[5632,176]{1,0:T(8,128)(2,1)}, u32[]{:S(2)}) copy-start(bf16[5632,176]{1,0:T(8,128)(2,1)} %all-gather.3.cloned.1.call-done) | copy-start | bytes 5947396
  126.4 1.4 copy-start.5
  133.1 28.2 %all-to-all-start.4 = ((bf16[32,8,704]{2,1,0:T(8,128)(2,1)}), bf16[32,8,704]{2,1,0:T(8,128)(2,1)S(1)}, u32[]{:S(2)}, u32[]{:S(2)}) async-start(bf16[32,8,704]{2,1,0:T(8,128)(2,1)} %bitcast.21), calls=%async_computation.4 | async-start | bytes 786432 | tf_op jit(solution)/shard_map/all_to_all | solution.py:425
  137.2 1.4 copy-start.7
  138.6 1.2 copy-start.16
  139.8 1.1 copy-start.18
  140.9 1.2 copy-start.20
  161.3 1.2 copy-start.2
  (5 other events, 4.1 us)
Sparse Core Ops, SparseCore 0:
  49.9 62.3 all-gather.2

commit v3 on v2

v3 whole, which is shorter than its diff:
```python
import math

import jax
import jax.numpy as jnp
from jax import lax
from jax.experimental import pallas as pl
from jax.experimental.pallas import tpu as pltpu
from jax.sharding import Mesh
from jax.sharding import PartitionSpec as P

HEAD_DIM = 88
HEADS = 8
ATT = 704
WIDTH = 1408
HALF = 704
TOKENS = 256
VIDEOS = 16
FRAMES = 32
PAIR = 2 * HEAD_DIM
WINDOW = 96
BACK = PAIR - WINDOW
VID = ("zh", "y", "c")
SEQ = ("x", "zl")
RING = ("zh", "zl")
SIZES = {"zh": 2, "y": 4, "c": 2, "x": 4, "zl": 8}

logit_scale = 20.0
teacher_softness = 4.0
F32 = jnp.float32
BF16 = jnp.bfloat16
ROOT = 1.0 / math.sqrt(HEAD_DIM)
VMEM = pl.BlockSpec(memory_space=pltpu.VMEM)
SMEM = pl.BlockSpec(memory_space=pltpu.SMEM)
HBM = pl.BlockSpec(memory_space=pltpu.HBM)
MAIN = 128
REST = PAIR - MAIN
FOLD = 96
PACKED = PAIR + FOLD
LABELLED = PACKED + 16


def dot(a, b, contract):
    return lax.dot_general(a, b, (contract, ((), ())), preferred_element_type=F32)


NN = ((1,), (0,))
NT = ((1,), (1,))
TN = ((0,), (0,))


def call(kernel, out_shape, args, flops, moved, ins="", outs="", scratch=(), copies=0):
    places = {"s": SMEM, "v": VMEM, "h": HBM, "d": pl.BlockSpec()}
    sems = [pltpu.SemaphoreType.DMA((copies,))] if copies else []
    single = not isinstance(out_shape, tuple)
    shapes = [
        pltpu.HBM(o.shape, o.dtype) if p == "h" else o
        for o, p in zip((out_shape,) if single else out_shape, outs)
    ]
    specs = [places[p] for p in outs]
    args = [
        pltpu.with_memory_space_constraint(a, pltpu.HBM) if p == "h" else a
        for a, p in zip(args, ins)
    ]
    return pl.pallas_call(
        kernel,
        out_shape=shapes[0] if single else tuple(shapes),
        in_specs=[places[p] for p in ins],
        out_specs=specs[0] if single else tuple(specs),
        scratch_shapes=list(scratch) + sems,
        compiler_params=pltpu.CompilerParams(vmem_limit_bytes=20 * 2**20),
        cost_estimate=pl.CostEstimate(flops=flops, bytes_accessed=moved, transcendentals=0),
    )(*args)


def begin(source, target, sem):
    copy = pltpu.make_async_copy(source, target, sem)
    copy.start()
    return copy


def spread(block, axes):
    count = math.prod(SIZES[axis] for axis in axes)
    return lax.all_to_all(jnp.broadcast_to(block[None], (count,) + block.shape), axes, 0, 0)


def swap(block, axis):
    return lax.ppermute(block, axis, [(0, 1), (1, 0)])


def halves(rows):
    parts = []
    for c in range(2):
        blocks = [(zh * 4 + y) * 2 + c for y in range(4) for zh in range(2)]
        parts.append(
            jnp.concatenate([rows[:, b * HEAD_DIM : (b + 1) * HEAD_DIM] for b in blocks], axis=1)
        )
    return parts


def split_kernel(core_ref, res_ref, gain_ref, res_out, gain_out):
    core = core_ref[0]
    for ref, out in ((res_ref, res_out), (gain_ref, gain_out)):
        parts = halves(ref[...])
        for c in range(2):
            out[core ^ c] = parts[c]


def pack_kernel(place_ref, space_ref, time_ref, text_ref, out):
    zl = place_ref[0]
    rows = []
    for side, ref in enumerate((space_ref, time_ref)):
        block = jnp.zeros((1, HEAD_DIM), F32)
        for i in range(8):
            first = (2 * i + side) * HEAD_DIM
            block = jnp.where(zl == i, text_ref[:, first : first + HEAD_DIM], block)
        high = block.astype(BF16).astype(F32)
        rows += [ref[...].astype(F32), high, block - high]
    rows = jnp.concatenate(rows)
    rows = jnp.concatenate([rows, jnp.zeros((48, 128 - HEAD_DIM), F32)], axis=1).astype(BF16)
    for i in range(16):
        out[i] = rows


def assemble_kernel(place_ref, ring_ref, space_out, time_out, pieces, sems):
    rows, x = 22, place_ref[0]
    labels = [[], []]
    for zh in range(2):
        for pair in range(2):
            block = ring_ref[8 * zh + 2 * x + pair].astype(F32)
            for side in range(2):
                for term in range(2):
                    row = rows + 24 * side + term
                    labels[term].append(block[row : row + 1])
    pieces[0, PACKED:] = jnp.concatenate(labels[0] + labels[1]).astype(BF16)
    piece = lax.broadcasted_iota(jnp.int32, (48, PAIR), 0)
    column = lax.broadcasted_iota(jnp.int32, (48, PAIR), 1)
    copies = []
    for slot, first in enumerate((0, 24)):
        pick = jnp.concatenate(
            [
                ((piece - first + rows * zl == column) & (piece >= first) & (piece < first + rows))
                .astype(F32)
                .astype(BF16)
                for zl in range(8)
            ]
        )
        both = []
        for zh in range(2):
            blocks = ring_ref[8 * zh : 8 * zh + 8].reshape(8 * 48, 128)
            both.append(dot(blocks, pick, TN)[:HEAD_DIM])
        whole = jnp.concatenate(both)
        rest = whole[:, MAIN:]
        low = jnp.concatenate([rest[FOLD:], jnp.zeros((2 * FOLD - PAIR, REST), F32)])
        fold = jnp.concatenate([rest[:FOLD], low, jnp.zeros((FOLD, 128 - 2 * REST), F32)], axis=1)
        pieces[slot, :PAIR] = whole[:, :MAIN].astype(BF16)
        pieces[slot, PAIR:PACKED] = fold.astype(BF16)
        if slot == 0:
            for i in range(16):
                copies.append(begin(pieces.at[0], space_out.at[i], sems.at[i]))
        else:
            copies.append(begin(pieces.at[1, pl.ds(0, PACKED)], time_out, sems.at[16]))
    for copy in copies:
        copy.wait()


def unfold(packed, wide, narrow):
    for y in range(4):
        rows = slice(PAIR * y, PAIR * (y + 1))
        rest = []
        for x in range(4):
            wide[rows, MAIN * x : MAIN * (x + 1)] = packed[4 * x + y, :PAIR]
            fold = packed[4 * x + y, PAIR:PACKED]
            rest.append(jnp.concatenate([fold[:, :REST], fold[: PAIR - FOLD, REST : 2 * REST]]))
        narrow[rows] = jnp.concatenate(rest, axis=1)


def head_rows(head):
    start = (head // 2) * PAIR + (head % 2) * BACK
    return slice(start, start + WINDOW)


def head_valid(head):
    row = lax.broadcasted_iota(jnp.int32, (WINDOW, 1), 0)
    return row < HEAD_DIM if head % 2 == 0 else row >= WINDOW - HEAD_DIM


def own_rows(block, head):
    return block[:HEAD_DIM] if head % 2 == 0 else block[WINDOW - HEAD_DIM :]


def keep(valid, block):
    return jnp.where(valid, block, jnp.zeros_like(block))


def softmax_down(scores):
    peak = jnp.max(scores, axis=0, keepdims=True)
    weights = jnp.exp(scores - peak)
    return (weights * (1.0 / jnp.sum(weights, axis=0, keepdims=True))).astype(BF16)


def slopes_down(weights, dots):
    weights = weights.astype(F32)
    delta = jnp.sum(weights * dots, axis=0, keepdims=True)
    return (weights * (dots - delta) * ROOT).astype(BF16)


def space_forward_kernel(
    qkv_ref, weights_out, wide_out, narrow_out, kept, wide, narrow, down, sems
):
    pair, copies = [], []
    for head in range(HEADS):
        rows, valid = head_rows(head), head_valid(head)
        scores = dot(qkv_ref[1, rows], keep(valid, qkv_ref[0, rows]), TN) * ROOT
        weights = softmax_down(scores)
        kept[head] = weights
        copies.append(begin(kept.at[head], weights_out.at[head], sems.at[head]))
        pair.append(own_rows(dot(qkv_ref[2, rows], weights, NN), head))
        if head % 2:
            x = head // 2
            both = jnp.concatenate(pair)
            wide[:, MAIN * x : MAIN * (x + 1)] = both[:MAIN].T.astype(BF16)
            down[REST * x : REST * (x + 1)] = both[MAIN:]
            pair = []
    copies.append(begin(wide, wide_out, sems.at[HEADS]))
    narrow[...] = down[...].T.astype(BF16)
    copies.append(begin(narrow, narrow_out, sems.at[HEADS + 1]))
    for copy in copies:
        copy.wait()


def space_back_kernel(mixed_ref, own_ref, other_ref, qkv_ref, weights_ref, out, wide, narrow):
    grads = []
    for half, w_ref in enumerate((own_ref, other_ref)):
        unfold(w_ref, wide, narrow)
        grads.append((dot(mixed_ref[half], wide[...], NN), dot(mixed_ref[half], narrow[...], NN)))
    main = (grads[0][0] + grads[1][0]).T.astype(BF16)
    rest = (grads[0][1] + grads[1][1]).T.astype(BF16)
    for x in range(4):
        grad = jnp.concatenate([main[MAIN * x : MAIN * (x + 1)], rest[REST * x : REST * (x + 1)]])
        pairs = [[], [], []]
        for head in (2 * x, 2 * x + 1):
            rows, valid = head_rows(head), head_valid(head)
            grad_rows = grad[:WINDOW] if head % 2 == 0 else grad[BACK:]
            dots = dot(qkv_ref[2, rows], keep(valid, grad_rows), TN)
            weights = weights_ref[head]
            slopes = slopes_down(weights, dots)
            pairs[0].append(own_rows(dot(qkv_ref[1, rows], slopes, NN), head))
            pairs[1].append(own_rows(dot(qkv_ref[0, rows], slopes, NT), head))
            pairs[2].append(own_rows(dot(grad_rows, weights, NT), head))
        for slot in range(3):
            out[slot, x * PAIR : (x + 1) * PAIR] = jnp.concatenate(pairs[slot]).astype(BF16)


def head_lanes(head):
    start = (head * HEAD_DIM) // 128 * 128
    width = min(256, ATT - start)
    lane = lax.broadcasted_iota(jnp.int32, (1, width), 1) + (start - head * HEAD_DIM)
    return slice(start, start + width), (lane >= 0) & (lane < HEAD_DIM)


def time_forward_kernel(qkv_ref, weights_out, kept, sems):
    key = lax.broadcasted_iota(jnp.int32, (TOKENS, TOKENS), 0)
    query = lax.broadcasted_iota(jnp.int32, (TOKENS, TOKENS), 1)
    same = ((key ^ query) & 7) == 0
    copies = []
    for head in range(HEADS):
        lanes, valid = head_lanes(head)
        scores = dot(qkv_ref[1, :, lanes], keep(valid, qkv_ref[0, :, lanes]), NT) * ROOT
        kept[head] = softmax_down(jnp.where(same, scores, -1e30))
        copies.append(begin(kept.at[head], weights_out.at[head], sems.at[head]))
    for copy in copies:
        copy.wait()


def time_back_kernel(grad_ref, qkv_ref, weights_ref, out, kept, total, sems):
    loads = [begin(weights_ref.at[head], kept.at[head], sems.at[head]) for head in range(HEADS)]
    for head in range(HEADS):
        lanes, valid = head_lanes(head)
        grad = grad_ref[:, lanes]
        dots = dot(qkv_ref[2, :, lanes], keep(valid, grad), NT)
        loads[head].wait()
        weights = kept[head]
        slopes = slopes_down(weights, dots)
        for slot, part in enumerate(
            (
                dot(slopes, qkv_ref[1, :, lanes], TN),
                dot(slopes, qkv_ref[0, :, lanes], NN),
                dot(weights, grad, NN),
            )
        ):
            total[slot, :, lanes] = jnp.where(valid, part, total[slot, :, lanes])
    out[...] = total[...].astype(BF16)


def labels_of(y, core, half):
    row = lax.broadcasted_iota(jnp.int32, (8, 1), 0)
    return (row // 4 * 4 + y) * 2 + (core ^ half)


def embed_own_kernel(wide_ref, narrow_ref, res_ref, own_ref, out, att, rest, w_wide, w_narrow, sems):
    loads = [begin(wide_ref, att, sems.at[0]), begin(narrow_ref, rest, sems.at[1])]
    unfold(own_ref, w_wide, w_narrow)
    for load in loads:
        load.wait()
    out[...] = (
        res_ref[0].astype(F32)
        + dot(att[...], w_wide[...], NT)
        + dot(rest[...], w_narrow[...], NT)
    )


def embed_kernel(
    place_ref,
    wide_ref,
    narrow_ref,
    res_ref,
    mixed_ref,
    own_ref,
    other_ref,
    gain_ref,
    normed_out,
    inv_out,
    unit_out,
    norm_out,
    text_out,
    row_out,
    att,
    rest,
    w_wide,
    w_narrow,
    normed,
    inv_kept,
    sems,
):
    core = place_ref[0]
    loads = [begin(wide_ref, att, sems.at[0]), begin(narrow_ref, rest, sems.at[1])]
    unfold(other_ref, w_wide, w_narrow)
    for half, ref in enumerate((own_ref, other_ref)):
        for y in range(4):
            tiles, square = [], 0.0
            for x in range(4):
                terms = ref[4 * x + y, PACKED:].astype(F32)
                tiles.append(terms[:8] + terms[8:])
                square += jnp.sum(tiles[x] * tiles[x], axis=1, keepdims=True)
            upper = lax.broadcasted_iota(jnp.int32, (8, 1), 0) < 4
            first = jnp.sum(jnp.where(upper, square, 0.0), axis=0, keepdims=True)
            second = jnp.sum(jnp.where(upper, 0.0, square), axis=0, keepdims=True)
            size = jnp.sqrt(jnp.where(upper, first, second) + 1e-06)
            for x in range(4):
                text_out[half, 4 * x + y] = tiles[x] / size
    for load in loads:
        load.wait()
    sums = [mixed_ref[...]]
    sums.append(
        res_ref[1].astype(F32) + dot(att[...], w_wide[...], NT) + dot(rest[...], w_narrow[...], NT)
    )
    mean = sum(jnp.sum(s, axis=1, keepdims=True) for s in sums) / WIDTH
    sums = [s - mean for s in sums]
    square = sum(jnp.sum(s * s, axis=1, keepdims=True) for s in sums) / WIDTH
    inv = 1.0 / jnp.sqrt(square + 1e-05)
    inv_kept[...] = jnp.broadcast_to(inv, (TOKENS, 128))
    copies = [begin(inv_kept, inv_out, sems.at[2])]
    embs = []
    for half in range(2):
        part = sums[half] * inv
        normed[half] = part
        copies.append(begin(normed.at[half], normed_out.at[half], sems.at[3 + half]))
        embs.append(jnp.sum(part, axis=0, keepdims=True) * gain_ref[half] / TOKENS)
    norm = jnp.sqrt(sum(jnp.sum(e * e, axis=1, keepdims=True) for e in embs) + 1e-06)
    norm_out[...] = norm
    units = [e / norm for e in embs]
    for half in range(2):
        unit_out[half] = units[half]
    by_core = [jnp.where(core == c, units[0], units[1]) for c in range(2)]
    blank = jnp.zeros((8, 128 - HEAD_DIM), F32)
    blocks = []
    for x in range(4):
        four = []
        for q in range(4):
            start = ((x % 2 * 2 + q // 2) * 2 + x // 2) * HEAD_DIM
            four.append(by_core[q % 2][:, start : start + HEAD_DIM])
        blocks.append(jnp.concatenate([jnp.concatenate(four + four), blank], axis=1))
    lane = lax.broadcasted_iota(jnp.int32, (8, 128), 1)
    row = jnp.zeros((1, 128), F32)
    for half in range(2):
        for y in range(4):
            products = sum(text_out[half, 4 * x + y] * blocks[x] for x in range(4))
            cosines = jnp.sum(products, axis=1, keepdims=True)
            here = lane == labels_of(y, core, half)
            row += jnp.sum(jnp.where(here, cosines, 0.0), axis=0, keepdims=True)
    row = row * (logit_scale / FRAMES)
    for i in range(VIDEOS):
        row_out[i] = row
    for copy in copies:
        copy.wait()


def unfold_kernel(place_ref, w_ref, wide_out, narrow_out, w, wide, narrow, sems):
    core = place_ref[0]
    loads = [begin(w_ref.at[core ^ half], w.at[half], sems.at[half]) for half in range(2)]
    copies = []
    for half in range(2):
        loads[half].wait()
        unfold(w.at[half], wide.at[half], narrow.at[half])
        copies.append(begin(wide.at[half], wide_out.at[half], sems.at[2 + half]))
        copies.append(begin(narrow.at[half], narrow_out.at[half], sems.at[4 + half]))
    for copy in copies:
        copy.wait()


def mixed_grad_kernel(
    place_ref,
    shares_ref,
    teacher_ref,
    normed_ref,
    inv_ref,
    unit_ref,
    norm_ref,
    gain_ref,
    text_ref,
    wide_ref,
    narrow_ref,
    score_out,
    mixed_out,
    time_out,
    normed,
    inv_kept,
    w_wide,
    w_narrow,
    mixed_kept,
    sems,
):
    core, own = place_ref[0], place_ref[1]
    load_normed = begin(normed_ref, normed, sems.at[0])
    load_inv = begin(inv_ref, inv_kept, sems.at[1])
    load_wide = begin(wide_ref, w_wide, sems.at[2])
    load_narrow = begin(narrow_ref, w_narrow, sems.at[3])
    scores = shares_ref[...].reshape(8, 4, 2, 128).sum(axis=1)
    video = lax.broadcasted_iota(jnp.int32, scores.shape, 0) + 8 * lax.broadcasted_iota(
        jnp.int32, scores.shape, 1
    )
    lane = lax.broadcasted_iota(jnp.int32, (1, 128), 1)
    exps = jnp.exp(scores)
    own_exp = jnp.sum(jnp.sum(jnp.where(video == own, exps, 0.0), axis=0), axis=0, keepdims=True)
    own_exp = jnp.where(lane < VIDEOS, own_exp, 0.0)
    column = jnp.sum(jnp.sum(exps, axis=0), axis=0, keepdims=True)
    row_soft = own_exp / jnp.sum(own_exp, axis=1, keepdims=True)
    col_soft = own_exp / column
    teacher = jnp.exp(teacher_ref[...].astype(F32) / teacher_softness)
    teacher = jnp.where(lane < VIDEOS, teacher, 0.0)
    teacher_soft = teacher / jnp.sum(teacher, axis=1, keepdims=True)
    one_hot = (lane == own).astype(F32)
    score_grad = (row_soft - one_hot + (col_soft - one_hot)) / (2.0 * VIDEOS) + (
        row_soft - teacher_soft
    ) / VIDEOS
    score_out[...] = score_grad[:, :VIDEOS]
    pull = score_grad * (VIDEOS * logit_scale)
    wide_lane = lax.broadcasted_iota(jnp.int32, (8, 128), 1)
    blocks = [0.0] * 4
    for half in range(2):
        for y in range(4):
            here = wide_lane == labels_of(y, core, half)
            share = jnp.sum(jnp.where(here, pull, 0.0), axis=1, keepdims=True)
            for x in range(4):
                blocks[x] += share * text_ref[half, 4 * x + y]
    blocks = [b[:4] + b[4:] for b in blocks]
    by_core = []
    for c in range(2):
        row = []
        for y in range(4):
            for zh in range(2):
                q = y % 2 * 2 + c
                row.append(blocks[2 * zh + y // 2][q : q + 1, :HEAD_DIM])
        by_core.append(jnp.concatenate(row, axis=1))
    direction = [
        jnp.where(core == 0, by_core[0], by_core[1]),
        jnp.where(core == 0, by_core[1], by_core[0]),
    ]
    along = sum(
        jnp.sum(unit_ref[half] * direction[half], axis=1, keepdims=True) for half in range(2)
    )
    token = [
        (direction[half] - unit_ref[half] * along) / norm_ref[...] * gain_ref[half]
        for half in range(2)
    ]
    mean = sum(jnp.sum(t, axis=1, keepdims=True) for t in token) / WIDTH
    load_normed.wait()
    load_inv.wait()
    cross = (
        sum(jnp.sum(normed[half] * token[half], axis=1, keepdims=True) for half in range(2)) / WIDTH
    )
    inv = inv_kept[:, :1]
    load_wide.wait()
    load_narrow.wait()
    copies, wide, narrow = [], 0.0, 0.0
    for half in range(2):
        mixed = (inv * (token[half] - mean - normed[half] * cross)).astype(BF16)
        mixed_kept[half] = mixed
        copies.append(begin(mixed_kept.at[half], mixed_out.at[half], sems.at[4 + half]))
        wide += dot(mixed, w_wide[half], NN)
        narrow += dot(mixed, w_narrow[half], NN)
    parts = []
    for x in range(4):
        parts += [wide[:, MAIN * x : MAIN * (x + 1)], narrow[:, REST * x : REST * (x + 1)]]
    time_out[...] = jnp.concatenate(parts, axis=1).astype(BF16)
    for copy in copies:
        copy.wait()


def shaped(shape, dtype):
    return jax.ShapeDtypeStruct(shape, dtype)


def shards(time_qkv, space_qkv, residual, space_proj, time_proj, norm_gain, text_emb, teacher):
    core = lax.axis_index("c")
    own_video = lax.axis_index(VID)
    big = pltpu.VMEM
    place = jnp.stack([core, own_video])
    pack = call(
        pack_kernel,
        shaped((16, 48, 128), BF16),
        (lax.axis_index("zl")[None], space_proj, time_proj, text_emb),
        10**5,
        10**6,
        "sddd",
        "v",
    )
    ring = lax.all_to_all(pack, RING, 0, 0)

    space = space_qkv.reshape(3, TOKENS, ATT).swapaxes(1, 2)
    space_weights, att_wide, att_narrow = call(
        space_forward_kernel,
        (
            shaped((HEADS, TOKENS, TOKENS), BF16),
            shaped((TOKENS, 4 * MAIN), BF16),
            shaped((TOKENS, 4 * REST), BF16),
        ),
        (space,),
        6 * 10**8,
        3 * 10**6,
        "v",
        "hhh",
        [
            big((HEADS, TOKENS, TOKENS), BF16),
            big((TOKENS, 4 * MAIN), BF16),
            big((TOKENS, 4 * REST), BF16),
            big((4 * REST, TOKENS), F32),
        ],
        HEADS + 2,
    )
    res, gain = call(
        split_kernel,
        (shaped((2, TOKENS, HALF), BF16), shaped((2, 1, HALF), F32)),
        (core[None], residual.reshape(TOKENS, WIDTH), norm_gain[None]),
        10**8,
        2 * 10**6,
        "svv",
        "vv",
    )
    ring, res, gain, att_wide, att_narrow = lax.optimization_barrier(
        (ring, res, gain, att_wide, att_narrow)
    )

    space_copies, time_piece = call(
        assemble_kernel,
        (shaped((16, LABELLED, 128), BF16), shaped((PACKED, 128), BF16)),
        (lax.axis_index("x")[None], ring),
        2 * 10**7,
        2 * 10**6,
        "sv",
        "hh",
        [big((2, LABELLED, 128), BF16)],
        17,
    )
    w_time = lax.all_gather(time_piece, ("c", "x", "y")).reshape(2, 16, PACKED, 128)
    w_own = lax.all_to_all(space_copies, ("x", "y"), 0, 0)

    time = time_qkv.reshape(3, TOKENS, ATT)
    time_weights = call(
        time_forward_kernel,
        shaped((HEADS, TOKENS, TOKENS), BF16),
        (time,),
        6 * 10**8,
        3 * 10**6,
        "v",
        "h",
        [big((HEADS, TOKENS, TOKENS), BF16)],
        HEADS,
    )
    w_own, time_weights = lax.optimization_barrier((w_own, time_weights))
    w_other = swap(w_own, "c")
    mixed_own = call(
        embed_own_kernel,
        shaped((TOKENS, HALF), F32),
        (att_wide, att_narrow, res, w_own),
        5 * 10**8,
        3 * 10**6,
        "hhvv",
        "v",
        [
            big((TOKENS, 4 * MAIN), BF16),
            big((TOKENS, 4 * REST), BF16),
            big((HALF, 4 * MAIN), BF16),
            big((HALF, 4 * REST), BF16),
        ],
        2,
    )
    w_other, mixed_own = lax.optimization_barrier((w_other, mixed_own))
    normed, inv, unit, norm, text, row = call(
        embed_kernel,
        (
            shaped((2, TOKENS, HALF), F32),
            shaped((TOKENS, 128), F32),
            shaped((2, 1, HALF), F32),
            shaped((1, 1), F32),
            shaped((2, 16, 8, 128), F32),
            shaped((VIDEOS, 1, 128), F32),
        ),
        (core[None], att_wide, att_narrow, res, mixed_own, w_own, w_other, gain),
        10**9,
        6 * 10**6,
        "shhvvvvv",
        "hhvvvv",
        [
            big((TOKENS, 4 * MAIN), BF16),
            big((TOKENS, 4 * REST), BF16),
            big((HALF, 4 * MAIN), BF16),
            big((HALF, 4 * REST), BF16),
            big((2, TOKENS, HALF), F32),
            big((TOKENS, 128), F32),
        ],
        5,
    )
    ring_rows = lax.all_to_all(row, RING, 0, 0)
    shares = spread(ring_rows.reshape(2, 8, 128).sum(axis=1), ("y", "c", "x"))
    w_wide, w_narrow = call(
        unfold_kernel,
        (shaped((2, HALF, 4 * MAIN), BF16), shaped((2, HALF, 4 * REST), BF16)),
        (core[None], w_time),
        10**7,
        5 * 10**6,
        "sh",
        "hh",
        [
            big((2, 16, PACKED, 128), BF16),
            big((2, HALF, 4 * MAIN), BF16),
            big((2, HALF, 4 * REST), BF16),
        ],
        6,
    )
    shares, w_wide, w_narrow = lax.optimization_barrier((shares, w_wide, w_narrow))
    score_grad, mixed, time_grad = call(
        mixed_grad_kernel,
        (
            shaped((1, VIDEOS), F32),
            shaped((2, TOKENS, HALF), BF16),
            shaped((TOKENS, ATT), BF16),
        ),
        (
            place,
            shares,
            jnp.pad(teacher, ((0, 0), (0, 128 - VIDEOS))),
            normed,
            inv,
            unit,
            norm,
            gain,
            text,
            w_wide,
            w_narrow,
        ),
        10**9,
        6 * 10**6,
        "svvhhvvvvhh",
        "vhv",
        [
            big((2, TOKENS, HALF), F32),
            big((TOKENS, 128), F32),
            big((2, HALF, 4 * MAIN), BF16),
            big((2, HALF, 4 * REST), BF16),
            big((2, TOKENS, HALF), BF16),
        ],
        6,
    )
    moved = lax.all_to_all(time_grad.reshape(FRAMES, 8, ATT), SEQ, 0, 0).reshape(TOKENS, ATT)
    space_grad = call(
        space_back_kernel,
        shaped((3, ATT, TOKENS), BF16),
        (mixed, w_own, w_other, space, space_weights),
        2 * 10**9,
        8 * 10**6,
        "vvvvv",
        "v",
        [big((HALF, 4 * MAIN), BF16), big((HALF, 4 * REST), BF16)],
    )
    moved, space_grad = lax.optimization_barrier((moved, space_grad))
    time_out = call(
        time_back_kernel,
        shaped((3, TOKENS, ATT), BF16),
        (moved, time, time_weights),
        10**9,
        5 * 10**6,
        "vvh",
        "v",
        [big((HEADS, TOKENS, TOKENS), BF16), big((3, TOKENS, ATT), F32)],
        HEADS,
    )
    return (
        space_grad.swapaxes(1, 2).reshape(3, 1, 1, TOKENS, ATT),
        time_out.reshape(3, 1, FRAMES, 8, ATT),
        score_grad,
    )


def solution(mesh):
    fine = Mesh(mesh.devices.reshape(2, 4, 2, 4, 8), ("zh", "y", "c", "x", "zl"))
    in_specs = (
        P(None, VID, None, SEQ, None),
        P(None, VID, SEQ, None, None),
        P(VID, SEQ, None, None),
        P(SEQ, VID),
        P(SEQ, VID),
        P(),
        P(VID, None),
        P(VID, None),
    )
    out_specs = (
        P(None, VID, SEQ, None, None),
        P(None, VID, None, SEQ, None),
        P(VID, None),
    )
    return jax.shard_map(shards, mesh=fine, in_specs=in_specs, out_specs=out_specs, check_vma=False)
```

time: 174 us -> 158 us (0.908)
  starting transfers between devices: 72.9 us -> 51.7 us
  local copies, waits for them, and re-layouts: 23.4 us -> 10.6 us
  Pallas kernels: 21.7 us -> 34 us
  waiting for transfers between devices: 39.9 us -> 46.5 us
    ppermute x3 -> x1, starting transfers between devices: 26.9 us -> 9.26 us  [swap(): return lax.ppermute(block, axis, [(0, 1), (1, 0)])]
    all_to_all x1 -> x2, starting transfers between devices: 11.5 us -> 24.7 us  [the longest x1 15.7 us: shards(): ring = lax.all_to_all(pack, RING, 0, 0)]
    pallas_call x9 -> x11, Pallas kernels: 21.7 us -> 34 us  [call(): pl.pallas_call(kernel, out_shape=shapes[0] if single else tuple(shapes),...]
    all_to_all x2 -> x1, starting transfers between devices: 16.1 us -> 5.08 us  [spread(): lax.all_to_all(jnp.broadcast_to(block[None], (count,) + block.shape), axe...]
    unnamed x51 -> x24, local copies, waits for them, and re-layouts: 20.1 us -> 9.28 us
    ppermute x3 -> x0, starting transfers between devices: 10.1 us -> none  [gather_column_texts(): lax.ppermute(both, 'y', [(i, (i + k) % 4) for i in range(4)])]
    all_to_all x1, waiting for transfers between devices: 2.63 us -> 11 us  [shards(): w_own = lax.all_to_all(space_copies, ('x', 'y'), 0, 0)]
    all_to_all x1 -> x2, waiting for transfers between devices: 11.3 us -> 16.7 us  [the longest x1 11.3 us: shards(): ring_rows = lax.all_to_all(row, RING, 0, 0)]
  transfers between devices with their start and end apart: 12 -> 7, of which waited for: 7 -> 6; matrix products, arithmetic and copies ran while one was open for 2% -> 1% of each run, Pallas kernels for 8% -> 13%
where the time goes in v3:
time: 158 us; the launch traced here: 157 us
  starting transfers between devices  51.7 us (33%)
  waiting for transfers between devices  46.5 us (29%)
  Pallas kernels  34 us (22%)
  between operations  14.3 us (9%)
  local copies, waits for them, and re-layouts  10.6 us (7%)
    pallas_call x11, Pallas kernels, call(): pl.pallas_call(kernel, out_shape=shapes[0] if single else tuple(shapes),...  34 us
    all_to_all x1, starting transfers between devices, shards(): ring = lax.all_to_all(pack, RING, 0, 0)  15.7 us
    all_to_all x1, waiting for transfers between devices, shards(): lax.all_to_all(time_grad.reshape(FRAMES, 8, ATT), SEQ, 0, 0)  13.9 us
    all_to_all x1, waiting for transfers between devices, shards(): ring_rows = lax.all_to_all(row, RING, 0, 0)  11.3 us
    all_to_all x1, waiting for transfers between devices, shards(): w_own = lax.all_to_all(space_copies, ('x', 'y'), 0, 0)  11 us
    unnamed x24, local copies, waits for them, and re-layouts  9.28 us
    ppermute x1, starting transfers between devices, swap(): return lax.ppermute(block, axis, [(0, 1), (1, 0)])  9.26 us
    all_to_all x1, starting transfers between devices, shards(): ring_rows = lax.all_to_all(row, RING, 0, 0)  9 us
  transfers between devices with their start and end apart: 7, of which 6 were waited for; matrix products, arithmetic and copies ran while one was open for 1% of the time, Pallas kernels for 13%

profile of v3, /device:TPU:1, one launch (start us, length us, event | category | flops | bytes accessed | tf_op | source)
XLA Modules:
  0.0 157.2 jit_solution(17064600602263823670)
XLA Ops:
  7.2 0.7 copy-done.4
  7.9 0.7 copy-done.5
  8.6 0.7 copy-done.6
  9.2 1.3 shard_map.103
  10.5 15.7 %all-to-all-start = ((bf16[16,48,128]{2,1,0:T(8,128)(2,1)}), bf16[16,48,128]{2,1,0:T(8,128)(2,1)S(1)}, u32[]{:S(2)}, u32[]{:S(2)}) async-start(bf16[16,48,128]{2,1,0:T(8,128)(2,1)} %shard_map.103), calls=%async_computation | async-start | bytes 393216 | tf_op jit(solution)/shard_map/all_to_all | solution.py:528
  26.3 0.7 broadcast_in_dim.9.gain_ref
  27.0 1.1 copy-done.3
  28.5 1.2 copy-done.7
  29.7 3.7 %shard_map.105 = (bf16[8,256,256]{2,1,0:T(8,128)(2,1)}, bf16[256,512]{1,0:T(8,128)(2,1)}, bf16[256,192]{1,0:T(8,128)(2,1)}) custom-call(bf16[3,704,256]{2,1,0:T(8,128)(2,1)S(1)} %bitcast.27), custom_call_target="tpu_custom_call" | custom-call | flops 600000000 | bytes 3000000 | tf_op jit(solution)/shard_map/pallas_call | solution.py:64
  33.4 5.4 %all-to-all-done.ring_ref = bf16[16,48,128]{2,1,0:T(8,128)(2,1)S(1)} async-done(((bf16[16,48,128]{2,1,0:T(8,128)(2,1)}), bf16[16,48,128]{2,1,0:T(8,128)(2,1)S(1)}, u32[]{:S(2)}, u32[]{:S(2)}) %all-to-all-start) | async-done | bytes 196640 | tf_op jit(solution)/shard_map/all_to_all | solution.py:528
  38.8 1.5 shard_map.106
  40.4 6.9 %all-to-all-start.1 = ((bf16[16,288,128]{2,1,0:T(8,128)(2,1)}), bf16[16,288,128]{2,1,0:T(8,128)(2,1)S(1)}, u32[]{:S(2)}, u32[]{:S(2)}) async-start(bf16[16,288,128]{2,1,0:T(8,128)(2,1)} %get-tuple-element.43), calls=%async_computation.1 | async-start | bytes 2359296 | tf_op jit(solution)/shard_map/all_to_all | solution.py:576
  47.3 1.8 %shard_map.107.weights_ref = bf16[8,256,256]{2,1,0:T(8,128)(2,1)} custom-call(bf16[3,256,704]{2,1,0:T(8,128)(2,1)S(1)} %bitcast.23), custom_call_target="tpu_custom_call" | custom-call | flops 600000000 | bytes 3000000 | tf_op jit(solution)/shard_map/pallas_call | solution.py:64
  49.2 11.0 %all-to-all-done.1.own_ref = bf16[16,288,128]{2,1,0:T(8,128)(2,1)S(1)} async-done(((bf16[16,288,128]{2,1,0:T(8,128)(2,1)}), bf16[16,288,128]{2,1,0:T(8,128)(2,1)S(1)}, u32[]{:S(2)}, u32[]{:S(2)}) %all-to-all-start.1) | async-done | bytes 1179680 | tf_op jit(solution)/shard_map/all_to_all | solution.py:576
  60.2 9.3 %collective-permute-start = (bf16[16,288,128]{2,1,0:T(8,128)(2,1)S(1)}, bf16[16,288,128]{2,1,0:T(8,128)(2,1)S(1)}, u32[]{:S(2)}, u32[]{:S(2)}) collective-permute-start(bf16[16,288,128]{2,1,0:T(8,128)(2,1)S(1)} %all-to-all-done.1.own_ref), channel_id=1, source_target_pairs={{0,32},{32,0},{1,33},{33,1},{2,34},{34,2},{3,35},{35,3},{4,36},{36... | collective-permute-start | bytes 3538952 | tf_op jit(solution)/shard_map/ppermute | solution.py:87
  69.4 1.5 shard_map.108.mixed_ref
  71.0 0.9 collective-permute-done.other_ref
  71.9 4.2 %shard_map.109 = (f32[2,256,704]{2,1,0:T(8,128)}, f32[256,128]{1,0:T(8,128)}, f32[2,1,704]{2,1,0:T(1,128)S(1)}, f32[1,1]{1,0:T(1,128)}, f32[2,16,8,128]{3,2,1,0:T(8,128)S(1)}, /*index=5*/f32[16,1,128]{2,1,0:T(1,128)}) custom-call(s32[1]{0:T(128)} %bitcast.core_ref.place_ref, bf16[256,512]{1,0:T(8,128)(2,1)} %get-tuple-element.39.wide_ref, ...), custom_call_target="tpu_custom_call" | custom-call | flops 1000000000 | bytes 6000000 | tf_op jit(solution)/shard_map/pallas_call | solution.py:64
  76.1 9.0 %all-to-all-start.2 = ((f32[16,1,128]{2,1,0:T(1,128)}), f32[16,1,128]{2,1,0:T(1,128)S(1)}, u32[]{:S(2)}, u32[]{:S(2)}) async-start(f32[16,1,128]{2,1,0:T(1,128)} %get-tuple-element.48), calls=%async_computation.2 | async-start | bytes 16384 | tf_op jit(solution)/shard_map/all_to_all | solution.py:634
  85.2 11.3 %all-to-all-done.2 = f32[16,1,128]{2,1,0:T(1,128)S(1)} async-done(((f32[16,1,128]{2,1,0:T(1,128)}), f32[16,1,128]{2,1,0:T(1,128)S(1)}, u32[]{:S(2)}, u32[]{:S(2)}) %all-to-all-start.2) | async-done | bytes 8224 | tf_op jit(solution)/shard_map/all_to_all | solution.py:634
  97.1 5.1 %all-to-all-start.3 = ((f32[32,2,128]{2,1,0:T(2,128)}), f32[32,2,128]{2,1,0:T(2,128)S(1)}, u32[]{:S(2)}, u32[]{:S(2)}) async-start(f32[32,2,128]{2,1,0:T(2,128)} %broadcast_in_dim.21), calls=%async_computation.3 | async-start | bytes 65536 | tf_op jit(solution)/shard_map/all_to_all | solution.py:83
  102.3 3.2 %shard_map.110 = (bf16[2,704,512]{2,1,0:T(8,128)(2,1)}, bf16[2,704,192]{2,1,0:T(8,128)(2,1)}) custom-call(s32[1]{0:T(128)} %bitcast.core_ref.place_ref, bf16[2,16,272,128]{3,2,1,0:T(8,128)(2,1)} %bitcast.29), custom_call_target="tpu_custom_call" | custom-call | flops 10000000 | bytes 5000000 | tf_op jit(solution)/shard_map/pallas_call | solution.py:64
  105.5 4.0 %all-to-all-done.3.shares_ref = f32[32,2,128]{2,1,0:T(2,128)S(1)} async-done(((f32[32,2,128]{2,1,0:T(2,128)}), f32[32,2,128]{2,1,0:T(2,128)S(1)}, u32[]{:S(2)}, u32[]{:S(2)}) %all-to-all-start.3) | async-done | bytes 32800 | tf_op jit(solution)/shard_map/all_to_all | solution.py:83
  109.5 6.0 %shard_map.111 = (f32[1,16]{1,0:T(1,128)}, bf16[2,256,704]{2,1,0:T(8,128)(2,1)}, bf16[256,704]{1,0:T(8,128)(2,1)}) custom-call(s32[2]{0:T(128)S(1)} %pad_add_fusion.place_ref, f32[32,2,128]{2,1,0:T(2,128)S(1)} %all-to-all-done.3.shares_ref, s32[1,128]{1,0:T(1,128)S(1)} %pad.4.teacher_ref, f32[2,256,704]{2,1,0:T(8,128)} %get-tuple-element.53.normed_ref, ...), custom_call_target="tpu_custom_call" | custom-call | flops 1000000000 | bytes 6000000 | tf_op jit(solution)/shard_map/pallas_call | solution.py:64
  115.5 5.7 %all-to-all-start.4 = ((bf16[32,8,704]{2,1,0:T(8,128)(2,1)}), bf16[32,8,704]{2,1,0:T(8,128)(2,1)S(1)}, u32[]{:S(2)}, u32[]{:S(2)}) async-start(bf16[32,8,704]{2,1,0:T(8,128)(2,1)} %bitcast.10), calls=%async_computation.4 | async-start | bytes 786432 | tf_op jit(solution)/shard_map/all_to_all | solution.py:685
  121.2 1.3 copy-done.2
  122.5 1.2 copy-done.8
  123.7 1.1 copy-done.9
  124.8 1.2 copy-done.10
  126.1 5.2 %shard_map.112 = bf16[3,704,256]{2,1,0:T(8,128)(2,1)} custom-call(bf16[2,256,704]{2,1,0:T(8,128)(2,1)S(1)} %copy-done.9, bf16[16,288,128]{2,1,0:T(8,128)(2,1)S(1)} %all-to-all-done.1.own_ref, bf16[16,288,128]{2,1,0:T(8,128)(2,1)S(1)} %copy-done.2, bf16[3,704,256]{2,1,0:T(8,128)(2,1)S(1)} %bitcast.28, bf16[8,256,256]{2,1,0:T(8,128)(2,1)S(1)} %copy-done.10), custom_call_target="tpu_custom_call" | custom-call | flops 2000000000 | bytes 8000000 | tf_op jit(solution)/shard_map/pallas_call | solution.py:64
  131.3 13.9 %all-to-all-done.4 = bf16[32,8,704]{2,1,0:T(8,128)(2,1)S(1)} async-done(((bf16[32,8,704]{2,1,0:T(8,128)(2,1)}), bf16[32,8,704]{2,1,0:T(8,128)(2,1)S(1)}, u32[]{:S(2)}, u32[]{:S(2)}) %all-to-all-start.4) | async-done | bytes 360480 | tf_op jit(solution)/shard_map/all_to_all | solution.py:685
  145.2 5.1 %shard_map.113 = bf16[3,256,704]{2,1,0:T(8,128)(2,1)} custom-call(bf16[256,704]{1,0:T(8,128)(2,1)S(1)} %bitcast.25, bf16[3,256,704]{2,1,0:T(8,128)(2,1)S(1)} %bitcast.24, bf16[8,256,256]{2,1,0:T(8,128)(2,1)} %shard_map.107.weights_ref), custom_call_target="tpu_custom_call" | custom-call | flops 1000000000 | bytes 5000000 | tf_op jit(solution)/shard_map/pallas_call | solution.py:64
  (23 shorter events, 1.2 us)
Async XLA Ops:
  7.2 0.7 copy-start.4
  7.9 0.7 copy-start.5
  8.6 0.7 copy-start.6
  10.5 28.3 %all-to-all-start = ((bf16[16,48,128]{2,1,0:T(8,128)(2,1)}), bf16[16,48,128]{2,1,0:T(8,128)(2,1)S(1)}, u32[]{:S(2)}, u32[]{:S(2)}) async-start(bf16[16,48,128]{2,1,0:T(8,128)(2,1)} %shard_map.103), calls=%async_computation | async-start | bytes 393216 | tf_op jit(solution)/shard_map/all_to_all | solution.py:528
  26.3 76.0 %all-gather.3.cloned.1.call-start = ((), (), s32[]{:S(2)}) async-start(), calls=%async_computation.5 | async-start | bytes 2297856 | tf_op jit(solution)/shard_map/all_gather | solution.py:575
  27.0 1.1 copy-start.3
  28.5 1.2 copy-start.7
  40.4 6.9 %copy-start = (bf16[3,1,32,8,704]{4,3,2,1,0:T(8,128)(2,1)S(1)}, bf16[3,1,32,8,704]{4,3,2,1,0:T(8,128)(2,1)}, u32[]{:S(2)}) copy-start(bf16[3,1,32,8,704]{4,3,2,1,0:T(8,128)(2,1)} %param.8) | copy-start | bytes 3244036
  40.4 19.8 %all-to-all-start.1 = ((bf16[16,288,128]{2,1,0:T(8,128)(2,1)}), bf16[16,288,128]{2,1,0:T(8,128)(2,1)S(1)}, u32[]{:S(2)}, u32[]{:S(2)}) async-start(bf16[16,288,128]{2,1,0:T(8,128)(2,1)} %get-tuple-element.43), calls=%async_computation.1 | async-start | bytes 2359296 | tf_op jit(solution)/shard_map/all_to_all | solution.py:576
  60.2 11.7 %collective-permute-start = (bf16[16,288,128]{2,1,0:T(8,128)(2,1)S(1)}, bf16[16,288,128]{2,1,0:T(8,128)(2,1)S(1)}, u32[]{:S(2)}, u32[]{:S(2)}) collective-permute-start(bf16[16,288,128]{2,1,0:T(8,128)(2,1)S(1)} %all-to-all-done.1.own_ref), channel_id=1, source_target_pairs={{0,32},{32,0},{1,33},{33,1},{2,34},{34,2},{3,35},{35,3},{4,36},{36... | collective-permute-start | bytes 3538952 | tf_op jit(solution)/shard_map/ppermute | solution.py:87
  70.9 31.3 %copy-start.11 = (s32[1,16]{1,0:T(1,128)S(1)}, s32[1,16]{1,0:T(1,128)}, u32[]{:S(2)}) copy-start(s32[1,16]{1,0:T(1,128)} %param.15) | copy-start | bytes 196
  71.9 4.3 %copy-start.1 = (bf16[16,288,128]{2,1,0:T(8,128)(2,1)}, bf16[16,288,128]{2,1,0:T(8,128)(2,1)S(1)}, u32[]{:S(2)}) copy-start(bf16[16,288,128]{2,1,0:T(8,128)(2,1)S(1)} %collective-permute-done.other_ref) | copy-start | bytes 3538948
  76.1 20.3 %all-to-all-start.2 = ((f32[16,1,128]{2,1,0:T(1,128)}), f32[16,1,128]{2,1,0:T(1,128)S(1)}, u32[]{:S(2)}, u32[]{:S(2)}) async-start(f32[16,1,128]{2,1,0:T(1,128)} %get-tuple-element.48), calls=%async_computation.2 | async-start | bytes 16384 | tf_op jit(solution)/shard_map/all_to_all | solution.py:634
  97.1 12.4 %all-to-all-start.3 = ((f32[32,2,128]{2,1,0:T(2,128)}), f32[32,2,128]{2,1,0:T(2,128)S(1)}, u32[]{:S(2)}, u32[]{:S(2)}) async-start(f32[32,2,128]{2,1,0:T(2,128)} %broadcast_in_dim.21), calls=%async_computation.3 | async-start | bytes 65536 | tf_op jit(solution)/shard_map/all_to_all | solution.py:83
  115.5 29.7 %all-to-all-start.4 = ((bf16[32,8,704]{2,1,0:T(8,128)(2,1)}), bf16[32,8,704]{2,1,0:T(8,128)(2,1)S(1)}, u32[]{:S(2)}, u32[]{:S(2)}) async-start(bf16[32,8,704]{2,1,0:T(8,128)(2,1)} %bitcast.10), calls=%async_computation.4 | async-start | bytes 786432 | tf_op jit(solution)/shard_map/all_to_all | solution.py:685
  121.2 1.3 copy-start.2
  122.5 1.2 copy-start.8
  123.7 1.1 copy-start.9
  124.8 1.2 copy-start.10
Sparse Core Ops, SparseCore 0:
  40.5 59.2 all-gather.2

commit v4 on v3

--- a/solution.py
+++ b/solution.py
@@ -49,16 +49,17 @@
 
 
 def call(kernel, out_shape, args, flops, moved, ins="", outs="", scratch=(), copies=0):
-    places = {"s": SMEM, "v": VMEM, "h": HBM, "d": pl.BlockSpec()}
+    places = {"s": SMEM, "v": VMEM, "m": VMEM, "h": HBM}
+    pinned = {"m": pltpu.VMEM, "h": pltpu.HBM}
     sems = [pltpu.SemaphoreType.DMA((copies,))] if copies else []
     single = not isinstance(out_shape, tuple)
     shapes = [
-        pltpu.HBM(o.shape, o.dtype) if p == "h" else o
+        pinned[p](o.shape, o.dtype) if p in pinned else o
         for o, p in zip((out_shape,) if single else out_shape, outs)
     ]
     specs = [places[p] for p in outs]
     args = [
-        pltpu.with_memory_space_constraint(a, pltpu.HBM) if p == "h" else a
+        pltpu.with_memory_space_constraint(a, pinned[p]) if p in pinned else a
         for a, p in zip(args, ins)
     ]
     return pl.pallas_call(
@@ -105,8 +106,15 @@
             out[core ^ c] = parts[c]
 
 
-def pack_kernel(place_ref, space_ref, time_ref, text_ref, out):
+def pack_kernel(place_ref, space_hbm, time_hbm, text_hbm, out, space_ref, time_ref, text_ref, sems):
     zl = place_ref[0]
+    loads = [
+        begin(space_hbm, space_ref, sems.at[0]),
+        begin(time_hbm, time_ref, sems.at[1]),
+        begin(text_hbm, text_ref, sems.at[2]),
+    ]
+    for load in loads:
+        load.wait()
     rows = []
     for side, ref in enumerate((space_ref, time_ref)):
         block = jnp.zeros((1, HEAD_DIM), F32)
@@ -204,35 +212,33 @@
     return (weights * (dots - delta) * ROOT).astype(BF16)
 
 
-def space_forward_kernel(
-    qkv_ref, weights_out, wide_out, narrow_out, kept, wide, narrow, down, sems
-):
-    pair, copies = [], []
+def space_forward_kernel(qkv_ref, weights_out, wide_out, narrow_out, down):
+    pair = []
     for head in range(HEADS):
         rows, valid = head_rows(head), head_valid(head)
         scores = dot(qkv_ref[1, rows], keep(valid, qkv_ref[0, rows]), TN) * ROOT
         weights = softmax_down(scores)
-        kept[head] = weights
-        copies.append(begin(kept.at[head], weights_out.at[head], sems.at[head]))
+        weights_out[head] = weights
         pair.append(own_rows(dot(qkv_ref[2, rows], weights, NN), head))
         if head % 2:
             x = head // 2
             both = jnp.concatenate(pair)
-            wide[:, MAIN * x : MAIN * (x + 1)] = both[:MAIN].T.astype(BF16)
+            wide_out[:, MAIN * x : MAIN * (x + 1)] = both[:MAIN].T.astype(BF16)
             down[REST * x : REST * (x + 1)] = both[MAIN:]
             pair = []
-    copies.append(begin(wide, wide_out, sems.at[HEADS]))
-    narrow[...] = down[...].T.astype(BF16)
-    copies.append(begin(narrow, narrow_out, sems.at[HEADS + 1]))
-    for copy in copies:
-        copy.wait()
-
-
-def space_back_kernel(mixed_ref, own_ref, other_ref, qkv_ref, weights_ref, out, wide, narrow):
+    narrow_out[...] = down[...].T.astype(BF16)
+
+
+def space_back_kernel(
+    normed_ref, inv_ref, pulls_ref, token_ref, own_ref, other_ref, qkv_ref, weights_ref, out, wide, narrow
+):
     grads = []
     for half, w_ref in enumerate((own_ref, other_ref)):
         unfold(w_ref, wide, narrow)
-        grads.append((dot(mixed_ref[half], wide[...], NN), dot(mixed_ref[half], narrow[...], NN)))
+        token = jnp.sum(pulls_ref[TOKENS:, :1] * token_ref[half], axis=0, keepdims=True)
+        mixed = inv_ref[:, :1] * (token - normed_ref[half].astype(F32) * pulls_ref[:TOKENS, :1])
+        mixed = mixed.astype(BF16)
+        grads.append((dot(mixed, wide[...], NN), dot(mixed, narrow[...], NN)))
     main = (grads[0][0] + grads[1][0]).T.astype(BF16)
     rest = (grads[0][1] + grads[1][1]).T.astype(BF16)
     for x in range(4):
@@ -258,28 +264,22 @@
     return slice(start, start + width), (lane >= 0) & (lane < HEAD_DIM)
 
 
-def time_forward_kernel(qkv_ref, weights_out, kept, sems):
+def time_forward_kernel(qkv_ref, weights_out):
     key = lax.broadcasted_iota(jnp.int32, (TOKENS, TOKENS), 0)
     query = lax.broadcasted_iota(jnp.int32, (TOKENS, TOKENS), 1)
     same = ((key ^ query) & 7) == 0
-    copies = []
     for head in range(HEADS):
         lanes, valid = head_lanes(head)
         scores = dot(qkv_ref[1, :, lanes], keep(valid, qkv_ref[0, :, lanes]), NT) * ROOT
-        kept[head] = softmax_down(jnp.where(same, scores, -1e30))
-        copies.append(begin(kept.at[head], weights_out.at[head], sems.at[head]))
-    for copy in copies:
-        copy.wait()
-
-
-def time_back_kernel(grad_ref, qkv_ref, weights_ref, out, kept, total, sems):
-    loads = [begin(weights_ref.at[head], kept.at[head], sems.at[head]) for head in range(HEADS)]
+        weights_out[head] = softmax_down(jnp.where(same, scores, -1e30))
+
+
+def time_back_kernel(grad_ref, qkv_ref, weights_ref, out, total):
     for head in range(HEADS):
         lanes, valid = head_lanes(head)
         grad = grad_ref[:, lanes]
         dots = dot(qkv_ref[2, :, lanes], keep(valid, grad), NT)
-        loads[head].wait()
-        weights = kept[head]
+        weights = weights_ref[head]
         slopes = slopes_down(weights, dots)
         for slot, part in enumerate(
             (
@@ -297,15 +297,12 @@
     return (row // 4 * 4 + y) * 2 + (core ^ half)
 
 
-def embed_own_kernel(wide_ref, narrow_ref, res_ref, own_ref, out, att, rest, w_wide, w_narrow, sems):
-    loads = [begin(wide_ref, att, sems.at[0]), begin(narrow_ref, rest, sems.at[1])]
+def embed_own_kernel(wide_ref, narrow_ref, res_ref, own_ref, out, w_wide, w_narrow):
     unfold(own_ref, w_wide, w_narrow)
-    for load in loads:
-        load.wait()
     out[...] = (
         res_ref[0].astype(F32)
-        + dot(att[...], w_wide[...], NT)
-        + dot(rest[...], w_narrow[...], NT)
+        + dot(wide_ref[...], w_wide[...], NT)
+        + dot(narrow_ref[...], w_narrow[...], NT)
     )
 
 
@@ -324,16 +321,14 @@
     norm_out,
     text_out,
     row_out,
-    att,
-    rest,
     w_wide,
     w_narrow,
     normed,
     inv_kept,
+    texts,
     sems,
 ):
     core = place_ref[0]
-    loads = [begin(wide_ref, att, sems.at[0]), begin(narrow_ref, rest, sems.at[1])]
     unfold(other_ref, w_wide, w_narrow)
     for half, ref in enumerate((own_ref, other_ref)):
         for y in range(4):
@@ -347,24 +342,25 @@
             second = jnp.sum(jnp.where(upper, 0.0, square), axis=0, keepdims=True)
             size = jnp.sqrt(jnp.where(upper, first, second) + 1e-06)
             for x in range(4):
-                text_out[half, 4 * x + y] = tiles[x] / size
-    for load in loads:
-        load.wait()
+                texts[half, 4 * x + y] = tiles[x] / size
+    copies = [begin(texts, text_out, sems.at[3])]
     sums = [mixed_ref[...]]
     sums.append(
-        res_ref[1].astype(F32) + dot(att[...], w_wide[...], NT) + dot(rest[...], w_narrow[...], NT)
+        res_ref[1].astype(F32)
+        + dot(wide_ref[...], w_wide[...], NT)
+        + dot(narrow_ref[...], w_narrow[...], NT)
     )
     mean = sum(jnp.sum(s, axis=1, keepdims=True) for s in sums) / WIDTH
     sums = [s - mean for s in sums]
     square = sum(jnp.sum(s * s, axis=1, keepdims=True) for s in sums) / WIDTH
     inv = 1.0 / jnp.sqrt(square + 1e-05)
     inv_kept[...] = jnp.broadcast_to(inv, (TOKENS, 128))
-    copies = [begin(inv_kept, inv_out, sems.at[2])]
+    copies.append(begin(inv_kept, inv_out, sems.at[0]))
     embs = []
     for half in range(2):
         part = sums[half] * inv
-        normed[half] = part
-        copies.append(begin(normed.at[half], normed_out.at[half], sems.at[3 + half]))
+        normed[half] = part.astype(BF16)
+        copies.append(begin(normed.at[half], normed_out.at[half], sems.at[1 + half]))
         embs.append(jnp.sum(part, axis=0, keepdims=True) * gain_ref[half] / TOKENS)
     norm = jnp.sqrt(sum(jnp.sum(e * e, axis=1, keepdims=True) for e in embs) + 1e-06)
     norm_out[...] = norm
@@ -384,7 +380,7 @@
     row = jnp.zeros((1, 128), F32)
     for half in range(2):
         for y in range(4):
-            products = sum(text_out[half, 4 * x + y] * blocks[x] for x in range(4))
+            products = sum(texts[half, 4 * x + y] * blocks[x] for x in range(4))
             cosines = jnp.sum(products, axis=1, keepdims=True)
             here = lane == labels_of(y, core, half)
             row += jnp.sum(jnp.where(here, cosines, 0.0), axis=0, keepdims=True)
@@ -395,46 +391,124 @@
         copy.wait()
 
 
-def unfold_kernel(place_ref, w_ref, wide_out, narrow_out, w, wide, narrow, sems):
+def video_of(core):
+    row = lax.broadcasted_iota(jnp.int32, (VIDEOS, 1), 0)
+    return ((row & 1) * 4 + ((row >> 1) & 3)) * 2 + (core ^ (row >> 3))
+
+
+def basis_kernel(place_ref, normed_ref, unit_ref, norm_ref, gain_ref, text_hbm, token_out, cross_out, normed, cross, text_ref, sems):
+    core = place_ref[0]
+    load_text = begin(text_hbm, text_ref, sems.at[2])
+    load = begin(normed_ref, normed, sems.at[0])
+    load_text.wait()
+    by_core = []
+    for c in range(2):
+        parts = []
+        for y in range(4):
+            for zh in range(2):
+                x, q = 2 * zh + y // 2, y % 2 * 2 + c
+                rows = []
+                for half in range(2):
+                    for at in range(4):
+                        tile = text_ref[half, 4 * x + at]
+                        rows += [tile[q : q + 1, :HEAD_DIM], tile[4 + q : 5 + q, :HEAD_DIM]]
+                parts.append(jnp.concatenate(rows))
+        by_core.append(jnp.concatenate(parts, axis=1))
+    texts = [
+        jnp.where(core == 0, by_core[0], by_core[1]),
+        jnp.where(core == 0, by_core[1], by_core[0]),
+    ]
+    along = sum(jnp.sum(texts[h] * unit_ref[h], axis=1, keepdims=True) for h in range(2))
+    scale = VIDEOS * logit_scale / norm_ref[...]
+    token = [(texts[h] - unit_ref[h] * along) * scale * gain_ref[h] for h in range(2)]
+    mean = sum(jnp.sum(t, axis=1, keepdims=True) for t in token) / WIDTH
+    load.wait()
+    columns = sum(dot(normed[h], token[h].astype(BF16), NT) for h in range(2)) * (1.0 / WIDTH)
+    cross[...] = jnp.concatenate([columns, jnp.zeros((TOKENS, 128 - VIDEOS), F32)], axis=1)
+    copy = begin(cross, cross_out, sems.at[1])
+    for half in range(2):
+        token_out[half] = token[half] - mean
+    copy.wait()
+
+
+def project_kernel(
+    place_ref,
+    w_ref,
+    normed_ref,
+    token_ref,
+    wide_out,
+    narrow_out,
+    pull_wide_out,
+    pull_narrow_out,
+    w,
+    normed,
+    w_wide,
+    w_narrow,
+    wide,
+    narrow,
+    pull_wide,
+    pull_narrow,
+    sems,
+):
     core = place_ref[0]
     loads = [begin(w_ref.at[core ^ half], w.at[half], sems.at[half]) for half in range(2)]
-    copies = []
+    load_normed = begin(normed_ref, normed, sems.at[2])
+    sums = [0.0] * 4
     for half in range(2):
+        token = token_ref[half]
+        high = token.astype(BF16)
+        terms = jnp.concatenate([high.astype(F32), token - high.astype(F32)]).astype(BF16)
         loads[half].wait()
-        unfold(w.at[half], wide.at[half], narrow.at[half])
-        copies.append(begin(wide.at[half], wide_out.at[half], sems.at[2 + half]))
-        copies.append(begin(narrow.at[half], narrow_out.at[half], sems.at[4 + half]))
+        unfold(w.at[half], w_wide, w_narrow)
+        if half == 0:
+            load_normed.wait()
+        for i, part in enumerate((w_wide, w_narrow)):
+            sums[i] += dot(normed[half], part[...], NN)
+            sums[2 + i] += dot(terms, part[...], NN)
+    wide[...] = sums[0].astype(BF16)
+    narrow[...] = sums[1].astype(BF16)
+    copies = [begin(wide, wide_out, sems.at[3]), begin(narrow, narrow_out, sems.at[4])]
+    pull_wide[...] = sums[2][:VIDEOS] + sums[2][VIDEOS:]
+    pull_narrow[...] = sums[3][:VIDEOS] + sums[3][VIDEOS:]
+    copies.append(begin(pull_wide, pull_wide_out, sems.at[5]))
+    copies.append(begin(pull_narrow, pull_narrow_out, sems.at[6]))
     for copy in copies:
         copy.wait()
 
 
-def mixed_grad_kernel(
+def score_kernel(
     place_ref,
     shares_ref,
     teacher_ref,
-    normed_ref,
     inv_ref,
-    unit_ref,
-    norm_ref,
-    gain_ref,
-    text_ref,
+    cross_ref,
     wide_ref,
     narrow_ref,
+    pull_wide_ref,
+    pull_narrow_ref,
     score_out,
-    mixed_out,
+    rows_out,
     time_out,
-    normed,
-    inv_kept,
-    w_wide,
-    w_narrow,
-    mixed_kept,
+    inv,
+    cross,
+    wide,
+    narrow,
+    pull_wide,
+    pull_narrow,
+    rows,
+    result,
     sems,
 ):
     core, own = place_ref[0], place_ref[1]
-    load_normed = begin(normed_ref, normed, sems.at[0])
-    load_inv = begin(inv_ref, inv_kept, sems.at[1])
-    load_wide = begin(wide_ref, w_wide, sems.at[2])
-    load_narrow = begin(narrow_ref, w_narrow, sems.at[3])
+    pairs = (
+        (cross_ref, cross),
+        (pull_wide_ref, pull_wide),
+        (pull_narrow_ref, pull_narrow),
+        (inv_ref, inv),
+        (wide_ref, wide),
+        (narrow_ref, narrow),
+    )
+    loads = [begin(source, target, sems.at[i]) for i, (source, target) in enumerate(pairs)]
     scores = shares_ref[...].reshape(8, 4, 2, 128).sum(axis=1)
     video = lax.broadcasted_iota(jnp.int32, scores.shape, 0) + 8 * lax.broadcasted_iota(
         jnp.int32, scores.shape, 1
@@ -454,57 +528,31 @@
         row_soft - teacher_soft
     ) / VIDEOS
     score_out[...] = score_grad[:, :VIDEOS]
-    pull = score_grad * (VIDEOS * logit_scale)
-    wide_lane = lax.broadcasted_iota(jnp.int32, (8, 128), 1)
-    blocks = [0.0] * 4
-    for half in range(2):
-        for y in range(4):
-            here = wide_lane == labels_of(y, core, half)
-            share = jnp.sum(jnp.where(here, pull, 0.0), axis=1, keepdims=True)
-            for x in range(4):
-                blocks[x] += share * text_ref[half, 4 * x + y]
-    blocks = [b[:4] + b[4:] for b in blocks]
-    by_core = []
-    for c in range(2):
-        row = []
-        for y in range(4):
-            for zh in range(2):
-                q = y % 2 * 2 + c
-                row.append(blocks[2 * zh + y // 2][q : q + 1, :HEAD_DIM])
-        by_core.append(jnp.concatenate(row, axis=1))
-    direction = [
-        jnp.where(core == 0, by_core[0], by_core[1]),
-        jnp.where(core == 0, by_core[1], by_core[0]),
-    ]
-    along = sum(
-        jnp.sum(unit_ref[half] * direction[half], axis=1, keepdims=True) for half in range(2)
-    )
-    token = [
-        (direction[half] - unit_ref[half] * along) / norm_ref[...] * gain_ref[half]
-        for half in range(2)
-    ]
-    mean = sum(jnp.sum(t, axis=1, keepdims=True) for t in token) / WIDTH
-    load_normed.wait()
-    load_inv.wait()
-    cross = (
-        sum(jnp.sum(normed[half] * token[half], axis=1, keepdims=True) for half in range(2)) / WIDTH
-    )
-    inv = inv_kept[:, :1]
-    load_wide.wait()
-    load_narrow.wait()
-    copies, wide, narrow = [], 0.0, 0.0
-    for half in range(2):
-        mixed = (inv * (token[half] - mean - normed[half] * cross)).astype(BF16)
-        mixed_kept[half] = mixed
-        copies.append(begin(mixed_kept.at[half], mixed_out.at[half], sems.at[4 + half]))
-        wide += dot(mixed, w_wide[half], NN)
-        narrow += dot(mixed, w_narrow[half], NN)
+    columns = lax.broadcasted_iota(jnp.int32, (VIDEOS, 128), 1)
+    pull = jnp.sum(
+        jnp.where(columns == video_of(core), score_grad, 0.0), axis=1, keepdims=True
+    )
+    rows[TOKENS:] = jnp.broadcast_to(pull, (VIDEOS, 128))
+    column = lax.broadcasted_iota(jnp.int32, (VIDEOS, VIDEOS), 1)
+    row = lax.broadcasted_iota(jnp.int32, (VIDEOS, VIDEOS), 0)
+    pull_row = jnp.sum(jnp.where(row == column, pull, 0.0), axis=0, keepdims=True)
+    for load in loads:
+        load.wait()
+    along = jnp.sum(cross[:, :VIDEOS] * pull_row, axis=1, keepdims=True)
+    rows[:TOKENS] = jnp.broadcast_to(along, (TOKENS, 128))
+    copy = begin(rows, rows_out, sems.at[6])
+    base_wide = jnp.sum(pull * pull_wide[...], axis=0, keepdims=True)
+    base_narrow = jnp.sum(pull * pull_narrow[...], axis=0, keepdims=True)
+    scale = inv[:, :1]
+    out_wide = scale * (base_wide - along * wide[...].astype(F32))
+    out_narrow = scale * (base_narrow - along * narrow[...].astype(F32))
     parts = []
     for x in range(4):
-        parts += [wide[:, MAIN * x : MAIN * (x + 1)], narrow[:, REST * x : REST * (x + 1)]]
-    time_out[...] = jnp.concatenate(parts, axis=1).astype(BF16)
-    for copy in copies:
-        copy.wait()
+        parts += [out_wide[:, MAIN * x : MAIN * (x + 1)], out_narrow[:, REST * x : REST * (x + 1)]]
+    result[...] = jnp.concatenate(parts, axis=1).astype(BF16)
+    send = begin(result, time_out, sems.at[7])
+    copy.wait()
+    send.wait()
 
 
 def shaped(shape, dtype):
@@ -522,10 +570,26 @@
         (lax.axis_index("zl")[None], space_proj, time_proj, text_emb),
         10**5,
         10**6,
-        "sddd",
+        "shhh",
         "v",
+        [big(space_proj.shape, BF16), big(time_proj.shape, BF16), big(text_emb.shape, F32)],
+        3,
     )
     ring = lax.all_to_all(pack, RING, 0, 0)
+
+    space_copies, time_piece = call(
+        assemble_kernel,
+        (shaped((16, LABELLED, 128), BF16), shaped((PACKED, 128), BF16)),
+        (lax.axis_index("x")[None], ring),
+        2 * 10**7,
+        2 * 10**6,
+        "sv",
+        "hh",
+        [big((2, LABELLED, 128), BF16)],
+        17,
+    )
+    w_time = lax.all_gather(time_piece, ("c", "x", "y")).reshape(2, 16, PACKED, 128)
+    w_own = lax.all_to_all(space_copies, ("x", "y"), 0, 0)
 
     space = space_qkv.reshape(3, TOKENS, ATT).swapaxes(1, 2)
     space_weights, att_wide, att_narrow = call(
@@ -539,14 +603,8 @@
         6 * 10**8,
         3 * 10**6,
         "v",
-        "hhh",
-        [
-            big((HEADS, TOKENS, TOKENS), BF16),
-            big((TOKENS, 4 * MAIN), BF16),
-            big((TOKENS, 4 * REST), BF16),
-            big((4 * REST, TOKENS), F32),
-        ],
-        HEADS + 2,
+        "mmm",
+        [big((4 * REST, TOKENS), F32)],
     )
     res, gain = call(
         split_kernel,
@@ -555,26 +613,8 @@
         10**8,
         2 * 10**6,
         "svv",
-        "vv",
-    )
-    ring, res, gain, att_wide, att_narrow = lax.optimization_barrier(
-        (ring, res, gain, att_wide, att_narrow)
-    )
-
-    space_copies, time_piece = call(
-        assemble_kernel,
-        (shaped((16, LABELLED, 128), BF16), shaped((PACKED, 128), BF16)),
-        (lax.axis_index("x")[None], ring),
-        2 * 10**7,
-        2 * 10**6,
-        "sv",
-        "hh",
-        [big((2, LABELLED, 128), BF16)],
-        17,
-    )
-    w_time = lax.all_gather(time_piece, ("c", "x", "y")).reshape(2, 16, PACKED, 128)
-    w_own = lax.all_to_all(space_copies, ("x", "y"), 0, 0)
-
+        "mm",
+    )
     time = time_qkv.reshape(3, TOKENS, ATT)
     time_weights = call(
         time_forward_kernel,
@@ -583,11 +623,11 @@
         6 * 10**8,
         3 * 10**6,
         "v",
-        "h",
-        [big((HEADS, TOKENS, TOKENS), BF16)],
-        HEADS,
-    )
-    w_own, time_weights = lax.optimization_barrier((w_own, time_weights))
+        "m",
+    )
+    w_own, time_weights, res, gain, att_wide, att_narrow = lax.optimization_barrier(
+        (w_own, time_weights, res, gain, att_wide, att_narrow)
+    )
     w_other = swap(w_own, "c")
     mixed_own = call(
         embed_own_kernel,
@@ -595,21 +635,15 @@
         (att_wide, att_narrow, res, w_own),
         5 * 10**8,
         3 * 10**6,
-        "hhvv",
-        "v",
-        [
-            big((TOKENS, 4 * MAIN), BF16),
-            big((TOKENS, 4 * REST), BF16),
-            big((HALF, 4 * MAIN), BF16),
-            big((HALF, 4 * REST), BF16),
-        ],
-        2,
+        "mmmv",
+        "m",
+        [big((HALF, 4 * MAIN), BF16), big((HALF, 4 * REST), BF16)],
     )
     w_other, mixed_own = lax.optimization_barrier((w_other, mixed_own))
     normed, inv, unit, norm, text, row = call(
         embed_kernel,
         (
-            shaped((2, TOKENS, HALF), F32),
+            shaped((2, TOKENS, HALF), BF16),
             shaped((TOKENS, 128), F32),
             shaped((2, 1, HALF), F32),
             shaped((1, 1), F32),
@@ -619,77 +653,101 @@
         (core[None], att_wide, att_narrow, res, mixed_own, w_own, w_other, gain),
         10**9,
         6 * 10**6,
-        "shhvvvvv",
-        "hhvvvv",
+        "smmmmvvm",
+        "hhvvhv",
         [
+            big((HALF, 4 * MAIN), BF16),
+            big((HALF, 4 * REST), BF16),
+            big((2, TOKENS, HALF), BF16),
+            big((TOKENS, 128), F32),
+            big((2, 16, 8, 128), F32),
+        ],
+        4,
+    )
+    ring_rows = lax.all_to_all(row, RING, 0, 0)
+    token, cross = call(
+        basis_kernel,
+        (shaped((2, VIDEOS, HALF), F32), shaped((TOKENS, 128), F32)),
+        (core[None], normed, unit, norm, gain, text),
+        10**8,
+        2 * 10**6,
+        "shvvmh",
+        "vh",
+        [big((2, TOKENS, HALF), BF16), big((TOKENS, 128), F32), big((2, 16, 8, 128), F32)],
+        3,
+    )
+    ring_rows, token, cross = lax.optimization_barrier((ring_rows, token, cross))
+    shares = spread(ring_rows.reshape(2, 8, 128).sum(axis=1), ("y", "c", "x"))
+    wide, narrow, pull_wide, pull_narrow = call(
+        project_kernel,
+        (
+            shaped((TOKENS, 4 * MAIN), BF16),
+            shaped((TOKENS, 4 * REST), BF16),
+            shaped((VIDEOS, 4 * MAIN), F32),
+            shaped((VIDEOS, 4 * REST), F32),
+        ),
+        (core[None], w_time, normed, token),
+        5 * 10**8,
+        5 * 10**6,
+        "shhv",
+        "hhhh",
+        [
+            big((2, 16, PACKED, 128), BF16),
+            big((2, TOKENS, HALF), BF16),
+            big((HALF, 4 * MAIN), BF16),
+            big((HALF, 4 * REST), BF16),
             big((TOKENS, 4 * MAIN), BF16),
             big((TOKENS, 4 * REST), BF16),
-            big((HALF, 4 * MAIN), BF16),
-            big((HALF, 4 * REST), BF16),
-            big((2, TOKENS, HALF), F32),
-            big((TOKENS, 128), F32),
+            big((VIDEOS, 4 * MAIN), F32),
+            big((VIDEOS, 4 * REST), F32),
         ],
-        5,
-    )
-    ring_rows = lax.all_to_all(row, RING, 0, 0)
-    shares = spread(ring_rows.reshape(2, 8, 128).sum(axis=1), ("y", "c", "x"))
-    w_wide, w_narrow = call(
-        unfold_kernel,
-        (shaped((2, HALF, 4 * MAIN), BF16), shaped((2, HALF, 4 * REST), BF16)),
-        (core[None], w_time),
-        10**7,
-        5 * 10**6,
-        "sh",
-        "hh",
-        [
-            big((2, 16, PACKED, 128), BF16),
-            big((2, HALF, 4 * MAIN), BF16),
-            big((2, HALF, 4 * REST), BF16),
-        ],
-        6,
-    )
-    shares, w_wide, w_narrow = lax.optimization_barrier((shares, w_wide, w_narrow))
-    score_grad, mixed, time_grad = call(
-        mixed_grad_kernel,
+        7,
+    )
+    shares, wide, narrow, pull_wide, pull_narrow = lax.optimization_barrier(
+        (shares, wide, narrow, pull_wide, pull_narrow)
+    )
+    score_grad, pulls, time_grad = call(
+        score_kernel,
         (
             shaped((1, VIDEOS), F32),
-            shaped((2, TOKENS, HALF), BF16),
+            shaped((TOKENS + VIDEOS, 128), F32),
             shaped((TOKENS, ATT), BF16),
         ),
         (
             place,
             shares,
             jnp.pad(teacher, ((0, 0), (0, 128 - VIDEOS))),
-            normed,
             inv,
-            unit,
-            norm,
-            gain,
-            text,
-            w_wide,
-            w_narrow,
+            cross,
+            wide,
+            narrow,
+            pull_wide,
+            pull_narrow,
         ),
-        10**9,
-        6 * 10**6,
-        "svvhhvvvvhh",
-        "vhv",
+        10**7,
+        10**6,
+        "svvhhhhhh",
+        "vhh",
         [
-            big((2, TOKENS, HALF), F32),
             big((TOKENS, 128), F32),
-            big((2, HALF, 4 * MAIN), BF16),
-            big((2, HALF, 4 * REST), BF16),
-            big((2, TOKENS, HALF), BF16),
+            big((TOKENS, 128), F32),
+            big((TOKENS, 4 * MAIN), BF16),
+            big((TOKENS, 4 * REST), BF16),
+            big((VIDEOS, 4 * MAIN), F32),
+            big((VIDEOS, 4 * REST), F32),
+            big((TOKENS + VIDEOS, 128), F32),
+            big((TOKENS, ATT), BF16),
         ],
-        6,
+        8,
     )
     moved = lax.all_to_all(time_grad.reshape(FRAMES, 8, ATT), SEQ, 0, 0).reshape(TOKENS, ATT)
     space_grad = call(
         space_back_kernel,
         shaped((3, ATT, TOKENS), BF16),
-        (mixed, w_own, w_other, space, space_weights),
+        (normed, inv, pulls, token, w_own, w_other, space, space_weights),
         2 * 10**9,
         8 * 10**6,
-        "vvvvv",
+        "vvvvvvvm",
         "v",
         [big((HALF, 4 * MAIN), BF16), big((HALF, 4 * REST), BF16)],
     )
@@ -700,10 +758,9 @@
         (moved, time, time_weights),
         10**9,
         5 * 10**6,
-        "vvh",
+        "vvm",
         "v",
-        [big((HEADS, TOKENS, TOKENS), BF16), big((3, TOKENS, ATT), F32)],
-        HEADS,
+        [big((3, TOKENS, ATT), F32)],
     )
     return (
         space_grad.swapaxes(1, 2).reshape(3, 1, 1, TOKENS, ATT),

time: 158 us -> 154 us (0.975)
  waiting for transfers between devices: 46.5 us -> 39 us
  local copies, waits for them, and re-layouts: 10.6 us -> 13.7 us
    all_to_all x1, waiting for transfers between devices: 5.39 us -> 12.5 us  [shards(): ring = lax.all_to_all(pack, RING, 0, 0)]
    all_to_all x1, waiting for transfers between devices: 11 us -> 4.55 us  [shards(): w_own = lax.all_to_all(space_copies, ('x', 'y'), 0, 0)]
    all_to_all x1, waiting for transfers between devices: 11.3 us -> 6.42 us  [shards(): ring_rows = lax.all_to_all(row, RING, 0, 0)]
    unnamed x24 -> x34, local copies, waits for them, and re-layouts: 9.28 us -> 11.9 us
    all_to_all x1, waiting for transfers between devices: 13.9 us -> 12 us  [shards(): lax.all_to_all(time_grad.reshape(FRAMES, 8, ATT), SEQ, 0, 0)]
    pallas_call x11 -> x12, Pallas kernels: 34 us -> 34 us  [call(): pl.pallas_call(kernel, out_shape=shapes[0] if single else tuple(shapes),...]
  transfers between devices with their start and end apart: 7 -> 7, of which waited for: 6 -> 5; matrix products, arithmetic and copies ran while one was open for 1% -> 2% of each run, Pallas kernels for 13% -> 15%
where the time goes in v4:
time: 154 us; the launch traced here: 153 us
  starting transfers between devices  51.6 us (34%)
  waiting for transfers between devices  39 us (25%)
  Pallas kernels  34 us (22%)
  between operations  14.3 us (9%)
  local copies, waits for them, and re-layouts  13.7 us (9%)
    pallas_call x12, Pallas kernels, call(): pl.pallas_call(kernel, out_shape=shapes[0] if single else tuple(shapes),...  34 us
    all_to_all x1, starting transfers between devices, shards(): ring = lax.all_to_all(pack, RING, 0, 0)  15.8 us
    all_to_all x1, waiting for transfers between devices, shards(): ring = lax.all_to_all(pack, RING, 0, 0)  12.5 us
    all_to_all x1, waiting for transfers between devices, shards(): lax.all_to_all(time_grad.reshape(FRAMES, 8, ATT), SEQ, 0, 0)  12 us
    unnamed x34, local copies, waits for them, and re-layouts  11.9 us
    ppermute x1, starting transfers between devices, swap(): return lax.ppermute(block, axis, [(0, 1), (1, 0)])  9.21 us
    all_to_all x1, starting transfers between devices, shards(): ring_rows = lax.all_to_all(row, RING, 0, 0)  9.07 us
    all_to_all x1, starting transfers between devices, shards(): w_own = lax.all_to_all(space_copies, ('x', 'y'), 0, 0)  6.9 us
  transfers between devices with their start and end apart: 7, of which 5 were waited for; matrix products, arithmetic and copies ran while one was open for 2% of the time, Pallas kernels for 15%

profile of v4, /device:TPU:1, one launch (start us, length us, event | category | flops | bytes accessed | tf_op | source)
XLA Modules:
  0.0 153.3 jit_solution(9356131865280710681)
XLA Ops:
  7.2 2.0 %shard_map.103 = bf16[16,48,128]{2,1,0:T(8,128)(2,1)} custom-call(s32[1]{0:T(128)} %bitcast.3.place_ref, bf16[22,88]{1,0:T(8,128)(2,1)} %space_hbm.1, bf16[22,88]{1,0:T(8,128)(2,1)} %time_hbm.1, f32[1,1408]{1,0:T(1,128)} %text_hbm.1), custom_call_target="tpu_custom_call" | custom-call | flops 100000 | bytes 1000000 | tf_op jit(solution)/shard_map/pallas_call | solution.py:65
  9.2 15.8 %all-to-all-start = ((bf16[16,48,128]{2,1,0:T(8,128)(2,1)}), bf16[16,48,128]{2,1,0:T(8,128)(2,1)S(1)}, u32[]{:S(2)}, u32[]{:S(2)}) async-start(bf16[16,48,128]{2,1,0:T(8,128)(2,1)} %shard_map.103), calls=%async_computation | async-start | bytes 393216 | tf_op jit(solution)/shard_map/all_to_all | solution.py:578
  25.0 12.5 %all-to-all-done.ring_ref = bf16[16,48,128]{2,1,0:T(8,128)(2,1)S(1)} async-done(((bf16[16,48,128]{2,1,0:T(8,128)(2,1)}), bf16[16,48,128]{2,1,0:T(8,128)(2,1)S(1)}, u32[]{:S(2)}, u32[]{:S(2)}) %all-to-all-start) | async-done | bytes 196640 | tf_op jit(solution)/shard_map/all_to_all | solution.py:578
  37.5 1.5 shard_map.104
  39.1 6.9 %all-to-all-start.1 = ((bf16[16,288,128]{2,1,0:T(8,128)(2,1)}), bf16[16,288,128]{2,1,0:T(8,128)(2,1)S(1)}, u32[]{:S(2)}, u32[]{:S(2)}) async-start(bf16[16,288,128]{2,1,0:T(8,128)(2,1)} %get-tuple-element.43), calls=%async_computation.1 | async-start | bytes 2359296 | tf_op jit(solution)/shard_map/all_to_all | solution.py:592
  46.4 0.9 copy-done.1
  47.3 1.3 copy-done.11
  48.6 2.9 %shard_map.107 = (bf16[8,256,256]{2,1,0:T(8,128)(2,1)S(1)}, bf16[256,512]{1,0:T(8,128)(2,1)S(1)}, bf16[256,192]{1,0:T(8,128)(2,1)S(1)}) custom-call(bf16[3,704,256]{2,1,0:T(8,128)(2,1)S(1)} %bitcast.26), custom_call_target="tpu_custom_call" | custom-call | flops 600000000 | bytes 3000000 | tf_op jit(solution)/shard_map/pallas_call | solution.py:65
  52.2 1.0 copy-done.14
  53.2 1.1 shard_map.105.weights_ref
  54.3 4.6 %all-to-all-done.1.own_ref = bf16[16,288,128]{2,1,0:T(8,128)(2,1)S(1)} async-done(((bf16[16,288,128]{2,1,0:T(8,128)(2,1)}), bf16[16,288,128]{2,1,0:T(8,128)(2,1)S(1)}, u32[]{:S(2)}, u32[]{:S(2)}) %all-to-all-start.1) | async-done | bytes 1179680 | tf_op jit(solution)/shard_map/all_to_all | solution.py:592
  58.8 9.2 %collective-permute-start = (bf16[16,288,128]{2,1,0:T(8,128)(2,1)S(1)}, bf16[16,288,128]{2,1,0:T(8,128)(2,1)}, u32[]{:S(2)}, u32[]{:S(2)}) collective-permute-start(bf16[16,288,128]{2,1,0:T(8,128)(2,1)S(1)} %all-to-all-done.1.own_ref), channel_id=1, source_target_pairs={{0,32},{32,0},{1,33},{33,1},{2,34},{34,2},{3,35},{35,3},{4,36},{36... | collective-permute-start | bytes 3538952 | tf_op jit(solution)/shard_map/ppermute | solution.py:88
  68.1 1.1 copy-done.2
  69.2 0.9 copy-done.6
  71.3 4.2 %shard_map.109 = (bf16[2,256,704]{2,1,0:T(8,128)(2,1)}, f32[256,128]{1,0:T(8,128)}, f32[2,1,704]{2,1,0:T(1,128)S(1)}, f32[1,1]{1,0:T(1,128)}, f32[2,16,8,128]{3,2,1,0:T(8,128)}, /*index=5*/f32[16,1,128]{2,1,0:T(1,128)}) custom-call(s32[1]{0:T(128)} %bitcast.core_ref.place_ref, bf16[256,512]{1,0:T(8,128)(2,1)S(1)} %copy-done.6, ...), custom_call_target="tpu_custom_call" | custom-call | flops 1000000000 | bytes 6000000 | tf_op jit(solution)/shard_map/pallas_call | solution.py:65
  75.5 9.1 %all-to-all-start.2 = ((f32[16,1,128]{2,1,0:T(1,128)}), f32[16,1,128]{2,1,0:T(1,128)S(1)}, u32[]{:S(2)}, u32[]{:S(2)}) async-start(f32[16,1,128]{2,1,0:T(1,128)} %get-tuple-element.55), calls=%async_computation.2 | async-start | bytes 16384 | tf_op jit(solution)/shard_map/all_to_all | solution.py:667
  85.2 1.2 pad.4.teacher_ref
  86.5 2.9 %shard_map.110 = (f32[2,16,704]{2,1,0:T(8,128)S(1)}, f32[256,128]{1,0:T(8,128)}) custom-call(s32[1]{0:T(128)} %bitcast.core_ref.place_ref, bf16[2,256,704]{2,1,0:T(8,128)(2,1)} %get-tuple-element.56.normed_ref, f32[2,1,704]{2,1,0:T(1,128)S(1)} %get-tuple-element.57.unit_ref, f32[1,1]{1,0:T(1,128)} %get-tuple-element.58.norm_ref, ...), custom_call_target="tpu_custom_call" | custom-call | flops 100000000 | bytes 2000000 | tf_op jit(solution)/shard_map/pallas_call | solution.py:65
  89.4 6.4 %all-to-all-done.2 = f32[16,1,128]{2,1,0:T(1,128)S(1)} async-done(((f32[16,1,128]{2,1,0:T(1,128)}), f32[16,1,128]{2,1,0:T(1,128)S(1)}, u32[]{:S(2)}, u32[]{:S(2)}) %all-to-all-start.2) | async-done | bytes 8224 | tf_op jit(solution)/shard_map/all_to_all | solution.py:667
  96.5 5.0 %all-to-all-start.3 = ((f32[32,2,128]{2,1,0:T(2,128)}), f32[32,2,128]{2,1,0:T(2,128)S(1)}, u32[]{:S(2)}, u32[]{:S(2)}) async-start(f32[32,2,128]{2,1,0:T(2,128)} %broadcast_in_dim.22), calls=%async_computation.3 | async-start | bytes 65536 | tf_op jit(solution)/shard_map/all_to_all | solution.py:84
  101.5 3.7 %shard_map.111 = (bf16[256,512]{1,0:T(8,128)(2,1)}, bf16[256,192]{1,0:T(8,128)(2,1)}, f32[16,512]{1,0:T(8,128)}, f32[16,192]{1,0:T(8,128)}) custom-call(s32[1]{0:T(128)} %bitcast.core_ref.place_ref, bf16[2,16,272,128]{3,2,1,0:T(8,128)(2,1)} %bitcast.28, bf16[2,256,704]{2,1,0:T(8,128)(2,1)} %get-tuple-element.56.normed_ref, ...), custom_call_target="tpu_custom_call" | custom-call | flops 500000000 | bytes 5000000 | tf_op jit(solution)/shard_map/pallas_call | solution.py:65
  105.3 3.5 %all-to-all-done.3.shares_ref = f32[32,2,128]{2,1,0:T(2,128)S(1)} async-done(((f32[32,2,128]{2,1,0:T(2,128)}), f32[32,2,128]{2,1,0:T(2,128)S(1)}, u32[]{:S(2)}, u32[]{:S(2)}) %all-to-all-start.3) | async-done | bytes 32800 | tf_op jit(solution)/shard_map/all_to_all | solution.py:84
  108.8 3.3 %shard_map.112 = (f32[1,16]{1,0:T(1,128)}, f32[272,128]{1,0:T(8,128)}, bf16[256,704]{1,0:T(8,128)(2,1)}) custom-call(s32[2]{0:T(128)S(1)} %copy-done.9, f32[32,2,128]{2,1,0:T(2,128)S(1)} %all-to-all-done.3.shares_ref, s32[1,128]{1,0:T(1,128)S(1)} %copy-done.10, f32[256,128]{1,0:T(8,128)} %get-tuple-element.70.inv_ref, ...), custom_call_target="tpu_custom_call" | custom-call | flops 10000000 | bytes 1000000 | tf_op jit(solution)/shard_map/pallas_call | solution.py:65
  112.1 5.6 %all-to-all-start.4 = ((bf16[32,8,704]{2,1,0:T(8,128)(2,1)}), bf16[32,8,704]{2,1,0:T(8,128)(2,1)}, u32[]{:S(2)}, u32[]{:S(2)}) async-start(bf16[32,8,704]{2,1,0:T(8,128)(2,1)} %bitcast.30), calls=%async_computation.4 | async-start | bytes 786432 | tf_op jit(solution)/shard_map/all_to_all | solution.py:743
  117.8 1.1 copy-done.4
  118.9 0.9 copy-done.8
  119.8 1.2 copy-done.12
  121.0 0.9 copy-done.13
  121.9 1.2 copy-done.15
  123.2 6.6 %shard_map.113 = bf16[3,704,256]{2,1,0:T(8,128)(2,1)} custom-call(bf16[2,256,704]{2,1,0:T(8,128)(2,1)S(1)} %copy-done.4, f32[256,128]{1,0:T(8,128)S(1)} %copy-done.8, f32[272,128]{1,0:T(8,128)S(1)} %copy-done.13, f32[2,16,704]{2,1,0:T(8,128)S(1)} %get-tuple-element.64.token_ref, bf16[16,288,128]{2,1,0:T(8,128)(2,1)S(1)} %all-to-all-done.1.own_ref, ...), custom_call_target="tpu_custom_call" | custom-call | flops 2000000000 | bytes 8000000 | tf_op jit(solution)/shard_map/pallas_call | solution.py:65
  129.7 12.0 %all-to-all-done.4 = bf16[32,8,704]{2,1,0:T(8,128)(2,1)} async-done(((bf16[32,8,704]{2,1,0:T(8,128)(2,1)}), bf16[32,8,704]{2,1,0:T(8,128)(2,1)}, u32[]{:S(2)}, u32[]{:S(2)}) %all-to-all-start.4) | async-done | bytes 360480 | tf_op jit(solution)/shard_map/all_to_all | solution.py:743
  141.7 4.8 %shard_map.114 = bf16[3,256,704]{2,1,0:T(8,128)(2,1)} custom-call(bf16[256,704]{1,0:T(8,128)(2,1)} %bitcast.11.grad_ref, bf16[3,256,704]{2,1,0:T(8,128)(2,1)S(1)} %bitcast.24, bf16[8,256,256]{2,1,0:T(8,128)(2,1)S(1)} %shard_map.105.weights_ref), custom_call_target="tpu_custom_call" | custom-call | flops 1000000000 | bytes 5000000 | tf_op jit(solution)/shard_map/pallas_call | solution.py:65
  (34 shorter events, 3.6 us)
Async XLA Ops:
  9.2 28.3 %all-to-all-start = ((bf16[16,48,128]{2,1,0:T(8,128)(2,1)}), bf16[16,48,128]{2,1,0:T(8,128)(2,1)S(1)}, u32[]{:S(2)}, u32[]{:S(2)}) async-start(bf16[16,48,128]{2,1,0:T(8,128)(2,1)} %shard_map.103), calls=%async_computation | async-start | bytes 393216 | tf_op jit(solution)/shard_map/all_to_all | solution.py:578
  24.9 76.5 %all-gather.3.cloned.1.call-start = ((), (), s32[]{:S(2)}) async-start(), calls=%async_computation.5 | async-start | bytes 2297856 | tf_op jit(solution)/shard_map/all_gather | solution.py:591
  39.1 6.9 %copy-start.16 = (f32[1408]{0:T(1024)S(1)}, f32[1408]{0:T(1024)}, u32[]{:S(2)}) copy-start(f32[1408]{0:T(1024)} %param.13) | copy-start | bytes 16900
  39.1 6.9 %copy-start.7 = (bf16[1,1,256,1408]{3,2,1,0:T(8,128)(2,1)S(1)}, bf16[1,1,256,1408]{3,2,1,0:T(8,128)(2,1)}, u32[]{:S(2)}) copy-start(bf16[1,1,256,1408]{3,2,1,0:T(8,128)(2,1)} %param.10) | copy-start | bytes 2162692
  39.1 19.8 %all-to-all-start.1 = ((bf16[16,288,128]{2,1,0:T(8,128)(2,1)}), bf16[16,288,128]{2,1,0:T(8,128)(2,1)S(1)}, u32[]{:S(2)}, u32[]{:S(2)}) async-start(bf16[16,288,128]{2,1,0:T(8,128)(2,1)} %get-tuple-element.43), calls=%async_computation.1 | async-start | bytes 2359296 | tf_op jit(solution)/shard_map/all_to_all | solution.py:592
  46.4 0.9 copy-start.1
  47.3 5.9 %copy-start = (bf16[3,1,32,8,704]{4,3,2,1,0:T(8,128)(2,1)S(1)}, bf16[3,1,32,8,704]{4,3,2,1,0:T(8,128)(2,1)}, u32[]{:S(2)}) copy-start(bf16[3,1,32,8,704]{4,3,2,1,0:T(8,128)(2,1)} %param.8) | copy-start | bytes 3244036
  47.3 1.3 copy-start.11
  51.5 0.7 copy-start.5
  52.2 1.0 copy-start.14
  58.8 11.9 %collective-permute-start = (bf16[16,288,128]{2,1,0:T(8,128)(2,1)S(1)}, bf16[16,288,128]{2,1,0:T(8,128)(2,1)}, u32[]{:S(2)}, u32[]{:S(2)}) collective-permute-start(bf16[16,288,128]{2,1,0:T(8,128)(2,1)S(1)} %all-to-all-done.1.own_ref), channel_id=1, source_target_pairs={{0,32},{32,0},{1,33},{33,1},{2,34},{34,2},{3,35},{35,3},{4,36},{36... | collective-permute-start | bytes 3538952 | tf_op jit(solution)/shard_map/ppermute | solution.py:88
  68.1 1.1 copy-start.2
  69.2 0.9 copy-start.6
  70.2 1.1 copy-start.3
  75.5 20.3 %all-to-all-start.2 = ((f32[16,1,128]{2,1,0:T(1,128)}), f32[16,1,128]{2,1,0:T(1,128)S(1)}, u32[]{:S(2)}, u32[]{:S(2)}) async-start(f32[16,1,128]{2,1,0:T(1,128)} %get-tuple-element.55), calls=%async_computation.2 | async-start | bytes 16384 | tf_op jit(solution)/shard_map/all_to_all | solution.py:667
  96.5 12.3 %all-to-all-start.3 = ((f32[32,2,128]{2,1,0:T(2,128)}), f32[32,2,128]{2,1,0:T(2,128)S(1)}, u32[]{:S(2)}, u32[]{:S(2)}) async-start(f32[32,2,128]{2,1,0:T(2,128)} %broadcast_in_dim.22), calls=%async_computation.3 | async-start | bytes 65536 | tf_op jit(solution)/shard_map/all_to_all | solution.py:84
  101.5 7.3 %copy-start.9 = (s32[2]{0:T(128)S(1)}, s32[2]{0:T(128)}, u32[]{:S(2)}) copy-start(s32[2]{0:T(128)} %pad_add_fusion.place_ref) | copy-start | bytes 28
  101.5 7.3 %copy-start.10 = (s32[1,128]{1,0:T(1,128)S(1)}, s32[1,128]{1,0:T(1,128)}, u32[]{:S(2)}) copy-start(s32[1,128]{1,0:T(1,128)} %pad.4.teacher_ref) | copy-start | bytes 1540
  112.1 29.6 %all-to-all-start.4 = ((bf16[32,8,704]{2,1,0:T(8,128)(2,1)}), bf16[32,8,704]{2,1,0:T(8,128)(2,1)}, u32[]{:S(2)}, u32[]{:S(2)}) async-start(bf16[32,8,704]{2,1,0:T(8,128)(2,1)} %bitcast.30), calls=%async_computation.4 | async-start | bytes 786432 | tf_op jit(solution)/shard_map/all_to_all | solution.py:743
  117.7 1.1 copy-start.4
  118.9 0.9 copy-start.8
  119.8 1.2 copy-start.12
  121.0 0.9 copy-start.13
  121.9 1.2 copy-start.15
Sparse Core Ops, SparseCore 0:
  39.2 59.1 all-gather.2

commit v5 on v4

--- a/solution.py
+++ b/solution.py
@@ -106,8 +106,15 @@
             out[core ^ c] = parts[c]
 
 
+ROWS = 22
+LATE = 10
+SIDE = 128 - HEAD_DIM
+TEXT = 44
+TEXT_ROW = 27
+
+
 def pack_kernel(place_ref, space_hbm, time_hbm, text_hbm, out, space_ref, time_ref, text_ref, sems):
-    zl = place_ref[0]
+    piece = place_ref[0]
     loads = [
         begin(space_hbm, space_ref, sems.at[0]),
         begin(time_hbm, time_ref, sems.at[1]),
@@ -115,47 +122,71 @@
     ]
     for load in loads:
         load.wait()
-    rows = []
-    for side, ref in enumerate((space_ref, time_ref)):
-        block = jnp.zeros((1, HEAD_DIM), F32)
-        for i in range(8):
-            first = (2 * i + side) * HEAD_DIM
-            block = jnp.where(zl == i, text_ref[:, first : first + HEAD_DIM], block)
-        high = block.astype(BF16).astype(F32)
-        rows += [ref[...].astype(F32), high, block - high]
-    rows = jnp.concatenate(rows)
-    rows = jnp.concatenate([rows, jnp.zeros((48, 128 - HEAD_DIM), F32)], axis=1).astype(BF16)
+    time = time_ref[...].astype(F32)
+    late = time[LATE:]
+    side = [late[:, :SIDE], late[:, SIDE : 2 * SIDE]]
+    ends = [late[i : i + 1, 2 * SIDE :] for i in range(ROWS - LATE)]
+    ends += [jnp.zeros((1, HEAD_DIM - 2 * SIDE), F32)] * 3
+    side += [jnp.concatenate(ends[5 * i : 5 * i + 5], axis=1) for i in range(3)]
+    text = jnp.zeros((1, TEXT), F32)
+    for i in range(32):
+        text = jnp.where(piece == i, text_ref[:, TEXT * i : TEXT * (i + 1)], text)
+    high = text.astype(BF16).astype(F32)
+    for term in (high, text - high):
+        blank = jnp.zeros((1, 2 * SIDE - TEXT), F32)
+        side += [term[:, :SIDE], jnp.concatenate([term[:, SIDE:], blank], axis=1)]
+    side.append(jnp.zeros((1, SIDE), F32))
+    main = jnp.concatenate([space_ref[...].astype(F32), time[:LATE]])
+    rows = jnp.concatenate([main, jnp.concatenate(side)], axis=1).astype(BF16)
     for i in range(16):
         out[i] = rows
 
 
-def assemble_kernel(place_ref, ring_ref, space_out, time_out, pieces, sems):
-    rows, x = 22, place_ref[0]
-    labels = [[], []]
-    for zh in range(2):
-        for pair in range(2):
-            block = ring_ref[8 * zh + 2 * x + pair].astype(F32)
-            for side in range(2):
-                for term in range(2):
-                    row = rows + 24 * side + term
-                    labels[term].append(block[row : row + 1])
-    pieces[0, PACKED:] = jnp.concatenate(labels[0] + labels[1]).astype(BF16)
-    piece = lax.broadcasted_iota(jnp.int32, (48, PAIR), 0)
-    column = lax.broadcasted_iota(jnp.int32, (48, PAIR), 1)
+def assemble_kernel(ring_ref, space_out, time_out, pieces, sems):
+    rows = []
+    for term in range(2):
+        for zh in range(2):
+            blocks = ring_ref[8 * zh : 8 * zh + 8].astype(F32)
+            first = TEXT_ROW + 2 * term
+            parts = jnp.concatenate(
+                [blocks[:, first, HEAD_DIM:], blocks[:, first + 1, HEAD_DIM : HEAD_DIM + TEXT - SIDE]],
+                axis=1,
+            )
+            for q in range(4):
+                both = [parts[2 * q : 2 * q + 1], parts[2 * q + 1 : 2 * q + 2]]
+                rows.append(jnp.concatenate(both, axis=1))
+    rows = jnp.concatenate([jnp.concatenate(rows), jnp.zeros((16, SIDE), F32)], axis=1)
+    pieces[0, PACKED:] = rows.astype(BF16)
+
+    line = lax.broadcasted_iota(jnp.int32, (256, 1), 0) & 31
+    ahead = lax.broadcasted_iota(jnp.int32, (256, PAIR), 1) - ROWS * (
+        lax.broadcasted_iota(jnp.int32, (256, PAIR), 0) >> 5
+    )
+
+    def pick(first, count, target, step=1):
+        there = (line >= first) & (line < first + count)
+        column = jnp.where(there, (line - first) * step + target, -1000)
+        return (ahead == column).astype(F32).astype(BF16)
+
+    picks = [pick(0, ROWS, 0), pick(ROWS, LATE, 0)]
+    picks += [pick(0, ROWS - LATE, LATE), pick(ROWS - LATE, ROWS - LATE, LATE)]
+    picks += [pick(24, 3 if n < 2 else 2, LATE + n, 5) for n in range(5)]
     copies = []
-    for slot, first in enumerate((0, 24)):
-        pick = jnp.concatenate(
-            [
-                ((piece - first + rows * zl == column) & (piece >= first) & (piece < first + rows))
-                .astype(F32)
-                .astype(BF16)
-                for zl in range(8)
-            ]
-        )
+    ring = [ring_ref[8 * zh : 8 * zh + 8].reshape(256, 128) for zh in range(2)]
+    for slot in range(2):
         both = []
         for zh in range(2):
-            blocks = ring_ref[8 * zh : 8 * zh + 8].reshape(8 * 48, 128)
-            both.append(dot(blocks, pick, TN)[:HEAD_DIM])
+            if slot == 0:
+                both.append(dot(ring[zh], picks[0], TN)[:HEAD_DIM])
+                continue
+            main = dot(ring[zh], picks[1], TN)[:HEAD_DIM]
+            side = [dot(ring[zh], p, TN)[HEAD_DIM:] for p in picks[2:4]]
+            width = HEAD_DIM - 2 * SIDE
+            last = sum(
+                dot(ring[zh], p, TN)[HEAD_DIM + width * n : HEAD_DIM + width * (n + 1)]
+                for n, p in enumerate(picks[4:])
+            )
+            both.append(main + jnp.concatenate(side + [last]))
         whole = jnp.concatenate(both)
         rest = whole[:, MAIN:]
         low = jnp.concatenate([rest[FOLD:], jnp.zeros((2 * FOLD - PAIR, REST), F32)])
@@ -274,22 +305,26 @@
         weights_out[head] = softmax_down(jnp.where(same, scores, -1e30))
 
 
-def time_back_kernel(grad_ref, qkv_ref, weights_ref, out, total):
+def time_back_kernel(grad_ref, qkv_ref, weights_ref, out, slopes, result, sems):
+    copies = []
+
+    def put(slot, head, part):
+        lanes, valid = head_lanes(head)
+        result[slot, :, lanes] = jnp.where(valid, part.astype(BF16), result[slot, :, lanes])
+
     for head in range(HEADS):
         lanes, valid = head_lanes(head)
         grad = grad_ref[:, lanes]
         dots = dot(qkv_ref[2, :, lanes], keep(valid, grad), NT)
-        weights = weights_ref[head]
-        slopes = slopes_down(weights, dots)
-        for slot, part in enumerate(
-            (
-                dot(slopes, qkv_ref[1, :, lanes], TN),
-                dot(slopes, qkv_ref[0, :, lanes], NN),
-                dot(weights, grad, NN),
-            )
-        ):
-            total[slot, :, lanes] = jnp.where(valid, part, total[slot, :, lanes])
-    out[...] = total[...].astype(BF16)
+        slopes[head] = slopes_down(weights_ref[head], dots)
+        put(2, head, dot(weights_ref[head], grad, NN))
+    copies.append(begin(result.at[2], out.at[2], sems.at[2]))
+    for slot, contract in ((1, NN), (0, TN)):
+        for head in range(HEADS):
+            put(slot, head, dot(slopes[head], qkv_ref[1 - slot, :, head_lanes(head)[0]], contract))
+        copies.append(begin(result.at[slot], out.at[slot], sems.at[slot]))
+    for copy in copies:
+        copy.wait()
 
 
 def labels_of(y, core, half):
@@ -451,7 +486,7 @@
     sems,
 ):
     core = place_ref[0]
-    loads = [begin(w_ref.at[core ^ half], w.at[half], sems.at[half]) for half in range(2)]
+    loads = [begin(w_ref.at[:, core ^ half], w.at[half], sems.at[half]) for half in range(2)]
     load_normed = begin(normed_ref, normed, sems.at[2])
     sums = [0.0] * 4
     for half in range(2):
@@ -566,8 +601,8 @@
     place = jnp.stack([core, own_video])
     pack = call(
         pack_kernel,
-        shaped((16, 48, 128), BF16),
-        (lax.axis_index("zl")[None], space_proj, time_proj, text_emb),
+        shaped((16, 32, 128), BF16),
+        (lax.axis_index(SEQ)[None], space_proj, time_proj, text_emb),
         10**5,
         10**6,
         "shhh",
@@ -580,15 +615,15 @@
     space_copies, time_piece = call(
         assemble_kernel,
         (shaped((16, LABELLED, 128), BF16), shaped((PACKED, 128), BF16)),
-        (lax.axis_index("x")[None], ring),
+        (ring,),
         2 * 10**7,
         2 * 10**6,
-        "sv",
+        "v",
         "hh",
         [big((2, LABELLED, 128), BF16)],
         17,
     )
-    w_time = lax.all_gather(time_piece, ("c", "x", "y")).reshape(2, 16, PACKED, 128)
+    w_time = lax.all_gather(time_piece, ("x", "y", "c")).reshape(16, 2, PACKED, 128)
     w_own = lax.all_to_all(space_copies, ("x", "y"), 0, 0)
 
     space = space_qkv.reshape(3, TOKENS, ATT).swapaxes(1, 2)
@@ -759,8 +794,9 @@
         10**9,
         5 * 10**6,
         "vvm",
-        "v",
-        [big((3, TOKENS, ATT), F32)],
+        "h",
+        [big((HEADS, TOKENS, TOKENS), BF16), big((3, TOKENS, ATT), BF16)],
+        3,
     )
     return (
         space_grad.swapaxes(1, 2).reshape(3, 1, 1, TOKENS, ATT),

time: 154 us -> 150 us (0.974)
  blocking collectives: 0 us -> 27.5 us
  starting transfers between devices: 51.6 us -> 33.2 us
  waiting for transfers between devices: 39 us -> 26.2 us
    all_to_all x0 -> x1, blocking collectives: none -> 27.5 us  [shards(): ring = lax.all_to_all(pack, RING, 0, 0)]
    all_to_all x1 -> x0, starting transfers between devices: 15.8 us -> none  [shards(): ring = lax.all_to_all(pack, RING, 0, 0)]
    all_to_all x1 -> x0, waiting for transfers between devices: 12.5 us -> none  [shards(): ring = lax.all_to_all(pack, RING, 0, 0)]
    all_to_all x1, starting transfers between devices: 9.07 us -> 5.57 us  [shards(): ring_rows = lax.all_to_all(row, RING, 0, 0)]
  transfers between devices with their start and end apart: 7 -> 6, of which waited for: 5 -> 4; matrix products, arithmetic and copies ran while one was open for 2% -> 2% of each run, Pallas kernels for 15% -> 15%
where the time goes in v5:
time: 150 us; the launch traced here: 149 us
  Pallas kernels  33.8 us (23%)
  starting transfers between devices  33.2 us (22%)
  blocking collectives  27.5 us (18%)
  waiting for transfers between devices  26.2 us (17%)
  between operations  14.3 us (10%)
  local copies, waits for them, and re-layouts  13.6 us (9%)
    pallas_call x12, Pallas kernels, call(): pl.pallas_call(kernel, out_shape=shapes[0] if single else tuple(shapes),...  33.8 us
    all_to_all x1, blocking collectives, shards(): ring = lax.all_to_all(pack, RING, 0, 0)  27.5 us
    all_to_all x1, waiting for transfers between devices, shards(): lax.all_to_all(time_grad.reshape(FRAMES, 8, ATT), SEQ, 0, 0)  12 us
    unnamed x34, local copies, waits for them, and re-layouts  11.9 us
    ppermute x1, starting transfers between devices, swap(): return lax.ppermute(block, axis, [(0, 1), (1, 0)])  9.83 us
    all_to_all x1, starting transfers between devices, shards(): w_own = lax.all_to_all(space_copies, ('x', 'y'), 0, 0)  6.9 us
    all_to_all x1, waiting for transfers between devices, shards(): ring_rows = lax.all_to_all(row, RING, 0, 0)  6.47 us
    all_to_all x1, starting transfers between devices, shards(): lax.all_to_all(time_grad.reshape(FRAMES, 8, ATT), SEQ, 0, 0)  5.7 us
  transfers between devices with their start and end apart: 6, of which 4 were waited for; matrix products, arithmetic and copies ran while one was open for 2% of the time, Pallas kernels for 15%

profile of v5, /device:TPU:1, one launch (start us, length us, event | category | flops | bytes accessed | tf_op | source)
XLA Modules:
  0.0 149.2 jit_solution(16695043603667671877)
XLA Ops:
  7.2 3.0 %shard_map.103 = bf16[16,32,128]{2,1,0:T(8,128)(2,1)S(1)} custom-call(s32[1]{0:T(128)} %bitcast.2.place_ref, bf16[22,88]{1,0:T(8,128)(2,1)} %space_hbm.1, bf16[22,88]{1,0:T(8,128)(2,1)} %time_hbm.1, f32[1,1408]{1,0:T(1,128)} %text_hbm.1), custom_call_target="tpu_custom_call" | custom-call | flops 100000 | bytes 1000000 | tf_op jit(solution)/shard_map/pallas_call | solution.py:65
  10.3 27.5 %all_to_all.25.ring_ref = bf16[16,32,128]{2,1,0:T(8,128)(2,1)S(1)} all-to-all(bf16[16,32,128]{2,1,0:T(8,128)(2,1)S(1)} %shard_map.103), channel_id=1, replica_groups=mesh['zh'=2,'y'=4,'c'=2,'x'=4,'zl'=8] {'zh','zl'}, dimensions={0} | all-to-all | bytes 262144 | tf_op jit(solution)/shard_map/all_to_all | solution.py:613
  37.8 1.7 %shard_map.104 = (bf16[16,288,128]{2,1,0:T(8,128)(2,1)}, bf16[272,128]{1,0:T(8,128)(2,1)}) custom-call(bf16[16,32,128]{2,1,0:T(8,128)(2,1)S(1)} %all_to_all.25.ring_ref), custom_call_target="tpu_custom_call" | custom-call | flops 20000000 | bytes 2000000 | tf_op jit(solution)/shard_map/pallas_call | solution.py:65
  39.6 6.9 %all-to-all-start.1 = ((bf16[16,288,128]{2,1,0:T(8,128)(2,1)}), bf16[16,288,128]{2,1,0:T(8,128)(2,1)S(1)}, u32[]{:S(2)}, u32[]{:S(2)}) async-start(bf16[16,288,128]{2,1,0:T(8,128)(2,1)} %get-tuple-element.43), calls=%async_computation.1 | async-start | bytes 2359296 | tf_op jit(solution)/shard_map/all_to_all | solution.py:627
  46.9 0.9 copy-done.1
  47.8 1.3 copy-done.11
  49.1 2.9 %shard_map.107 = (bf16[8,256,256]{2,1,0:T(8,128)(2,1)S(1)}, bf16[256,512]{1,0:T(8,128)(2,1)S(1)}, bf16[256,192]{1,0:T(8,128)(2,1)S(1)}) custom-call(bf16[3,704,256]{2,1,0:T(8,128)(2,1)S(1)} %bitcast.25), custom_call_target="tpu_custom_call" | custom-call | flops 600000000 | bytes 3000000 | tf_op jit(solution)/shard_map/pallas_call | solution.py:65
  52.0 0.7 copy-done.5
  52.7 1.0 copy-done.14
  53.6 1.1 shard_map.105.weights_ref
  54.8 4.2 %all-to-all-done.1.own_ref = bf16[16,288,128]{2,1,0:T(8,128)(2,1)S(1)} async-done(((bf16[16,288,128]{2,1,0:T(8,128)(2,1)}), bf16[16,288,128]{2,1,0:T(8,128)(2,1)S(1)}, u32[]{:S(2)}, u32[]{:S(2)}) %all-to-all-start.1) | async-done | bytes 1179680 | tf_op jit(solution)/shard_map/all_to_all | solution.py:627
  59.0 9.8 %collective-permute-start = (bf16[16,288,128]{2,1,0:T(8,128)(2,1)S(1)}, bf16[16,288,128]{2,1,0:T(8,128)(2,1)}, u32[]{:S(2)}, u32[]{:S(2)}) collective-permute-start(bf16[16,288,128]{2,1,0:T(8,128)(2,1)S(1)} %all-to-all-done.1.own_ref), channel_id=1, source_target_pairs={{0,32},{32,0},{1,33},{33,1},{2,34},{34,2},{3,35},{35,3},{4,36},{36... | collective-permute-start | bytes 3538952 | tf_op jit(solution)/shard_map/ppermute | solution.py:88
  68.8 1.1 copy-done.2
  70.0 0.9 copy-done.6
  72.1 4.2 %shard_map.109 = (bf16[2,256,704]{2,1,0:T(8,128)(2,1)}, f32[256,128]{1,0:T(8,128)}, f32[2,1,704]{2,1,0:T(1,128)S(1)}, f32[1,1]{1,0:T(1,128)}, f32[2,16,8,128]{3,2,1,0:T(8,128)}, /*index=5*/f32[16,1,128]{2,1,0:T(1,128)}) custom-call(s32[1]{0:T(128)} %bitcast.core_ref.place_ref, bf16[256,512]{1,0:T(8,128)(2,1)S(1)} %copy-done.6, ...), custom_call_target="tpu_custom_call" | custom-call | flops 1000000000 | bytes 6000000 | tf_op jit(solution)/shard_map/pallas_call | solution.py:65
  76.3 5.6 %all-to-all-start.2 = ((f32[16,1,128]{2,1,0:T(1,128)}), f32[16,1,128]{2,1,0:T(1,128)S(1)}, u32[]{:S(2)}, u32[]{:S(2)}) async-start(f32[16,1,128]{2,1,0:T(1,128)} %get-tuple-element.55), calls=%async_computation.2 | async-start | bytes 16384 | tf_op jit(solution)/shard_map/all_to_all | solution.py:702
  82.4 1.1 pad.4.teacher_ref
  83.6 2.9 %shard_map.110 = (f32[2,16,704]{2,1,0:T(8,128)S(1)}, f32[256,128]{1,0:T(8,128)}) custom-call(s32[1]{0:T(128)} %bitcast.core_ref.place_ref, bf16[2,256,704]{2,1,0:T(8,128)(2,1)} %get-tuple-element.56.normed_ref, f32[2,1,704]{2,1,0:T(1,128)S(1)} %get-tuple-element.57.unit_ref, f32[1,1]{1,0:T(1,128)} %get-tuple-element.58.norm_ref, ...), custom_call_target="tpu_custom_call" | custom-call | flops 100000000 | bytes 2000000 | tf_op jit(solution)/shard_map/pallas_call | solution.py:65
  86.5 6.5 %all-to-all-done.2 = f32[16,1,128]{2,1,0:T(1,128)S(1)} async-done(((f32[16,1,128]{2,1,0:T(1,128)}), f32[16,1,128]{2,1,0:T(1,128)S(1)}, u32[]{:S(2)}, u32[]{:S(2)}) %all-to-all-start.2) | async-done | bytes 8224 | tf_op jit(solution)/shard_map/all_to_all | solution.py:702
  93.6 5.1 %all-to-all-start.3 = ((f32[32,2,128]{2,1,0:T(2,128)}), f32[32,2,128]{2,1,0:T(2,128)S(1)}, u32[]{:S(2)}, u32[]{:S(2)}) async-start(f32[32,2,128]{2,1,0:T(2,128)} %broadcast_in_dim.8), calls=%async_computation.3 | async-start | bytes 65536 | tf_op jit(solution)/shard_map/all_to_all | solution.py:84
  98.8 3.8 %shard_map.111 = (bf16[256,512]{1,0:T(8,128)(2,1)}, bf16[256,192]{1,0:T(8,128)(2,1)}, f32[16,512]{1,0:T(8,128)}, f32[16,192]{1,0:T(8,128)}) custom-call(s32[1]{0:T(128)} %bitcast.core_ref.place_ref, bf16[16,2,272,128]{3,2,1,0:T(8,128)(2,1)} %bitcast.27, bf16[2,256,704]{2,1,0:T(8,128)(2,1)} %get-tuple-element.56.normed_ref, ...), custom_call_target="tpu_custom_call" | custom-call | flops 500000000 | bytes 5000000 | tf_op jit(solution)/shard_map/pallas_call | solution.py:65
  102.5 3.5 %all-to-all-done.3.shares_ref = f32[32,2,128]{2,1,0:T(2,128)S(1)} async-done(((f32[32,2,128]{2,1,0:T(2,128)}), f32[32,2,128]{2,1,0:T(2,128)S(1)}, u32[]{:S(2)}, u32[]{:S(2)}) %all-to-all-start.3) | async-done | bytes 32800 | tf_op jit(solution)/shard_map/all_to_all | solution.py:84
  106.0 3.3 %shard_map.112 = (f32[1,16]{1,0:T(1,128)}, f32[272,128]{1,0:T(8,128)}, bf16[256,704]{1,0:T(8,128)(2,1)}) custom-call(s32[2]{0:T(128)S(1)} %copy-done.9, f32[32,2,128]{2,1,0:T(2,128)S(1)} %all-to-all-done.3.shares_ref, s32[1,128]{1,0:T(1,128)S(1)} %copy-done.10, f32[256,128]{1,0:T(8,128)} %get-tuple-element.70.inv_ref, ...), custom_call_target="tpu_custom_call" | custom-call | flops 10000000 | bytes 1000000 | tf_op jit(solution)/shard_map/pallas_call | solution.py:65
  109.4 5.7 %all-to-all-start.4 = ((bf16[32,8,704]{2,1,0:T(8,128)(2,1)}), bf16[32,8,704]{2,1,0:T(8,128)(2,1)}, u32[]{:S(2)}, u32[]{:S(2)}) async-start(bf16[32,8,704]{2,1,0:T(8,128)(2,1)} %bitcast.29), calls=%async_computation.4 | async-start | bytes 786432 | tf_op jit(solution)/shard_map/all_to_all | solution.py:778
  115.1 1.1 copy-done.4
  116.2 0.9 copy-done.8
  117.1 1.2 copy-done.12
  118.3 0.9 copy-done.13
  119.2 1.2 copy-done.15
  120.5 6.6 %shard_map.113 = bf16[3,704,256]{2,1,0:T(8,128)(2,1)} custom-call(bf16[2,256,704]{2,1,0:T(8,128)(2,1)S(1)} %copy-done.4, f32[256,128]{1,0:T(8,128)S(1)} %copy-done.8, f32[272,128]{1,0:T(8,128)S(1)} %copy-done.13, f32[2,16,704]{2,1,0:T(8,128)S(1)} %get-tuple-element.64.token_ref, bf16[16,288,128]{2,1,0:T(8,128)(2,1)S(1)} %all-to-all-done.1.own_ref, ...), custom_call_target="tpu_custom_call" | custom-call | flops 2000000000 | bytes 8000000 | tf_op jit(solution)/shard_map/pallas_call | solution.py:65
  127.0 12.0 %all-to-all-done.4 = bf16[32,8,704]{2,1,0:T(8,128)(2,1)} async-done(((bf16[32,8,704]{2,1,0:T(8,128)(2,1)}), bf16[32,8,704]{2,1,0:T(8,128)(2,1)}, u32[]{:S(2)}, u32[]{:S(2)}) %all-to-all-start.4) | async-done | bytes 360480 | tf_op jit(solution)/shard_map/all_to_all | solution.py:778
  139.0 3.3 %shard_map.114 = bf16[3,256,704]{2,1,0:T(8,128)(2,1)} custom-call(bf16[256,704]{1,0:T(8,128)(2,1)} %bitcast.10.grad_ref, bf16[3,256,704]{2,1,0:T(8,128)(2,1)S(1)} %bitcast.23, bf16[8,256,256]{2,1,0:T(8,128)(2,1)S(1)} %shard_map.105.weights_ref), custom_call_target="tpu_custom_call" | custom-call | flops 1000000000 | bytes 5000000 | tf_op jit(solution)/shard_map/pallas_call | solution.py:65
  (33 shorter events, 2.8 us)
Async XLA Ops:
  7.2 91.6 %all-gather.3.cloned.1.call-start = ((), (), s32[]{:S(2)}) async-start(), calls=%async_computation.5 | async-start | bytes 2297856 | tf_op jit(solution)/shard_map/all_gather | solution.py:626
  39.5 6.9 %copy-start.16 = (f32[1408]{0:T(1024)S(1)}, f32[1408]{0:T(1024)}, u32[]{:S(2)}) copy-start(f32[1408]{0:T(1024)} %param.13) | copy-start | bytes 16900
  39.5 7.0 %copy-start.7 = (bf16[1,1,256,1408]{3,2,1,0:T(8,128)(2,1)S(1)}, bf16[1,1,256,1408]{3,2,1,0:T(8,128)(2,1)}, u32[]{:S(2)}) copy-start(bf16[1,1,256,1408]{3,2,1,0:T(8,128)(2,1)} %param.10) | copy-start | bytes 2162692
  39.6 19.4 %all-to-all-start.1 = ((bf16[16,288,128]{2,1,0:T(8,128)(2,1)}), bf16[16,288,128]{2,1,0:T(8,128)(2,1)S(1)}, u32[]{:S(2)}, u32[]{:S(2)}) async-start(bf16[16,288,128]{2,1,0:T(8,128)(2,1)} %get-tuple-element.43), calls=%async_computation.1 | async-start | bytes 2359296 | tf_op jit(solution)/shard_map/all_to_all | solution.py:627
  46.9 0.9 copy-start.1
  47.8 5.9 %copy-start = (bf16[3,1,32,8,704]{4,3,2,1,0:T(8,128)(2,1)S(1)}, bf16[3,1,32,8,704]{4,3,2,1,0:T(8,128)(2,1)}, u32[]{:S(2)}) copy-start(bf16[3,1,32,8,704]{4,3,2,1,0:T(8,128)(2,1)} %param.8) | copy-start | bytes 3244036
  47.8 1.3 copy-start.11
  52.0 0.7 copy-start.5
  52.7 1.0 copy-start.14
  59.0 12.6 %collective-permute-start = (bf16[16,288,128]{2,1,0:T(8,128)(2,1)S(1)}, bf16[16,288,128]{2,1,0:T(8,128)(2,1)}, u32[]{:S(2)}, u32[]{:S(2)}) collective-permute-start(bf16[16,288,128]{2,1,0:T(8,128)(2,1)S(1)} %all-to-all-done.1.own_ref), channel_id=1, source_target_pairs={{0,32},{32,0},{1,33},{33,1},{2,34},{34,2},{3,35},{35,3},{4,36},{36... | collective-permute-start | bytes 3538952 | tf_op jit(solution)/shard_map/ppermute | solution.py:88
  68.8 1.1 copy-start.2
  70.0 0.9 copy-start.6
  70.9 1.1 copy-start.3
  76.3 16.7 %all-to-all-start.2 = ((f32[16,1,128]{2,1,0:T(1,128)}), f32[16,1,128]{2,1,0:T(1,128)S(1)}, u32[]{:S(2)}, u32[]{:S(2)}) async-start(f32[16,1,128]{2,1,0:T(1,128)} %get-tuple-element.55), calls=%async_computation.2 | async-start | bytes 16384 | tf_op jit(solution)/shard_map/all_to_all | solution.py:702
  93.6 12.5 %all-to-all-start.3 = ((f32[32,2,128]{2,1,0:T(2,128)}), f32[32,2,128]{2,1,0:T(2,128)S(1)}, u32[]{:S(2)}, u32[]{:S(2)}) async-start(f32[32,2,128]{2,1,0:T(2,128)} %broadcast_in_dim.8), calls=%async_computation.3 | async-start | bytes 65536 | tf_op jit(solution)/shard_map/all_to_all | solution.py:84
  98.8 7.3 %copy-start.9 = (s32[2]{0:T(128)S(1)}, s32[2]{0:T(128)}, u32[]{:S(2)}) copy-start(s32[2]{0:T(128)} %pad_add_fusion.place_ref) | copy-start | bytes 28
  98.8 7.3 %copy-start.10 = (s32[1,128]{1,0:T(1,128)S(1)}, s32[1,128]{1,0:T(1,128)}, u32[]{:S(2)}) copy-start(s32[1,128]{1,0:T(1,128)} %pad.4.teacher_ref) | copy-start | bytes 1540
  109.4 29.7 %all-to-all-start.4 = ((bf16[32,8,704]{2,1,0:T(8,128)(2,1)}), bf16[32,8,704]{2,1,0:T(8,128)(2,1)}, u32[]{:S(2)}, u32[]{:S(2)}) async-start(bf16[32,8,704]{2,1,0:T(8,128)(2,1)} %bitcast.29), calls=%async_computation.4 | async-start | bytes 786432 | tf_op jit(solution)/shard_map/all_to_all | solution.py:778
  115.1 1.1 copy-start.4
  116.2 0.9 copy-start.8
  117.1 1.2 copy-start.12
  118.3 0.9 copy-start.13
  119.2 1.2 copy-start.15
Sparse Core Ops, SparseCore 0:
  39.6 55.9 all-gather.2

commit v6 on v5

--- a/solution.py
+++ b/solution.py
@@ -118,7 +118,7 @@
     loads = [
         begin(space_hbm, space_ref, sems.at[0]),
         begin(time_hbm, time_ref, sems.at[1]),
-        begin(text_hbm, text_ref, sems.at[2]),
+        begin(text_hbm, text_ref.at[:, pl.ds(0, WIDTH)], sems.at[2]),
     ]
     for load in loads:
         load.wait()
@@ -128,9 +128,10 @@
     ends = [late[i : i + 1, 2 * SIDE :] for i in range(ROWS - LATE)]
     ends += [jnp.zeros((1, HEAD_DIM - 2 * SIDE), F32)] * 3
     side += [jnp.concatenate(ends[5 * i : 5 * i + 5], axis=1) for i in range(3)]
-    text = jnp.zeros((1, TEXT), F32)
-    for i in range(32):
-        text = jnp.where(piece == i, text_ref[:, TEXT * i : TEXT * (i + 1)], text)
+    start = piece * TEXT
+    near = pl.multiple_of(start // 128 * 128, 128)
+    window = jnp.broadcast_to(text_ref[:, pl.ds(near, 256)], (8, 256))
+    text = pltpu.roll(window, 256 - (start - near), 1)[:1, :TEXT]
     high = text.astype(BF16).astype(F32)
     for term in (high, text - high):
         blank = jnp.zeros((1, 2 * SIDE - TEXT), F32)
@@ -512,7 +513,8 @@
 
 
 def score_kernel(
-    place_ref,
+    core_ref,
+    own_ref,
     shares_ref,
     teacher_ref,
     inv_ref,
@@ -534,7 +536,7 @@
     result,
     sems,
 ):
-    core, own = place_ref[0], place_ref[1]
+    core, own = core_ref[0], own_ref[0]
     pairs = (
         (cross_ref, cross),
         (pull_wide_ref, pull_wide),
@@ -556,7 +558,7 @@
     row_soft = own_exp / jnp.sum(own_exp, axis=1, keepdims=True)
     col_soft = own_exp / column
     teacher = jnp.exp(teacher_ref[...].astype(F32) / teacher_softness)
-    teacher = jnp.where(lane < VIDEOS, teacher, 0.0)
+    teacher = jnp.concatenate([teacher, jnp.zeros((1, 128 - VIDEOS), F32)], axis=1)
     teacher_soft = teacher / jnp.sum(teacher, axis=1, keepdims=True)
     one_hot = (lane == own).astype(F32)
     score_grad = (row_soft - one_hot + (col_soft - one_hot)) / (2.0 * VIDEOS) + (
@@ -598,7 +600,6 @@
     core = lax.axis_index("c")
     own_video = lax.axis_index(VID)
     big = pltpu.VMEM
-    place = jnp.stack([core, own_video])
     pack = call(
         pack_kernel,
         shaped((16, 32, 128), BF16),
@@ -607,7 +608,7 @@
         10**6,
         "shhh",
         "v",
-        [big(space_proj.shape, BF16), big(time_proj.shape, BF16), big(text_emb.shape, F32)],
+        [big(space_proj.shape, BF16), big(time_proj.shape, BF16), big((1, WIDTH + 128), F32)],
         3,
     )
     ring = lax.all_to_all(pack, RING, 0, 0)
@@ -749,9 +750,10 @@
             shaped((TOKENS, ATT), BF16),
         ),
         (
-            place,
+            core[None],
+            own_video[None],
             shares,
-            jnp.pad(teacher, ((0, 0), (0, 128 - VIDEOS))),
+            teacher,
             inv,
             cross,
             wide,
@@ -761,7 +763,7 @@
         ),
         10**7,
         10**6,
-        "svvhhhhhh",
+        "ssvvhhhhhh",
         "vhh",
         [
             big((TOKENS, 128), F32),

time: 150 us -> 148 us (0.987)
  Pallas kernels: 33.8 us -> 29.5 us
  waiting for transfers between devices: 26.2 us -> 28.1 us
    pallas_call x12, Pallas kernels: 33.8 us -> 29.5 us  [call(): pl.pallas_call(kernel, out_shape=shapes[0] if single else tuple(shapes),...]
    all_to_all x1, waiting for transfers between devices: 6.47 us -> 8.38 us  [shards(): ring_rows = lax.all_to_all(row, RING, 0, 0)]
    unnamed x34 -> x40, local copies, waits for them, and re-layouts: 11.9 us -> 13.1 us
  transfers between devices with their start and end apart: 6 -> 6, of which waited for: 4 -> 4; matrix products, arithmetic and copies ran while one was open for 2% -> 0% of each run, Pallas kernels for 15% -> 14%
where the time goes in v6:
time: 148 us; the launch traced here: 147 us
  starting transfers between devices  34.2 us (23%)
  Pallas kernels  29.5 us (20%)
  waiting for transfers between devices  28.1 us (19%)
  blocking collectives  27.5 us (19%)
  between operations  14.3 us (10%)
  local copies, waits for them, and re-layouts  13.8 us (9%)
    pallas_call x12, Pallas kernels, call(): pl.pallas_call(kernel, out_shape=shapes[0] if single else tuple(shapes),...  29.5 us
    all_to_all x1, blocking collectives, shards(): ring = lax.all_to_all(pack, RING, 0, 0)  27.5 us
    unnamed x40, local copies, waits for them, and re-layouts  13.1 us
    all_to_all x1, waiting for transfers between devices, shards(): lax.all_to_all(time_grad.reshape(FRAMES, 8, ATT), SEQ, 0, 0)  12 us
    ppermute x1, starting transfers between devices, swap(): return lax.ppermute(block, axis, [(0, 1), (1, 0)])  9.82 us
    all_to_all x1, waiting for transfers between devices, shards(): ring_rows = lax.all_to_all(row, RING, 0, 0)  8.38 us
    all_to_all x1, starting transfers between devices, shards(): w_own = lax.all_to_all(space_copies, ('x', 'y'), 0, 0)  6.9 us
    all_to_all x1, starting transfers between devices, shards(): lax.all_to_all(time_grad.reshape(FRAMES, 8, ATT), SEQ, 0, 0)  6.32 us
  transfers between devices with their start and end apart: 6, of which 4 were waited for; matrix products, arithmetic and copies ran while one was open for 0% of the time, Pallas kernels for 14%

profile of v6, /device:TPU:1, one launch (start us, length us, event | category | flops | bytes accessed | tf_op | source)
XLA Modules:
  0.0 147.4 jit_solution(3110113048708677919)
XLA Ops:
  7.2 1.0 shard_map.103
  8.2 27.5 %all_to_all.25.ring_ref = bf16[16,32,128]{2,1,0:T(8,128)(2,1)S(1)} all-to-all(bf16[16,32,128]{2,1,0:T(8,128)(2,1)S(1)} %shard_map.103), channel_id=1, replica_groups=mesh['zh'=2,'y'=4,'c'=2,'x'=4,'zl'=8] {'zh','zl'}, dimensions={0} | all-to-all | bytes 262144 | tf_op jit(solution)/shard_map/all_to_all | solution.py:614
  35.8 1.7 %shard_map.104 = (bf16[16,288,128]{2,1,0:T(8,128)(2,1)}, bf16[272,128]{1,0:T(8,128)(2,1)}) custom-call(bf16[16,32,128]{2,1,0:T(8,128)(2,1)S(1)} %all_to_all.25.ring_ref), custom_call_target="tpu_custom_call" | custom-call | flops 20000000 | bytes 2000000 | tf_op jit(solution)/shard_map/pallas_call | solution.py:65
  37.5 6.9 %all-to-all-start.1 = ((bf16[16,288,128]{2,1,0:T(8,128)(2,1)}), bf16[16,288,128]{2,1,0:T(8,128)(2,1)S(1)}, u32[]{:S(2)}, u32[]{:S(2)}) async-start(bf16[16,288,128]{2,1,0:T(8,128)(2,1)} %get-tuple-element.43), calls=%async_computation.1 | async-start | bytes 2359296 | tf_op jit(solution)/shard_map/all_to_all | solution.py:628
  44.8 0.9 copy-done.1
  45.7 1.3 copy-done.14
  47.0 2.9 %shard_map.107 = (bf16[8,256,256]{2,1,0:T(8,128)(2,1)S(1)}, bf16[256,512]{1,0:T(8,128)(2,1)S(1)}, bf16[256,192]{1,0:T(8,128)(2,1)S(1)}) custom-call(bf16[3,704,256]{2,1,0:T(8,128)(2,1)S(1)} %bitcast.25), custom_call_target="tpu_custom_call" | custom-call | flops 600000000 | bytes 3000000 | tf_op jit(solution)/shard_map/pallas_call | solution.py:65
  49.9 0.7 copy-done.7
  50.6 1.0 copy-done.17
  51.6 1.1 shard_map.105.weights_ref
  52.7 4.2 %all-to-all-done.1.own_ref = bf16[16,288,128]{2,1,0:T(8,128)(2,1)S(1)} async-done(((bf16[16,288,128]{2,1,0:T(8,128)(2,1)}), bf16[16,288,128]{2,1,0:T(8,128)(2,1)S(1)}, u32[]{:S(2)}, u32[]{:S(2)}) %all-to-all-start.1) | async-done | bytes 1179680 | tf_op jit(solution)/shard_map/all_to_all | solution.py:628
  56.9 9.8 %collective-permute-start = (bf16[16,288,128]{2,1,0:T(8,128)(2,1)S(1)}, bf16[16,288,128]{2,1,0:T(8,128)(2,1)S(1)}, u32[]{:S(2)}, u32[]{:S(2)}) collective-permute-start(bf16[16,288,128]{2,1,0:T(8,128)(2,1)S(1)} %all-to-all-done.1.own_ref), channel_id=1, source_target_pairs={{0,32},{32,0},{1,33},{33,1},{2,34},{34,2},{3,35},{35,3},{4,36},{36... | collective-permute-start | bytes 3538952 | tf_op jit(solution)/shard_map/ppermute | solution.py:88
  66.8 1.1 copy-done.2
  67.9 0.9 copy-done.8
  70.0 3.0 %shard_map.109 = (bf16[2,256,704]{2,1,0:T(8,128)(2,1)}, f32[256,128]{1,0:T(8,128)}, f32[2,1,704]{2,1,0:T(1,128)S(1)}, f32[1,1]{1,0:T(1,128)}, f32[2,16,8,128]{3,2,1,0:T(8,128)}, /*index=5*/f32[16,1,128]{2,1,0:T(1,128)}) custom-call(s32[1]{0:T(128)} %bitcast.core_ref.place_ref, bf16[256,512]{1,0:T(8,128)(2,1)S(1)} %copy-done.8, ...), custom_call_target="tpu_custom_call" | custom-call | flops 1000000000 | bytes 6000000 | tf_op jit(solution)/shard_map/pallas_call | solution.py:65
  73.0 5.6 %all-to-all-start.2 = ((f32[16,1,128]{2,1,0:T(1,128)}), f32[16,1,128]{2,1,0:T(1,128)S(1)}, u32[]{:S(2)}, u32[]{:S(2)}) async-start(f32[16,1,128]{2,1,0:T(1,128)} %get-tuple-element.55), calls=%async_computation.2 | async-start | bytes 16384 | tf_op jit(solution)/shard_map/all_to_all | solution.py:703
  78.6 2.9 %shard_map.110 = (f32[2,16,704]{2,1,0:T(8,128)S(1)}, f32[256,128]{1,0:T(8,128)}) custom-call(s32[1]{0:T(128)} %bitcast.core_ref.place_ref, bf16[2,256,704]{2,1,0:T(8,128)(2,1)} %get-tuple-element.56.normed_ref, f32[2,1,704]{2,1,0:T(1,128)S(1)} %get-tuple-element.57.unit_ref, f32[1,1]{1,0:T(1,128)} %get-tuple-element.58.norm_ref, ...), custom_call_target="tpu_custom_call" | custom-call | flops 100000000 | bytes 2000000 | tf_op jit(solution)/shard_map/pallas_call | solution.py:65
  81.5 8.4 %all-to-all-done.2 = f32[16,1,128]{2,1,0:T(1,128)S(1)} async-done(((f32[16,1,128]{2,1,0:T(1,128)}), f32[16,1,128]{2,1,0:T(1,128)S(1)}, u32[]{:S(2)}, u32[]{:S(2)}) %all-to-all-start.2) | async-done | bytes 8224 | tf_op jit(solution)/shard_map/all_to_all | solution.py:703
  90.5 5.5 %all-to-all-start.3 = ((f32[32,2,128]{2,1,0:T(2,128)}), f32[32,2,128]{2,1,0:T(2,128)}, u32[]{:S(2)}, u32[]{:S(2)}) async-start(f32[32,2,128]{2,1,0:T(2,128)} %broadcast_in_dim.26), calls=%async_computation.3 | async-start | bytes 65536 | tf_op jit(solution)/shard_map/all_to_all | solution.py:84
  96.1 3.8 %shard_map.111 = (bf16[256,512]{1,0:T(8,128)(2,1)}, bf16[256,192]{1,0:T(8,128)(2,1)}, f32[16,512]{1,0:T(8,128)}, f32[16,192]{1,0:T(8,128)}) custom-call(s32[1]{0:T(128)} %bitcast.core_ref.place_ref, bf16[16,2,272,128]{3,2,1,0:T(8,128)(2,1)} %bitcast.27, bf16[2,256,704]{2,1,0:T(8,128)(2,1)} %get-tuple-element.56.normed_ref, ...), custom_call_target="tpu_custom_call" | custom-call | flops 500000000 | bytes 5000000 | tf_op jit(solution)/shard_map/pallas_call | solution.py:65
  99.8 3.5 %all-to-all-done.3.shares_ref = f32[32,2,128]{2,1,0:T(2,128)} async-done(((f32[32,2,128]{2,1,0:T(2,128)}), f32[32,2,128]{2,1,0:T(2,128)}, u32[]{:S(2)}, u32[]{:S(2)}) %all-to-all-start.3) | async-done | bytes 32800 | tf_op jit(solution)/shard_map/all_to_all | solution.py:84
  103.4 3.5 %shard_map.112 = (f32[1,16]{1,0:T(1,128)}, f32[272,128]{1,0:T(8,128)}, bf16[256,704]{1,0:T(8,128)(2,1)}) custom-call(s32[1]{0:T(128)} %bitcast.core_ref.place_ref, s32[1]{0:T(128)} %bitcast.1.own_ref, f32[32,2,128]{2,1,0:T(2,128)} %all-to-all-done.3.shares_ref, s32[1,16]{1,0:T(1,128)S(1)} %copy-done.13, f32[256,128]{1,0:T(8,128)} %get-tuple-element.70.inv_ref, ...), custom_call_target="tpu_custom_call" | custom-call | flops 10000000 | bytes 1000000 | tf_op jit(solution)/shard_map/pallas_call | solution.py:65
  106.9 6.3 %all-to-all-start.4 = ((bf16[32,8,704]{2,1,0:T(8,128)(2,1)}), bf16[32,8,704]{2,1,0:T(8,128)(2,1)}, u32[]{:S(2)}, u32[]{:S(2)}) async-start(bf16[32,8,704]{2,1,0:T(8,128)(2,1)} %bitcast.29), calls=%async_computation.4 | async-start | bytes 786432 | tf_op jit(solution)/shard_map/all_to_all | solution.py:780
  113.3 1.1 copy-done.4
  114.4 1.3 copy-done.6
  115.7 0.9 copy-done.12
  116.6 1.2 copy-done.15
  117.8 0.9 copy-done.16
  118.7 1.2 copy-done.18
  119.9 5.3 %shard_map.113 = bf16[3,704,256]{2,1,0:T(8,128)(2,1)} custom-call(bf16[2,256,704]{2,1,0:T(8,128)(2,1)S(1)} %copy-done.4, f32[256,128]{1,0:T(8,128)S(1)} %copy-done.10, f32[272,128]{1,0:T(8,128)S(1)} %copy-done.16, f32[2,16,704]{2,1,0:T(8,128)S(1)} %copy-done.12, bf16[16,288,128]{2,1,0:T(8,128)(2,1)S(1)} %all-to-all-done.1.own_ref, ...), custom_call_target="tpu_custom_call" | custom-call | flops 2000000000 | bytes 8000000 | tf_op jit(solution)/shard_map/pallas_call | solution.py:65
  125.3 12.0 %all-to-all-done.4 = bf16[32,8,704]{2,1,0:T(8,128)(2,1)} async-done(((bf16[32,8,704]{2,1,0:T(8,128)(2,1)}), bf16[32,8,704]{2,1,0:T(8,128)(2,1)}, u32[]{:S(2)}, u32[]{:S(2)}) %all-to-all-start.4) | async-done | bytes 360480 | tf_op jit(solution)/shard_map/all_to_all | solution.py:780
  137.2 3.3 %shard_map.114 = bf16[3,256,704]{2,1,0:T(8,128)(2,1)} custom-call(bf16[256,704]{1,0:T(8,128)(2,1)} %bitcast.10.grad_ref, bf16[3,256,704]{2,1,0:T(8,128)(2,1)S(1)} %bitcast.23, bf16[8,256,256]{2,1,0:T(8,128)(2,1)S(1)} %shard_map.105.weights_ref), custom_call_target="tpu_custom_call" | custom-call | flops 1000000000 | bytes 5000000 | tf_op jit(solution)/shard_map/pallas_call | solution.py:65
  (37 shorter events, 2.3 us)
Async XLA Ops:
  7.2 88.9 %all-gather.3.cloned.1.call-start = ((), (), s32[]{:S(2)}) async-start(), calls=%async_computation.5 | async-start | bytes 2297856 | tf_op jit(solution)/shard_map/all_gather | solution.py:627
  37.5 6.9 %copy-start.19 = (f32[1408]{0:T(1024)S(1)}, f32[1408]{0:T(1024)}, u32[]{:S(2)}) copy-start(f32[1408]{0:T(1024)} %param.13) | copy-start | bytes 16900
  37.5 6.9 %copy-start.9 = (bf16[1,1,256,1408]{3,2,1,0:T(8,128)(2,1)S(1)}, bf16[1,1,256,1408]{3,2,1,0:T(8,128)(2,1)}, u32[]{:S(2)}) copy-start(bf16[1,1,256,1408]{3,2,1,0:T(8,128)(2,1)} %param.10) | copy-start | bytes 2162692
  37.5 19.4 %all-to-all-start.1 = ((bf16[16,288,128]{2,1,0:T(8,128)(2,1)}), bf16[16,288,128]{2,1,0:T(8,128)(2,1)S(1)}, u32[]{:S(2)}, u32[]{:S(2)}) async-start(bf16[16,288,128]{2,1,0:T(8,128)(2,1)} %get-tuple-element.43), calls=%async_computation.1 | async-start | bytes 2359296 | tf_op jit(solution)/shard_map/all_to_all | solution.py:628
  44.8 0.9 copy-start.1
  45.7 5.9 %copy-start = (bf16[3,1,32,8,704]{4,3,2,1,0:T(8,128)(2,1)S(1)}, bf16[3,1,32,8,704]{4,3,2,1,0:T(8,128)(2,1)}, u32[]{:S(2)}) copy-start(bf16[3,1,32,8,704]{4,3,2,1,0:T(8,128)(2,1)} %param.8) | copy-start | bytes 3244036
  45.7 1.3 copy-start.14
  49.9 0.7 copy-start.7
  50.6 1.0 copy-start.17
  56.9 12.5 %collective-permute-start = (bf16[16,288,128]{2,1,0:T(8,128)(2,1)S(1)}, bf16[16,288,128]{2,1,0:T(8,128)(2,1)S(1)}, u32[]{:S(2)}, u32[]{:S(2)}) collective-permute-start(bf16[16,288,128]{2,1,0:T(8,128)(2,1)S(1)} %all-to-all-done.1.own_ref), channel_id=1, source_target_pairs={{0,32},{32,0},{1,33},{33,1},{2,34},{34,2},{3,35},{35,3},{4,36},{36... | collective-permute-start | bytes 3538952 | tf_op jit(solution)/shard_map/ppermute | solution.py:88
  66.7 1.1 copy-start.2
  67.9 0.9 copy-start.8
  68.8 1.1 copy-start.3
  70.0 3.0 %copy-start.5 = (bf16[16,288,128]{2,1,0:T(8,128)(2,1)}, bf16[16,288,128]{2,1,0:T(8,128)(2,1)S(1)}, u32[]{:S(2)}) copy-start(bf16[16,288,128]{2,1,0:T(8,128)(2,1)S(1)} %collective-permute-done.other_ref) | copy-start | bytes 3538948
  73.0 16.9 %all-to-all-start.2 = ((f32[16,1,128]{2,1,0:T(1,128)}), f32[16,1,128]{2,1,0:T(1,128)S(1)}, u32[]{:S(2)}, u32[]{:S(2)}) async-start(f32[16,1,128]{2,1,0:T(1,128)} %get-tuple-element.55), calls=%async_computation.2 | async-start | bytes 16384 | tf_op jit(solution)/shard_map/all_to_all | solution.py:703
  81.5 14.6 %copy-start.11 = (f32[2,16,704]{2,1,0:T(8,128)}, f32[2,16,704]{2,1,0:T(8,128)S(1)}, u32[]{:S(2)}) copy-start(f32[2,16,704]{2,1,0:T(8,128)S(1)} %get-tuple-element.64.token_ref) | copy-start | bytes 270340
  90.5 12.9 %all-to-all-start.3 = ((f32[32,2,128]{2,1,0:T(2,128)}), f32[32,2,128]{2,1,0:T(2,128)}, u32[]{:S(2)}, u32[]{:S(2)}) async-start(f32[32,2,128]{2,1,0:T(2,128)} %broadcast_in_dim.26), calls=%async_computation.3 | async-start | bytes 65536 | tf_op jit(solution)/shard_map/all_to_all | solution.py:84
  96.1 7.3 %copy-start.13 = (s32[1,16]{1,0:T(1,128)S(1)}, s32[1,16]{1,0:T(1,128)}, u32[]{:S(2)}) copy-start(s32[1,16]{1,0:T(1,128)} %teacher_ref.1) | copy-start | bytes 196
  99.8 13.4 %copy-start.10 = (f32[256,128]{1,0:T(8,128)S(1)}, f32[256,128]{1,0:T(8,128)}, u32[]{:S(2)}) copy-start(f32[256,128]{1,0:T(8,128)} %get-tuple-element.70.inv_ref) | copy-start | bytes 393220
  106.9 30.3 %all-to-all-start.4 = ((bf16[32,8,704]{2,1,0:T(8,128)(2,1)}), bf16[32,8,704]{2,1,0:T(8,128)(2,1)}, u32[]{:S(2)}, u32[]{:S(2)}) async-start(bf16[32,8,704]{2,1,0:T(8,128)(2,1)} %bitcast.29), calls=%async_computation.4 | async-start | bytes 786432 | tf_op jit(solution)/shard_map/all_to_all | solution.py:780
  113.3 1.1 copy-start.4
  114.4 1.3 copy-start.6
  115.7 0.9 copy-start.12
  116.6 1.2 copy-start.15
  117.8 0.9 copy-start.16
  118.7 1.2 copy-start.18
Sparse Core Ops, SparseCore 0:
  37.6 55.9 all-gather.2

commit v7 on v6

--- a/solution.py
+++ b/solution.py
@@ -131,7 +131,7 @@
     start = piece * TEXT
     near = pl.multiple_of(start // 128 * 128, 128)
     window = jnp.broadcast_to(text_ref[:, pl.ds(near, 256)], (8, 256))
-    text = pltpu.roll(window, 256 - (start - near), 1)[:1, :TEXT]
+    text = pltpu.roll(window, (256 - (start - near)) & 255, 1)[:1, :TEXT]
     high = text.astype(BF16).astype(F32)
     for term in (high, text - high):
         blank = jnp.zeros((1, 2 * SIDE - TEXT), F32)
@@ -576,20 +576,25 @@
     for load in loads:
         load.wait()
     along = jnp.sum(cross[:, :VIDEOS] * pull_row, axis=1, keepdims=True)
-    rows[:TOKENS] = jnp.broadcast_to(along, (TOKENS, 128))
-    copy = begin(rows, rows_out, sems.at[6])
     base_wide = jnp.sum(pull * pull_wide[...], axis=0, keepdims=True)
     base_narrow = jnp.sum(pull * pull_narrow[...], axis=0, keepdims=True)
-    scale = inv[:, :1]
-    out_wide = scale * (base_wide - along * wide[...].astype(F32))
-    out_narrow = scale * (base_narrow - along * narrow[...].astype(F32))
-    parts = []
-    for x in range(4):
-        parts += [out_wide[:, MAIN * x : MAIN * (x + 1)], out_narrow[:, REST * x : REST * (x + 1)]]
-    result[...] = jnp.concatenate(parts, axis=1).astype(BF16)
-    send = begin(result, time_out, sems.at[7])
-    copy.wait()
-    send.wait()
+    sends = []
+    for i in range(2):
+        part = slice(i * TOKENS // 2, (i + 1) * TOKENS // 2)
+        scale = inv[part, :1]
+        out_wide = scale * (base_wide - along[part] * wide[part].astype(F32))
+        out_narrow = scale * (base_narrow - along[part] * narrow[part].astype(F32))
+        parts = []
+        for x in range(4):
+            parts.append(out_wide[:, MAIN * x : MAIN * (x + 1)])
+            parts.append(out_narrow[:, REST * x : REST * (x + 1)])
+        result[part] = jnp.concatenate(parts, axis=1).astype(BF16)
+        span = pl.ds(i * TOKENS // 2, TOKENS // 2)
+        sends.append(begin(result.at[span], time_out.at[span], sems.at[7 + i]))
+    rows[:TOKENS] = jnp.broadcast_to(along, (TOKENS, 128))
+    sends.append(begin(rows, rows_out, sems.at[6]))
+    for send in sends:
+        send.wait()
 
 
 def shaped(shape, dtype):
@@ -775,7 +780,7 @@
             big((TOKENS + VIDEOS, 128), F32),
             big((TOKENS, ATT), BF16),
         ],
-        8,
+        9,
     )
     moved = lax.all_to_all(time_grad.reshape(FRAMES, 8, ATT), SEQ, 0, 0).reshape(TOKENS, ATT)
     space_grad = call(

time: 148 us -> 149 us (level)
  no operation moved by 1% of the time
where the time goes in v7:
time: 149 us; the launch traced here: 147 us
  starting transfers between devices  34.2 us (23%)
  Pallas kernels  29.5 us (20%)
  waiting for transfers between devices  28.1 us (19%)
  blocking collectives  27.5 us (18%)
  between operations  14.3 us (10%)
  local copies, waits for them, and re-layouts  13.8 us (9%)
    pallas_call x12, Pallas kernels, call(): pl.pallas_call(kernel, out_shape=shapes[0] if single else tuple(shapes),...  29.5 us
    all_to_all x1, blocking collectives, shards(): ring = lax.all_to_all(pack, RING, 0, 0)  27.5 us
    unnamed x40, local copies, waits for them, and re-layouts  13.1 us
    all_to_all x1, waiting for transfers between devices, shards(): lax.all_to_all(time_grad.reshape(FRAMES, 8, ATT), SEQ, 0, 0)  12 us
    ppermute x1, starting transfers between devices, swap(): return lax.ppermute(block, axis, [(0, 1), (1, 0)])  9.82 us
    all_to_all x1, waiting for transfers between devices, shards(): ring_rows = lax.all_to_all(row, RING, 0, 0)  8.38 us
    all_to_all x1, starting transfers between devices, shards(): w_own = lax.all_to_all(space_copies, ('x', 'y'), 0, 0)  6.9 us
    all_to_all x1, starting transfers between devices, shards(): lax.all_to_all(time_grad.reshape(FRAMES, 8, ATT), SEQ, 0, 0)  6.32 us
  transfers between devices with their start and end apart: 6, of which 4 were waited for; matrix products, arithmetic and copies ran while one was open for 0% of the time, Pallas kernels for 14%

profile of v7, /device:TPU:1, one launch (start us, length us, event | category | flops | bytes accessed | tf_op | source)
XLA Modules:
  0.0 147.5 jit_solution(17385548262834731526)
XLA Ops:
  7.2 1.0 shard_map.103
  8.2 27.5 %all_to_all.25.ring_ref = bf16[16,32,128]{2,1,0:T(8,128)(2,1)S(1)} all-to-all(bf16[16,32,128]{2,1,0:T(8,128)(2,1)S(1)} %shard_map.103), channel_id=1, replica_groups=mesh['zh'=2,'y'=4,'c'=2,'x'=4,'zl'=8] {'zh','zl'}, dimensions={0} | all-to-all | bytes 262144 | tf_op jit(solution)/shard_map/all_to_all | solution.py:619
  35.8 1.7 %shard_map.104 = (bf16[16,288,128]{2,1,0:T(8,128)(2,1)}, bf16[272,128]{1,0:T(8,128)(2,1)}) custom-call(bf16[16,32,128]{2,1,0:T(8,128)(2,1)S(1)} %all_to_all.25.ring_ref), custom_call_target="tpu_custom_call" | custom-call | flops 20000000 | bytes 2000000 | tf_op jit(solution)/shard_map/pallas_call | solution.py:65
  37.5 6.9 %all-to-all-start.1 = ((bf16[16,288,128]{2,1,0:T(8,128)(2,1)}), bf16[16,288,128]{2,1,0:T(8,128)(2,1)S(1)}, u32[]{:S(2)}, u32[]{:S(2)}) async-start(bf16[16,288,128]{2,1,0:T(8,128)(2,1)} %get-tuple-element.43), calls=%async_computation.1 | async-start | bytes 2359296 | tf_op jit(solution)/shard_map/all_to_all | solution.py:633
  44.8 0.9 copy-done.1
  45.7 1.3 copy-done.14
  47.0 2.9 %shard_map.107 = (bf16[8,256,256]{2,1,0:T(8,128)(2,1)S(1)}, bf16[256,512]{1,0:T(8,128)(2,1)S(1)}, bf16[256,192]{1,0:T(8,128)(2,1)S(1)}) custom-call(bf16[3,704,256]{2,1,0:T(8,128)(2,1)S(1)} %bitcast.25), custom_call_target="tpu_custom_call" | custom-call | flops 600000000 | bytes 3000000 | tf_op jit(solution)/shard_map/pallas_call | solution.py:65
  49.9 0.7 copy-done.7
  50.6 1.0 copy-done.17
  51.6 1.1 shard_map.105.weights_ref
  52.7 4.2 %all-to-all-done.1.own_ref = bf16[16,288,128]{2,1,0:T(8,128)(2,1)S(1)} async-done(((bf16[16,288,128]{2,1,0:T(8,128)(2,1)}), bf16[16,288,128]{2,1,0:T(8,128)(2,1)S(1)}, u32[]{:S(2)}, u32[]{:S(2)}) %all-to-all-start.1) | async-done | bytes 1179680 | tf_op jit(solution)/shard_map/all_to_all | solution.py:633
  56.9 9.8 %collective-permute-start = (bf16[16,288,128]{2,1,0:T(8,128)(2,1)S(1)}, bf16[16,288,128]{2,1,0:T(8,128)(2,1)S(1)}, u32[]{:S(2)}, u32[]{:S(2)}) collective-permute-start(bf16[16,288,128]{2,1,0:T(8,128)(2,1)S(1)} %all-to-all-done.1.own_ref), channel_id=1, source_target_pairs={{0,32},{32,0},{1,33},{33,1},{2,34},{34,2},{3,35},{35,3},{4,36},{36... | collective-permute-start | bytes 3538952 | tf_op jit(solution)/shard_map/ppermute | solution.py:88
  66.8 1.1 copy-done.2
  67.9 0.9 copy-done.8
  70.0 3.0 %shard_map.109 = (bf16[2,256,704]{2,1,0:T(8,128)(2,1)}, f32[256,128]{1,0:T(8,128)}, f32[2,1,704]{2,1,0:T(1,128)S(1)}, f32[1,1]{1,0:T(1,128)}, f32[2,16,8,128]{3,2,1,0:T(8,128)}, /*index=5*/f32[16,1,128]{2,1,0:T(1,128)}) custom-call(s32[1]{0:T(128)} %bitcast.core_ref.place_ref, bf16[256,512]{1,0:T(8,128)(2,1)S(1)} %copy-done.8, ...), custom_call_target="tpu_custom_call" | custom-call | flops 1000000000 | bytes 6000000 | tf_op jit(solution)/shard_map/pallas_call | solution.py:65
  73.0 5.6 %all-to-all-start.2 = ((f32[16,1,128]{2,1,0:T(1,128)}), f32[16,1,128]{2,1,0:T(1,128)S(1)}, u32[]{:S(2)}, u32[]{:S(2)}) async-start(f32[16,1,128]{2,1,0:T(1,128)} %get-tuple-element.55), calls=%async_computation.2 | async-start | bytes 16384 | tf_op jit(solution)/shard_map/all_to_all | solution.py:708
  78.6 2.9 %shard_map.110 = (f32[2,16,704]{2,1,0:T(8,128)S(1)}, f32[256,128]{1,0:T(8,128)}) custom-call(s32[1]{0:T(128)} %bitcast.core_ref.place_ref, bf16[2,256,704]{2,1,0:T(8,128)(2,1)} %get-tuple-element.56.normed_ref, f32[2,1,704]{2,1,0:T(1,128)S(1)} %get-tuple-element.57.unit_ref, f32[1,1]{1,0:T(1,128)} %get-tuple-element.58.norm_ref, ...), custom_call_target="tpu_custom_call" | custom-call | flops 100000000 | bytes 2000000 | tf_op jit(solution)/shard_map/pallas_call | solution.py:65
  81.5 8.4 %all-to-all-done.2 = f32[16,1,128]{2,1,0:T(1,128)S(1)} async-done(((f32[16,1,128]{2,1,0:T(1,128)}), f32[16,1,128]{2,1,0:T(1,128)S(1)}, u32[]{:S(2)}, u32[]{:S(2)}) %all-to-all-start.2) | async-done | bytes 8224 | tf_op jit(solution)/shard_map/all_to_all | solution.py:708
  90.5 5.5 %all-to-all-start.3 = ((f32[32,2,128]{2,1,0:T(2,128)}), f32[32,2,128]{2,1,0:T(2,128)}, u32[]{:S(2)}, u32[]{:S(2)}) async-start(f32[32,2,128]{2,1,0:T(2,128)} %broadcast_in_dim.26), calls=%async_computation.3 | async-start | bytes 65536 | tf_op jit(solution)/shard_map/all_to_all | solution.py:84
  96.1 3.8 %shard_map.111 = (bf16[256,512]{1,0:T(8,128)(2,1)}, bf16[256,192]{1,0:T(8,128)(2,1)}, f32[16,512]{1,0:T(8,128)}, f32[16,192]{1,0:T(8,128)}) custom-call(s32[1]{0:T(128)} %bitcast.core_ref.place_ref, bf16[16,2,272,128]{3,2,1,0:T(8,128)(2,1)} %bitcast.27, bf16[2,256,704]{2,1,0:T(8,128)(2,1)} %get-tuple-element.56.normed_ref, ...), custom_call_target="tpu_custom_call" | custom-call | flops 500000000 | bytes 5000000 | tf_op jit(solution)/shard_map/pallas_call | solution.py:65
  99.8 3.5 %all-to-all-done.3.shares_ref = f32[32,2,128]{2,1,0:T(2,128)} async-done(((f32[32,2,128]{2,1,0:T(2,128)}), f32[32,2,128]{2,1,0:T(2,128)}, u32[]{:S(2)}, u32[]{:S(2)}) %all-to-all-start.3) | async-done | bytes 32800 | tf_op jit(solution)/shard_map/all_to_all | solution.py:84
  103.4 3.6 %shard_map.112 = (f32[1,16]{1,0:T(1,128)}, f32[272,128]{1,0:T(8,128)}, bf16[256,704]{1,0:T(8,128)(2,1)}) custom-call(s32[1]{0:T(128)} %bitcast.core_ref.place_ref, s32[1]{0:T(128)} %bitcast.1.own_ref, f32[32,2,128]{2,1,0:T(2,128)} %all-to-all-done.3.shares_ref, s32[1,16]{1,0:T(1,128)S(1)} %copy-done.13, f32[256,128]{1,0:T(8,128)} %get-tuple-element.70.inv_ref, ...), custom_call_target="tpu_custom_call" | custom-call | flops 10000000 | bytes 1000000 | tf_op jit(solution)/shard_map/pallas_call | solution.py:65
  107.0 6.3 %all-to-all-start.4 = ((bf16[32,8,704]{2,1,0:T(8,128)(2,1)}), bf16[32,8,704]{2,1,0:T(8,128)(2,1)}, u32[]{:S(2)}, u32[]{:S(2)}) async-start(bf16[32,8,704]{2,1,0:T(8,128)(2,1)} %bitcast.29), calls=%async_computation.4 | async-start | bytes 786432 | tf_op jit(solution)/shard_map/all_to_all | solution.py:785
  113.3 1.1 copy-done.4
  114.5 1.3 copy-done.6
  115.7 0.9 copy-done.12
  116.6 1.2 copy-done.15
  117.9 0.9 copy-done.16
  118.8 1.2 copy-done.18
  120.0 5.3 %shard_map.113 = bf16[3,704,256]{2,1,0:T(8,128)(2,1)} custom-call(bf16[2,256,704]{2,1,0:T(8,128)(2,1)S(1)} %copy-done.4, f32[256,128]{1,0:T(8,128)S(1)} %copy-done.10, f32[272,128]{1,0:T(8,128)S(1)} %copy-done.16, f32[2,16,704]{2,1,0:T(8,128)S(1)} %copy-done.12, bf16[16,288,128]{2,1,0:T(8,128)(2,1)S(1)} %all-to-all-done.1.own_ref, ...), custom_call_target="tpu_custom_call" | custom-call | flops 2000000000 | bytes 8000000 | tf_op jit(solution)/shard_map/pallas_call | solution.py:65
  125.3 12.0 %all-to-all-done.4 = bf16[32,8,704]{2,1,0:T(8,128)(2,1)} async-done(((bf16[32,8,704]{2,1,0:T(8,128)(2,1)}), bf16[32,8,704]{2,1,0:T(8,128)(2,1)}, u32[]{:S(2)}, u32[]{:S(2)}) %all-to-all-start.4) | async-done | bytes 360480 | tf_op jit(solution)/shard_map/all_to_all | solution.py:785
  137.3 3.3 %shard_map.114 = bf16[3,256,704]{2,1,0:T(8,128)(2,1)} custom-call(bf16[256,704]{1,0:T(8,128)(2,1)} %bitcast.10.grad_ref, bf16[3,256,704]{2,1,0:T(8,128)(2,1)S(1)} %bitcast.23, bf16[8,256,256]{2,1,0:T(8,128)(2,1)S(1)} %shard_map.105.weights_ref), custom_call_target="tpu_custom_call" | custom-call | flops 1000000000 | bytes 5000000 | tf_op jit(solution)/shard_map/pallas_call | solution.py:65
  (37 shorter events, 2.3 us)
Async XLA Ops:
  7.2 88.9 %all-gather.3.cloned.1.call-start = ((), (), s32[]{:S(2)}) async-start(), calls=%async_computation.5 | async-start | bytes 2297856 | tf_op jit(solution)/shard_map/all_gather | solution.py:632
  37.5 6.9 %copy-start.19 = (f32[1408]{0:T(1024)S(1)}, f32[1408]{0:T(1024)}, u32[]{:S(2)}) copy-start(f32[1408]{0:T(1024)} %param.13) | copy-start | bytes 16900
  37.5 6.9 %copy-start.9 = (bf16[1,1,256,1408]{3,2,1,0:T(8,128)(2,1)S(1)}, bf16[1,1,256,1408]{3,2,1,0:T(8,128)(2,1)}, u32[]{:S(2)}) copy-start(bf16[1,1,256,1408]{3,2,1,0:T(8,128)(2,1)} %param.10) | copy-start | bytes 2162692
  37.5 19.4 %all-to-all-start.1 = ((bf16[16,288,128]{2,1,0:T(8,128)(2,1)}), bf16[16,288,128]{2,1,0:T(8,128)(2,1)S(1)}, u32[]{:S(2)}, u32[]{:S(2)}) async-start(bf16[16,288,128]{2,1,0:T(8,128)(2,1)} %get-tuple-element.43), calls=%async_computation.1 | async-start | bytes 2359296 | tf_op jit(solution)/shard_map/all_to_all | solution.py:633
  44.8 0.9 copy-start.1
  45.7 5.9 %copy-start = (bf16[3,1,32,8,704]{4,3,2,1,0:T(8,128)(2,1)S(1)}, bf16[3,1,32,8,704]{4,3,2,1,0:T(8,128)(2,1)}, u32[]{:S(2)}) copy-start(bf16[3,1,32,8,704]{4,3,2,1,0:T(8,128)(2,1)} %param.8) | copy-start | bytes 3244036
  45.7 1.3 copy-start.14
  49.9 0.7 copy-start.7
  50.6 1.0 copy-start.17
  56.9 12.5 %collective-permute-start = (bf16[16,288,128]{2,1,0:T(8,128)(2,1)S(1)}, bf16[16,288,128]{2,1,0:T(8,128)(2,1)S(1)}, u32[]{:S(2)}, u32[]{:S(2)}) collective-permute-start(bf16[16,288,128]{2,1,0:T(8,128)(2,1)S(1)} %all-to-all-done.1.own_ref), channel_id=1, source_target_pairs={{0,32},{32,0},{1,33},{33,1},{2,34},{34,2},{3,35},{35,3},{4,36},{36... | collective-permute-start | bytes 3538952 | tf_op jit(solution)/shard_map/ppermute | solution.py:88
  66.7 1.1 copy-start.2
  67.9 0.9 copy-start.8
  68.8 1.1 copy-start.3
  70.0 3.0 %copy-start.5 = (bf16[16,288,128]{2,1,0:T(8,128)(2,1)}, bf16[16,288,128]{2,1,0:T(8,128)(2,1)S(1)}, u32[]{:S(2)}) copy-start(bf16[16,288,128]{2,1,0:T(8,128)(2,1)S(1)} %collective-permute-done.other_ref) | copy-start | bytes 3538948
  73.0 16.9 %all-to-all-start.2 = ((f32[16,1,128]{2,1,0:T(1,128)}), f32[16,1,128]{2,1,0:T(1,128)S(1)}, u32[]{:S(2)}, u32[]{:S(2)}) async-start(f32[16,1,128]{2,1,0:T(1,128)} %get-tuple-element.55), calls=%async_computation.2 | async-start | bytes 16384 | tf_op jit(solution)/shard_map/all_to_all | solution.py:708
  81.5 14.6 %copy-start.11 = (f32[2,16,704]{2,1,0:T(8,128)}, f32[2,16,704]{2,1,0:T(8,128)S(1)}, u32[]{:S(2)}) copy-start(f32[2,16,704]{2,1,0:T(8,128)S(1)} %get-tuple-element.64.token_ref) | copy-start | bytes 270340
  90.5 12.9 %all-to-all-start.3 = ((f32[32,2,128]{2,1,0:T(2,128)}), f32[32,2,128]{2,1,0:T(2,128)}, u32[]{:S(2)}, u32[]{:S(2)}) async-start(f32[32,2,128]{2,1,0:T(2,128)} %broadcast_in_dim.26), calls=%async_computation.3 | async-start | bytes 65536 | tf_op jit(solution)/shard_map/all_to_all | solution.py:84
  96.1 7.3 %copy-start.13 = (s32[1,16]{1,0:T(1,128)S(1)}, s32[1,16]{1,0:T(1,128)}, u32[]{:S(2)}) copy-start(s32[1,16]{1,0:T(1,128)} %teacher_ref.1) | copy-start | bytes 196
  99.8 13.5 %copy-start.10 = (f32[256,128]{1,0:T(8,128)S(1)}, f32[256,128]{1,0:T(8,128)}, u32[]{:S(2)}) copy-start(f32[256,128]{1,0:T(8,128)} %get-tuple-element.70.inv_ref) | copy-start | bytes 393220
  107.0 30.3 %all-to-all-start.4 = ((bf16[32,8,704]{2,1,0:T(8,128)(2,1)}), bf16[32,8,704]{2,1,0:T(8,128)(2,1)}, u32[]{:S(2)}, u32[]{:S(2)}) async-start(bf16[32,8,704]{2,1,0:T(8,128)(2,1)} %bitcast.29), calls=%async_computation.4 | async-start | bytes 786432 | tf_op jit(solution)/shard_map/all_to_all | solution.py:785
  113.3 1.1 copy-start.4
  114.5 1.3 copy-start.6
  115.7 0.9 copy-start.12
  116.6 1.2 copy-start.15
  117.9 0.9 copy-start.16
  118.8 1.2 copy-start.18
Sparse Core Ops, SparseCore 0:
  37.6 55.9 all-gather.2
